TPU v7x, 32 devices: a whole 2x2x4 slice. The times are simulated.
32 devices in a mesh: dp: 8 (over y, x, core), mp: 4 (over z).
Axes of the slice: x: 2, y: 2, z: 4, core: 2. Of those that a mesh axis runs over, the one named last changes fastest.
Arguments:
- tokens: int32 [8, 1024], P('dp'), may hold values from 0 to 31
- lengths: int32 [8], P('dp'), may hold values from 30 to 1024, as said below
- tile_owner: int32 [192], replicated, may hold values from 0 to 191, each once
- step_count: int32 [], replicated, may hold values from 2 to 20
- weight_tiles: float32 [192, 128, 512], P('dp', None, 'mp'), may hold values from -0.1875 to 0.1875
- tiles_first: float32 [192, 128, 512], P('dp', None, 'mp'), may hold values from -9.536743e-06 to 9.536743e-06
- tiles_second: float32 [192, 128, 512], P('dp', None, 'mp'), may hold values from 1.6590697e-12 to 6.6520795e-12
- stats_left: float32 [192, 128, 512], P('dp', None, 'mp'), as said below
- stats_right: float32 [192, 128, 512], P('dp', None, 'mp'), as said below
- basis_left: float32 [192, 128, 512], P('dp', None, 'mp'), as said below
- basis_right: float32 [192, 128, 512], P('dp', None, 'mp'), as said below
- embedding: float32 [32, 1024], replicated, may hold values from -6 to 6
- embedding_first: float32 [32, 1024], replicated, may hold values from -2.670288e-05 to 2.670288e-05
- embedding_second: float32 [32, 1024], replicated, may hold values from 3.7329067e-13 to 1.4971129e-12
- head_table: float32 [1025, 32], replicated, may hold values from -0.1875 to 0.1875
- head_first: float32 [1025, 32], replicated, may hold values from -2.670288e-05 to 2.670288e-05
- head_second: float32 [1025, 32], replicated, may hold values from 1.4931627e-11 to 5.9884514e-11
- vectors: float32 [5, 1024], replicated
- vectors_first: float32 [5, 1024], replicated, may hold values from -2.670288e-05 to 2.670288e-05
- vectors_second: float32 [5, 1024], replicated, may hold values from 1.4931627e-11 to 5.9884514e-11
- fc_bias: float32 [1, 4096], P(None, 'mp'), may hold values from -4 to 4
- fc_bias_first: float32 [1, 4096], P(None, 'mp'), may hold values from -2.670288e-05 to 2.670288e-05
- fc_bias_second: float32 [1, 4096], P(None, 'mp'), may hold values from 1.4931627e-11 to 5.9884514e-11
Outputs:
- loss: float32 [], replicated
- grad_norm: float32 [], replicated
- new_tiles: float32 [192, 128, 512], P('dp', None, 'mp')
- tiles_low: bfloat16 [192, 128, 512], P('dp', None, 'mp')
- new_tiles_first: float32 [192, 128, 512], P('dp', None, 'mp')
- new_tiles_second: float32 [192, 128, 512], P('dp', None, 'mp')
- new_stats_left: float32 [192, 128, 512], P('dp', None, 'mp')
- new_stats_right: float32 [192, 128, 512], P('dp', None, 'mp')
- new_basis_left: float32 [192, 128, 512], P('dp', None, 'mp')
- new_basis_right: float32 [192, 128, 512], P('dp', None, 'mp')
- new_embedding: float32 [32, 1024], replicated
- new_embedding_first: float32 [32, 1024], replicated
- new_embedding_second: float32 [32, 1024], replicated
- new_head: float32 [1025, 32], replicated
- new_head_first: float32 [1025, 32], replicated
- new_head_second: float32 [1025, 32], replicated
- new_vectors: float32 [5, 1024], replicated
- new_vectors_first: float32 [5, 1024], replicated
- new_vectors_second: float32 [5, 1024], replicated
- new_fc_bias: float32 [1, 4096], P(None, 'mp')
- new_fc_bias_first: float32 [1, 4096], P(None, 'mp')
- new_fc_bias_second: float32 [1, 4096], P(None, 'mp')
Inputs may be any that keep to these rules, and one draw needn't show every extreme that they name: `lengths`: the 1 proteins of one length bucket stand in consecutive rows; some protein has length 1024. `tile_owner`: A permutation. `stats_left`: each tile is symmetric positive definite. `stats_right`: each tile is symmetric positive definite. `basis_left`: each tile has orthonormal columns. `basis_right`: each tile has orthonormal columns.
All inputs are finite; a program needn't handle non-finite values.
Results may differ from a plain program's by a relative error of at most 0.0063.
The roundings to bfloat16 on the way count: a program that leaves them out, or rounds other values in their place, can miss the bound.
Values may be sent and summed in bfloat16 or wider, within the bound.
No kernel may reach another device: no remote copies, remote signals or barrier semaphores. Data moves between devices by JAX's collectives and lax.ppermute only.
A program may use at most 192 MiB of HBM per device.

v0:
```python
import math

import jax
import jax.numpy as jnp
from jax import lax
from jax.sharding import PartitionSpec as P

D = 1024
H = 16
HD = 64
ROT = 32
LAYERS = 1
BS = 128


PRECISE = lax.Precision.HIGHEST
NORM_EPS = 1e-05
CLIP_NORM = 0.02
RATE_TILES = 0.02
RATE_SMALL = 0.2
BETA_ONE = 0.9
BETA_TWO = 0.95
ADAM_EPS = 1e-08
WEIGHT_DECAY = 0.01


def layer_norm(values, scale_row, shift_row):
    centred = values - jnp.mean(values, axis=-1, keepdims=True)
    spread = jnp.mean(centred * centred, axis=-1, keepdims=True)
    return centred * lax.rsqrt(spread + NORM_EPS) * scale_row + shift_row


def rotary(values, positions, direction):
    half_rot = ROT // 2
    frequency = 10000.0 ** (-2.0 * jnp.arange(half_rot, dtype=jnp.float32) / ROT)
    angles = positions.astype(jnp.float32)[:, None] * frequency[None, :]
    cosine = jnp.cos(angles)[:, None, :]
    sine_part = direction * jnp.sin(angles)[:, None, :]
    front_part = values[..., :half_rot]
    back_part = values[..., half_rot:ROT]
    return jnp.concatenate(
        [
            front_part * cosine - back_part * sine_part,
            back_part * cosine + front_part * sine_part,
            values[..., ROT:],
        ],
        axis=-1,
    )


def tiles_to_matrix(tiles, row_total, col_total):
    leading = tiles.shape[:-3]
    tile_grid = tiles.reshape(leading + (row_total // BS, col_total // BS, BS, BS))
    tile_grid = jnp.swapaxes(tile_grid, -3, -2)
    return tile_grid.reshape(leading + (row_total, col_total))


def matrix_to_tiles(matrix):
    leading = matrix.shape[:-2]
    row_total, col_total = matrix.shape[-2:]
    tile_grid = matrix.reshape(leading + (row_total // BS, BS, col_total // BS, BS))
    tile_grid = jnp.swapaxes(tile_grid, -3, -2)
    return tile_grid.reshape(leading + (row_total // BS * (col_total // BS), BS, BS))


def split_layer(tiles, heads_local, ff_local):
    shapes = ((D, 3 * heads_local * HD), (heads_local * HD, D), (D, ff_local), (ff_local, D))
    result = []
    offset = 0
    for row_total, col_total in shapes:
        amount = row_total // BS * (col_total // BS)
        result.append(
            tiles_to_matrix(tiles[..., offset : offset + amount, :, :], row_total, col_total)
        )
        offset = offset + amount
    return result


def orthonormal(product):
    gram_matrix = jnp.einsum("...ji,...jk->...ik", product, product, precision=PRECISE)
    lower_factor = lax.linalg.cholesky(gram_matrix)
    return lax.linalg.triangular_solve(
        lower_factor, product, left_side=False, lower=True, transpose_a=True
    )


def soap_update(
    weight,
    gradient,
    first_moment,
    second_moment,
    stats_one,
    stats_two,
    basis_one,
    basis_two,
    correct_one,
    correct_two,
):
    outer_one = jnp.einsum("...ij,...kj->...ik", gradient, gradient, precision=PRECISE)
    outer_two = jnp.einsum("...ji,...jk->...ik", gradient, gradient, precision=PRECISE)
    stats_one_new = BETA_TWO * stats_one + (1.0 - BETA_TWO) * outer_one
    stats_two_new = BETA_TWO * stats_two + (1.0 - BETA_TWO) * outer_two
    rotated = jnp.einsum("...ji,...jk->...ik", basis_one, gradient, precision=PRECISE)
    rotated = jnp.einsum("...ij,...jk->...ik", rotated, basis_two, precision=PRECISE)
    first_new = BETA_ONE * first_moment + (1.0 - BETA_ONE) * rotated
    second_new = BETA_TWO * second_moment + (1.0 - BETA_TWO) * rotated * rotated
    scaled = first_new / correct_one / (jnp.sqrt(second_new / correct_two) + ADAM_EPS)
    returned = jnp.einsum("...ij,...jk->...ik", basis_one, scaled, precision=PRECISE)
    returned = jnp.einsum("...ij,...kj->...ik", returned, basis_two, precision=PRECISE)
    weight_new = weight - RATE_TILES * (returned + WEIGHT_DECAY * weight)
    stats_both = jnp.stack([stats_one_new, stats_two_new])
    basis_both = jnp.stack([basis_one, basis_two])
    mixed_both = jnp.einsum("...ij,...jk->...ik", stats_both, basis_both, precision=PRECISE)
    renewed = orthonormal(mixed_both)
    return (weight_new, first_new, second_new, stats_one_new, stats_two_new, renewed[0], renewed[1])


def adamw_update(weight, gradient, first_moment, second_moment, correct_one, correct_two):
    first_new = BETA_ONE * first_moment + (1.0 - BETA_ONE) * gradient
    second_new = BETA_TWO * second_moment + (1.0 - BETA_TWO) * gradient * gradient
    scaled = first_new / correct_one / (jnp.sqrt(second_new / correct_two) + ADAM_EPS)
    return (weight - RATE_SMALL * (scaled + WEIGHT_DECAY * weight), first_new, second_new)


def mixed_rows(branch_part):
    return lax.psum(branch_part, "mp")


def normed_combine(normed_grad):
    return lax.psum(normed_grad, "mp")


def block_parts(block_index, queries, key_rows, values, slot_length, block_rows, seq_len):
    row_begin = block_index * block_rows
    seq_start = row_begin // seq_len * seq_len
    query_block = lax.dynamic_slice_in_dim(queries, row_begin, block_rows, 0)
    query_pos = row_begin - seq_start + jnp.arange(block_rows, dtype=jnp.int32)
    key_pos = jnp.arange(seq_len, dtype=jnp.int32)
    allowed = (key_pos[None, :] <= query_pos[:, None]) & (key_pos[None, :] < slot_length[row_begin])
    scores = jnp.einsum(
        "qhe,khe->hqk", query_block, key_rows, preferred_element_type=jnp.float32
    ) * (1.0 / math.sqrt(HD))
    return (
        jnp.where(allowed[None], scores, -1e30),
        query_block,
        key_rows,
        values,
        row_begin,
        seq_start,
    )


def attention_forward(queries, key_rows, values, slot_length, block_rows, seq_len):
    block_count = queries.shape[0] // block_rows

    def one_block(block_index):
        scores, query_block, key_seq, value_seq, row_begin, seq_start = block_parts(
            block_index, queries, key_rows, values, slot_length, block_rows, seq_len
        )
        maximum_row = jnp.max(scores, axis=-1, keepdims=True)
        exponent = jnp.exp(scores - maximum_row)
        row_total = jnp.sum(exponent, axis=-1, keepdims=True)
        weights_soft = (exponent / row_total).astype(jnp.bfloat16)
        output = jnp.einsum(
            "hqk,khe->qhe", weights_soft, value_seq, preferred_element_type=jnp.float32
        )
        return (output, (maximum_row + jnp.log(row_total))[..., 0])

    outputs, log_totals = lax.map(one_block, jnp.arange(block_count, dtype=jnp.int32))
    return (outputs.reshape(queries.shape), log_totals)


def attention_backward(
    queries, key_rows, values, output_grad, log_totals, slot_length, block_rows, seq_len
):
    block_count = queries.shape[0] // block_rows
    scale_value = 1.0 / math.sqrt(HD)

    def one_block(carried, block_index):
        key_grad, value_grad = carried
        scores, query_block, key_seq, value_seq, row_begin, seq_start = block_parts(
            block_index, queries, key_rows, values, slot_length, block_rows, seq_len
        )
        grad_block = lax.dynamic_slice_in_dim(output_grad, row_begin, block_rows, 0)
        weights_soft = jnp.exp(scores - log_totals[block_index][..., None])
        soft_grad = jnp.einsum(
            "qhe,khe->hqk", grad_block, value_seq, preferred_element_type=jnp.float32
        )
        value_part = jnp.einsum(
            "hqk,qhe->khe",
            weights_soft.astype(jnp.bfloat16),
            grad_block,
            preferred_element_type=jnp.float32,
        )
        score_grad = (
            weights_soft * (soft_grad - jnp.sum(weights_soft * soft_grad, axis=-1, keepdims=True))
        ).astype(jnp.bfloat16)
        query_part = (
            jnp.einsum("hqk,khe->qhe", score_grad, key_seq, preferred_element_type=jnp.float32)
            * scale_value
        )
        key_part = (
            jnp.einsum("hqk,qhe->khe", score_grad, query_block, preferred_element_type=jnp.float32)
            * scale_value
        )
        key_grad = key_grad + key_part
        value_grad = value_grad + value_part
        return ((key_grad, value_grad), query_part)

    zero_grad = jnp.zeros(key_rows.shape, jnp.float32)
    (key_grad, value_grad), query_parts = lax.scan(
        one_block, (zero_grad, zero_grad), jnp.arange(block_count, dtype=jnp.int32)
    )
    return (query_parts.reshape(queries.shape), key_grad, value_grad)


def layer_forward(
    residual,
    weights,
    vectors,
    in_bias,
    layer_index,
    positions,
    slot_length,
    block_rows,
    seq_len,
    heads_local,
):
    normed = layer_norm(residual, vectors[3 * layer_index], vectors[3 * layer_index + 1]).astype(
        jnp.bfloat16
    )
    slot_count = normed.shape[0]
    projected = jnp.dot(normed, weights[0], preferred_element_type=jnp.float32).reshape(
        slot_count, 3, heads_local, HD
    )
    queries = rotary(projected[:, 0], positions, 1.0).astype(jnp.bfloat16)
    key_rows = rotary(projected[:, 1], positions, 1.0).astype(jnp.bfloat16)
    values = projected[:, 2].astype(jnp.bfloat16)
    attended, log_totals = attention_forward(
        queries, key_rows, values, slot_length, block_rows, seq_len
    )
    attended_low = attended.reshape(slot_count, heads_local * HD).astype(jnp.bfloat16)
    upper_pre = jnp.dot(normed, weights[2], preferred_element_type=jnp.float32) + in_bias
    activated = jax.nn.gelu(upper_pre, approximate=True).astype(jnp.bfloat16)
    branch_part = jnp.dot(attended_low, weights[1], preferred_element_type=jnp.float32) + jnp.dot(
        activated, weights[3], preferred_element_type=jnp.float32
    )
    branch = mixed_rows(branch_part) + vectors[3 * layer_index + 2]
    kept_values = (residual, normed, queries, key_rows, values, log_totals, attended_low, upper_pre)
    return (residual + branch, kept_values)


def layer_backward(
    residual_grad,
    kept_values,
    weights,
    vectors,
    layer_index,
    positions,
    slot_length,
    block_rows,
    seq_len,
    heads_local,
):
    residual, normed_all, queries, key_rows, values, log_totals, attended_low, upper_pre = (
        kept_values
    )
    slot_count = normed_all.shape[0]
    branch_low = residual_grad.astype(jnp.bfloat16)
    out_bias_grad = jnp.sum(branch_low.astype(jnp.float32), axis=0)
    out_weight_grad = jnp.dot(attended_low.T, branch_low, preferred_element_type=jnp.float32)
    attended_grad = (
        jnp.dot(branch_low, weights[1].T, preferred_element_type=jnp.float32)
        .astype(jnp.bfloat16)
        .reshape(slot_count, heads_local, HD)
    )
    activated = jax.nn.gelu(upper_pre, approximate=True).astype(jnp.bfloat16)
    down_grad = jnp.dot(activated.T, branch_low, preferred_element_type=jnp.float32)
    unused, gelu_pull = jax.vjp(lambda pre_act: jax.nn.gelu(pre_act, approximate=True), upper_pre)
    upper_grad = gelu_pull(jnp.dot(branch_low, weights[3].T, preferred_element_type=jnp.float32))[
        0
    ].astype(jnp.bfloat16)
    up_grad = jnp.dot(normed_all.T, upper_grad, preferred_element_type=jnp.float32)
    in_bias_grad = jnp.sum(upper_grad.astype(jnp.float32), axis=0)
    query_grad, key_grad, value_grad = attention_backward(
        queries, key_rows, values, attended_grad, log_totals, slot_length, block_rows, seq_len
    )
    projected_grad = jnp.stack(
        [rotary(query_grad, positions, -1.0), rotary(key_grad, positions, -1.0), value_grad], axis=1
    )
    projected_grad = projected_grad.reshape(slot_count, 3 * heads_local * HD).astype(jnp.bfloat16)
    qkv_grad = jnp.dot(normed_all.T, projected_grad, preferred_element_type=jnp.float32)
    normed_grad = jnp.dot(
        projected_grad, weights[0].T, preferred_element_type=jnp.float32
    ) + jnp.dot(upper_grad, weights[2].T, preferred_element_type=jnp.float32)
    normed_rows = normed_combine(normed_grad)
    unused_norm, norm_pull = jax.vjp(
        layer_norm, residual, vectors[3 * layer_index], vectors[3 * layer_index + 1]
    )
    input_grad, gain_grad, shift_grad = norm_pull(normed_rows)
    return (
        residual_grad + input_grad,
        (qkv_grad, out_weight_grad, up_grad, down_grad),
        in_bias_grad,
        (gain_grad, shift_grad, out_bias_grad),
    )


def local(
    tokens,
    lengths,
    tile_owner,
    step_count,
    weight_tiles,
    tiles_first,
    tiles_second,
    stats_left,
    stats_right,
    basis_left,
    basis_right,
    embedding,
    embedding_first,
    embedding_second,
    head_table,
    head_first,
    head_second,
    vectors,
    vectors_first,
    vectors_second,
    fc_bias,
    fc_bias_first,
    fc_bias_second,
):
    group_rows, seq_len = tokens.shape
    slot_count = group_rows * seq_len
    mp_count = lax.axis_size("mp")
    dp_count = lax.axis_size("dp")
    heads_local = H // mp_count
    ff_local = fc_bias.shape[1]
    block_rows = min(512, seq_len)
    gathered = lax.all_gather(weight_tiles.astype(jnp.bfloat16), "dp", axis=0, tiled=True)
    natural = jnp.take(gathered, tile_owner, axis=0).reshape((LAYERS, -1, BS, BS))
    layer_weights = [split_layer(natural[0], heads_local, ff_local)]
    flat_tokens = tokens.reshape(slot_count)
    positions = jnp.arange(slot_count, dtype=jnp.int32) % seq_len
    slot_length = jnp.repeat(lengths, seq_len)
    slot_weight = jnp.where(
        positions < slot_length - 1, 1.0 / (slot_length - 1).astype(jnp.float32), 0.0
    )
    row_targets = jnp.roll(flat_tokens, -1)
    vocab_ids = jnp.arange(head_table.shape[1], dtype=jnp.int32)
    token_hot = (flat_tokens[:, None] == vocab_ids[None, :]).astype(jnp.float32)
    target_hot = (row_targets[:, None] == vocab_ids[None, :]).astype(jnp.float32)
    residual = jnp.dot(token_hot, embedding, precision=PRECISE)
    layer_index = 0
    residual, kept_values = layer_forward(
        residual,
        layer_weights[layer_index],
        vectors,
        fc_bias[layer_index],
        layer_index,
        positions,
        slot_length,
        block_rows,
        seq_len,
        heads_local,
    )
    saved = [kept_values]
    final_low = layer_norm(residual, vectors[3 * LAYERS], vectors[3 * LAYERS + 1]).astype(
        jnp.bfloat16
    )
    head_low = head_table[:-1].astype(jnp.bfloat16)
    logits = jnp.dot(final_low, head_low, preferred_element_type=jnp.float32) + head_table[-1]
    shifted = logits - jnp.max(logits, axis=-1, keepdims=True)
    log_probs = shifted - jnp.log(jnp.sum(jnp.exp(shifted), axis=-1, keepdims=True))
    loss_part = -jnp.sum(slot_weight * jnp.sum(target_hot * log_probs, axis=-1))
    logit_grad = ((jnp.exp(log_probs) - target_hot) * slot_weight[:, None]).astype(jnp.bfloat16)
    head_grad = jnp.concatenate(
        [
            jnp.dot(final_low.T, logit_grad, preferred_element_type=jnp.float32),
            jnp.sum(logit_grad.astype(jnp.float32), axis=0)[None],
        ],
        axis=0,
    )
    final_grad = jnp.dot(logit_grad, head_low.T, preferred_element_type=jnp.float32)
    unused_final, final_pull = jax.vjp(
        layer_norm, residual, vectors[3 * LAYERS], vectors[3 * LAYERS + 1]
    )
    residual_grad, final_gain_grad, final_shift_grad = final_pull(final_grad)
    vector_rows = [final_gain_grad] * (3 * LAYERS) + [final_gain_grad, final_shift_grad]
    tile_parts = [None] * LAYERS
    bias_rows = [None] * LAYERS
    for layer_index in reversed(range(LAYERS)):
        residual_grad, weight_grads, in_bias_grad, vector_grads = layer_backward(
            residual_grad,
            saved[layer_index],
            layer_weights[layer_index],
            vectors,
            layer_index,
            positions,
            slot_length,
            block_rows,
            seq_len,
            heads_local,
        )
        tile_parts[layer_index] = jnp.concatenate(
            [matrix_to_tiles(one_grad) for one_grad in weight_grads], axis=0
        )
        bias_rows[layer_index] = in_bias_grad
        vector_rows[3 * layer_index : 3 * layer_index + 3] = list(vector_grads)
    embed_grad = jnp.dot(token_hot.T, residual_grad, precision=PRECISE)
    vectors_grad = jnp.stack(vector_rows)
    fc_bias_grad = jnp.stack(bias_rows)
    natural_grads = tile_parts[0]
    inverse = (
        jnp.zeros_like(tile_owner)
        .at[tile_owner]
        .set(jnp.arange(tile_owner.shape[0], dtype=jnp.int32))
    )
    grad_share = lax.psum_scatter(
        jnp.take(natural_grads, inverse, axis=0), "dp", scatter_dimension=0, tiled=True
    )
    count_part = jnp.sum((lengths >= 2).astype(jnp.float32))
    embed_grad, head_grad, vectors_grad, fc_bias_grad, loss_sum, protein_count = lax.psum(
        (embed_grad, head_grad, vectors_grad, fc_bias_grad, loss_part, count_part), "dp"
    )
    grad_share = grad_share / protein_count
    embed_grad = embed_grad / protein_count
    head_grad = head_grad / protein_count
    vectors_grad = vectors_grad / protein_count
    fc_bias_grad = fc_bias_grad / protein_count
    replicated_sq = (
        jnp.sum(embed_grad * embed_grad)
        + jnp.sum(head_grad * head_grad)
        + jnp.sum(vectors_grad * vectors_grad)
    )
    square_part = (
        jnp.sum(grad_share * grad_share)
        + jnp.sum(fc_bias_grad * fc_bias_grad) / dp_count
        + replicated_sq / (dp_count * mp_count)
    )
    grad_norm = jnp.sqrt(lax.psum(square_part, ("dp", "mp")))
    factor = jnp.minimum(1.0, CLIP_NORM / grad_norm)
    correct_one = 1.0 - jnp.power(BETA_ONE, step_count.astype(jnp.float32))
    correct_two = 1.0 - jnp.power(BETA_TWO, step_count.astype(jnp.float32))
    results = soap_update(
        weight_tiles,
        factor * grad_share,
        tiles_first,
        tiles_second,
        stats_left,
        stats_right,
        basis_left,
        basis_right,
        correct_one,
        correct_two,
    )
    embed_out = adamw_update(
        embedding, factor * embed_grad, embedding_first, embedding_second, correct_one, correct_two
    )
    head_out = adamw_update(
        head_table, factor * head_grad, head_first, head_second, correct_one, correct_two
    )
    vector_out = adamw_update(
        vectors, factor * vectors_grad, vectors_first, vectors_second, correct_one, correct_two
    )
    bias_out = adamw_update(
        fc_bias, factor * fc_bias_grad, fc_bias_first, fc_bias_second, correct_one, correct_two
    )
    return (
        loss_sum / protein_count,
        grad_norm,
        results[0],
        results[0].astype(jnp.bfloat16),
        results[1],
        results[2],
        results[3],
        results[4],
        results[5],
        results[6],
        embed_out[0],
        embed_out[1],
        embed_out[2],
        head_out[0],
        head_out[1],
        head_out[2],
        vector_out[0],
        vector_out[1],
        vector_out[2],
        bias_out[0],
        bias_out[1],
        bias_out[2],
    )


def solution(mesh):
    in_specs = (
        P("dp", None),
        P("dp"),
        P(),
        P(),
        P("dp", None, "mp"),
        P("dp", None, "mp"),
        P("dp", None, "mp"),
        P("dp", None, "mp"),
        P("dp", None, "mp"),
        P("dp", None, "mp"),
        P("dp", None, "mp"),
        P(),
        P(),
        P(),
        P(),
        P(),
        P(),
        P(),
        P(),
        P(),
        P(None, "mp"),
        P(None, "mp"),
        P(None, "mp"),
    )
    out_specs = (
        P(),
        P(),
        P("dp", None, "mp"),
        P("dp", None, "mp"),
        P("dp", None, "mp"),
        P("dp", None, "mp"),
        P("dp", None, "mp"),
        P("dp", None, "mp"),
        P("dp", None, "mp"),
        P("dp", None, "mp"),
        P(),
        P(),
        P(),
        P(),
        P(),
        P(),
        P(),
        P(),
        P(),
        P(None, "mp"),
        P(None, "mp"),
        P(None, "mp"),
    )
    return jax.shard_map(local, mesh=mesh, in_specs=in_specs, out_specs=out_specs, check_vma=False)
```

profile of v0, /device:TPU:0, one launch (start us, length us, event | category | flops | bytes accessed | tf_op | source)
XLA Modules:
  0.0 1840.4 jit_solution(3837310473135062592)
XLA Ops:
  11.8 2.9 fusion.134
  19.2 39.6 %all-gather.2.cloned.1.call-done = bf16[192,128,128]{2,1,0:T(8,128)(2,1)} async-done(((bf16[24,128,128]{2,1,0:T(8,128)(2,1)}), bf16[192,128,128]{2,1,0:T(8,128)(2,1)}) %all-gather.2.cloned.1.call-update) | async-done | bytes 6291472 | tf_op jit(solution)/shard_map/all_gather | solution.py:341
  58.7 11.0 gather_fusion
  69.7 3.4 broadcast_select_fusion.1
  73.3 2.7 fusion.132
  79.2 3.4 fusion.68
  84.4 2.7 copy.103
  87.1 2.8 copy.104
  90.3 22.0 %while.31 = (s32[]{:T(128)}, bf16[2,512,4,64]{1,3,2,0:T(8,128)(2,1)}, f32[2,4,512]{2,1,0:T(4,128)S(1)}, s32[2]{0:T(128)S(1)}, s32[1024]{0:T(1024)S(1)}, /*index=...) while((s32[]{:T(128)}, ...), condition=%wide.region_5.6_spmd, body=%wide.region_2.5_spmd.sunk | while | flops 563084800 | bytes 33364428 | solution.py:169
  97.7 3.0 fusion.201
  108.5 3.0 fusion.201
  114.0 4.8 fusion.66
  118.9 2.6 fusion.60
  121.5 2.7 convolution_add_fusion
  126.4 153.0 %all-reduce.6.cloned.1.call-done = f32[1024,1024]{0,1:T(8,128)} async-done(((f32[1024,1024]{0,1:T(8,128)}), f32[1024,1024]{0,1:T(8,128)}) %all-reduce.6.cloned.1.call-update) | async-done | bytes 4194320 | tf_op jit(solution)/shard_map/psum | solution.py:126
  279.4 4.0 fusion.131
  294.4 7.1 convert_reduce_fusion.1
  301.6 60.5 %while.32 = (s32[]{:T(128)}, f32[1024,4,64]{0,2,1:T(8,128)S(1)}, f32[1024,4,64]{0,2,1:T(8,128)}, f32[2,512,4,64]{1,0,3,2:T(2,128)}, s32[2]{0:T(128)S(1)}, /*inde...) while((s32[]{:T(128)}, f32[1024,4,64]{0,2,1:T(8,128)S(1)}, ...), condition=%wide.region_20.21_spmd.clone, body=%wide.region_18.20_spmd.clone.sunk | while | flops 1376124416 | bytes 82901536 | solution.py:211
  307.8 3.6 fusion.214
  311.4 4.5 multiply_reduce_fusion.14
  321.2 10.4 dynamic_update_slice.28
  337.8 3.6 fusion.214
  341.4 4.5 multiply_reduce_fusion.14
  351.3 10.4 dynamic_update_slice.28
  368.2 4.3 fusion.72
  374.0 6.0 convolution_bitcast_fusion
  391.0 5.6 pad_maximum_fusion
  396.6 15.5 gather_fusion.1
  415.1 111.6 %all-reduce.8.cloned.1.call-done = f32[1024,1024]{0,1:T(8,128)} async-done(((f32[1024,1024]{0,1:T(8,128)}), f32[1024,1024]{0,1:T(8,128)}) %all-reduce.8.cloned.1.call-update) | async-done | bytes 4194320 | tf_op jit(solution)/shard_map/psum | solution.py:130
  526.7 4.5 fusion.125
  534.8 4.2 fusion.44
  539.1 10.0 broadcast_select_fusion
  551.5 26.0 %all-reduce = (f32[]{:T(128)}, f32[]{:T(128)}, f32[1,1024]{1,0:T(1,128)S(1)}, f32[5,1024]{1,0:T(8,128)S(1)}) all-reduce(f32[]{:T(128)S(6)} %neg.9, f32[]{:T(128)} %bitcast.29, f32[1,1024]{1,0:T(1,128)S(1)} %bitcast.298, f32[5,1024]{1,0:T(8,128)S(1)} %stack.49), channel_id=1, replica_groups=mesh['dp'=8,'mp'=4] {'dp'}, use_global_device_ids=true, to_apply=%region_13.14 | all-reduce | flops 6146 | bytes 49168 | tf_op jit(solution)/shard_map/psum | solution.py:424
  580.6 10.2 all-reduce.10.cloned.1.call-done
  597.1 90.2 %reduce-scatter.2.cloned.1.call-done = f32[24,128,128]{2,1,0:T(8,128)} async-done(((f32[192,128,128]{2,1,0:T(8,128)}), f32[24,128,128]{2,1,0:T(8,128)}) %reduce-scatter.2.cloned.1.call-update) | async-done | bytes 1572880 | tf_op jit(solution)/shard_map/reduce_scatter | solution.py:420
  687.3 3.1 multiply_reduce_fusion.7
  692.4 39.8 %psum.71 = f32[]{:T(128)} all-reduce(f32[]{:T(128)S(6)} %add.428), channel_id=1, replica_groups=mesh['dp'=8,'mp'=4] {'dp','mp'}, use_global_device_ids=true, to_apply=%region_41.42 | all-reduce | flops 1 | bytes 8 | tf_op jit(solution)/shard_map/psum | solution.py:442
  732.9 5.4 fusion.88
  743.0 4.9 fusion.136
  747.9 3.7 multiply_add_fusion
  751.6 4.0 multiply_add_fusion.1
  755.7 3.4 fusion.48
  760.8 6.9 fusion.140
  767.7 3.8 copy.119
  771.5 5.4 fusion.57
  776.8 564.3 %custom-call.6 = f32[2,24,128,128]{3,2,1,0:T(8,128)} custom-call(f32[2,24,128,128]{3,2,1,0:T(8,128)} %fusion.57), custom_call_target="Cholesky" | custom-call | tf_op jit(solution)/shard_map/cholesky | solution.py:81
  1346.1 473.0 %custom-call.7 = f32[2,24,1,128,128]{3,4,2,1,0:T(8,128)} custom-call(f32[2,24,1,128,128]{4,3,2,1,0:T(8,128)} %select_bitcast_fusion), custom_call_target="InvertDiagBlocksLowerTriangular" | custom-call | tf_op jit(solution)/shard_map/triangular_solve | solution.py:82
  1819.1 5.2 fusion.55
  (315 shorter events, 111.0 us)
Async XLA Ops:
  7.2 51.5 %all-gather.2.cloned.1.call-start = ((), (), s32[]{:S(2)}) async-start(), calls=%async_computation.1 | async-start | bytes 7077888 | tf_op jit(solution)/shard_map/all_gather | solution.py:341
  9.7 269.7 %all-reduce.6.cloned.1.call-start = ((), (), s32[]{:S(2)}) async-start(), calls=%async_computation.2 | async-start | bytes 8388608 | tf_op jit(solution)/shard_map/psum | solution.py:126
  11.1 3.6 copy-start.71
  11.8 4.3 copy-start.54
  14.7 4.4 copy-start.46
  16.2 53.6 %copy-start.56 = (f32[1024]{0:T(1024)}, f32[1024]{0:T(1024)S(1)}, u32[]{:S(2)}) copy-start(f32[1024]{0:T(1024)S(1)} %fusion.117) | copy-start | bytes 12292
  16.2 53.5 %copy-start.52 = (f32[1,1024]{1,0:T(1,128)}, f32[1,1024]{1,0:T(1,128)S(1)}, u32[]{:S(2)}) copy-start(f32[1,1024]{1,0:T(1,128)S(1)} %get-tuple-element.407) | copy-start | bytes 12292
  17.1 72.9 %copy-start.39 = (f32[1024,16]{0,1:T(8,128)}, f32[1024,16]{0,1:T(8,128)S(1)}, u32[]{:S(2)}) copy-start(f32[1024,16]{0,1:T(8,128)S(1)} %get-tuple-element.411) | copy-start | bytes 196612
  73.1 3.9 copy-start.6
  82.7 4.4 copy-start.12
  114.0 7.5 copy-start.17
  114.0 4.9 copy-start.21
  114.0 4.9 copy-start.72
  124.3 402.4 %all-reduce.8.cloned.1.call-start = ((), (), s32[]{:S(2)}) async-start(), calls=%async_computation.4 | async-start | bytes 8388608 | tf_op jit(solution)/shard_map/psum | solution.py:130
  284.6 3.6 copy-start.7
  289.3 5.2 copy-start.78
  290.3 11.2 copy-start.10
  301.5 62.8 %copy-start.40 = (f32[1024,16]{0,1:T(8,128)S(1)}, f32[1024,16]{0,1:T(8,128)}, u32[]{:S(2)}) copy-start(f32[1024,16]{0,1:T(8,128)} %copy-done.39) | copy-start | bytes 196612
  301.6 62.8 %copy-start.45 = (f32[1024,16]{0,1:T(8,128)S(1)}, f32[1024,16]{0,1:T(8,128)}, u32[]{:S(2)}) copy-start(f32[1024,16]{0,1:T(8,128)} %get-tuple-element.409) | copy-start | bytes 196612
  311.3 4.6 copy-start.34
  341.4 4.6 copy-start.34
  372.5 218.3 %all-reduce.10.cloned.1.call-start = ((), (), s32[]{:S(2)}) async-start(), calls=%async_computation.5 | async-start | bytes 557056 | tf_op jit(solution)/shard_map/psum | solution.py:424
  396.6 15.5 copy-start.37
  396.6 130.1 %copy-start.47 = (f32[1024]{0:T(1024)S(1)}, f32[1024]{0:T(1024)}, u32[]{:S(2)}) copy-start(f32[1024]{0:T(1024)} %copy-done.46) | copy-start | bytes 12292
  396.6 130.1 %copy-start.53 = (f32[1,1024]{1,0:T(1,128)S(1)}, f32[1,1024]{1,0:T(1,128)}, u32[]{:S(2)}) copy-start(f32[1,1024]{1,0:T(1,128)} %copy-done.52) | copy-start | bytes 12292
  415.1 116.2 %copy-start.63 = (f32[1024]{0:T(1024)S(1)}, f32[1024]{0:T(1024)}, u32[]{:S(2)}) copy-start(f32[1024]{0:T(1024)} %copy-done.62) | copy-start | bytes 12292
  415.1 116.2 %copy-start.57 = (f32[1024]{0:T(1024)S(1)}, f32[1024]{0:T(1024)}, u32[]{:S(2)}) copy-start(f32[1024]{0:T(1024)} %copy-done.56) | copy-start | bytes 12292
  526.7 4.6 copy-start.1
  526.7 5.9 copy-start.5
  539.0 148.3 %reduce-scatter.2.cloned.1.call-start = ((), (), s32[]{:S(2)}) async-start(), calls=%async_computation.3 | async-start | bytes 14155776 | tf_op jit(solution)/shard_map/reduce_scatter | solution.py:420
  549.1 189.1 %copy-start.8 = (f32[24,128,128]{2,1,0:T(8,128)S(1)}, f32[24,128,128]{2,1,0:T(8,128)}, u32[]{:S(2)}) copy-start(f32[24,128,128]{2,1,0:T(8,128)} %param.37) | copy-start | bytes 4718596
  549.2 189.1 %copy-start.23 = (f32[24,128,128]{2,1,0:T(8,128)S(1)}, f32[24,128,128]{2,1,0:T(8,128)}, u32[]{:S(2)}) copy-start(f32[24,128,128]{2,1,0:T(8,128)} %param.33) | copy-start | bytes 4718596
  732.9 5.4 copy-start.24
  743.0 4.9 copy-start.30
  743.0 4.9 copy-start.75
  747.9 3.7 copy-start.76
  751.6 7.5 copy-start.28
  755.7 3.5 copy-start.29
  1824.4 3.4 copy-start.41
  1824.4 3.4 copy-start.42
  1824.4 3.4 copy-start.50
  1824.4 3.4 copy-start.51
  1824.4 4.9 copy-start.32
  1824.4 4.9 copy-start.38
  1824.5 4.9 copy-start.48
  1824.5 4.8 copy-start.49
  1824.5 6.3 copy-start.73
  1824.5 6.3 copy-start.74
  (43 other events, 83.7 us)
Sparse Core Ops, SparseCore 0:
  10.5 48.2 all-gather.1
  124.4 154.9 all-reduce.5
  372.6 153.9 all-reduce.7
  539.1 51.5 all-reduce.9
  594.1 93.1 reduce-scatter.1
where the time goes:
time: 1850 us; the launch traced here: 1840 us
  other arithmetic  1120 us (61%)
  waiting for transfers between devices  405 us (22%)
  matrix products  122 us (7%)
  local copies, waits for them, and re-layouts  95.3 us (5%)
  blocking collectives  65.7 us (4%)
  between operations  25 us (1%)
    another operation x4, other arithmetic, orthonormal(): lower_factor = lax.linalg.cholesky(gram_matrix)  567 us
    another operation x3, other arithmetic, orthonormal(): lax.linalg.triangular_solve(lower_factor, product, left_side=False, lower...  475 us
    psum x1, waiting for transfers between devices, mixed_rows(): return lax.psum(branch_part, 'mp')  153 us
    psum x1, waiting for transfers between devices, normed_combine(): return lax.psum(normed_grad, 'mp')  112 us
    reduce_scatter x1, waiting for transfers between devices, local(): lax.psum_scatter(jnp.take(natural_grads, inverse, axis=0), 'dp', scatter_...  90.2 us
    psum x1, blocking collectives, local(): grad_norm = jnp.sqrt(lax.psum(square_part, ('dp', 'mp')))  39.8 us
    all_gather x1, waiting for transfers between devices, local(): lax.all_gather(weight_tiles.astype(jnp.bfloat16), 'dp', axis=0, tiled=True)  39.6 us
  transfers between devices with their start and end apart: 5, of which 5 were waited for; matrix products, arithmetic and copies ran while one was open for 4% of the time, Pallas kernels for 0%

commit v1 on v0

--- a/solution.py
+++ b/solution.py
@@ -1,8 +1,11 @@
+import functools
 import math
 
 import jax
 import jax.numpy as jnp
 from jax import lax
+from jax.experimental import pallas as pl
+from jax.experimental.pallas import tpu as pltpu
 from jax.sharding import PartitionSpec as P
 
 D = 1024
@@ -48,72 +51,223 @@
     )
 
 
-def tiles_to_matrix(tiles, row_total, col_total):
-    leading = tiles.shape[:-3]
-    tile_grid = tiles.reshape(leading + (row_total // BS, col_total // BS, BS, BS))
-    tile_grid = jnp.swapaxes(tile_grid, -3, -2)
-    return tile_grid.reshape(leading + (row_total, col_total))
-
-
-def matrix_to_tiles(matrix):
-    leading = matrix.shape[:-2]
-    row_total, col_total = matrix.shape[-2:]
-    tile_grid = matrix.reshape(leading + (row_total // BS, BS, col_total // BS, BS))
-    tile_grid = jnp.swapaxes(tile_grid, -3, -2)
-    return tile_grid.reshape(leading + (row_total // BS * (col_total // BS), BS, BS))
-
-
-def split_layer(tiles, heads_local, ff_local):
-    shapes = ((D, 3 * heads_local * HD), (heads_local * HD, D), (D, ff_local), (ff_local, D))
-    result = []
-    offset = 0
-    for row_total, col_total in shapes:
-        amount = row_total // BS * (col_total // BS)
-        result.append(
-            tiles_to_matrix(tiles[..., offset : offset + amount, :, :], row_total, col_total)
-        )
-        offset = offset + amount
-    return result
-
-
-def orthonormal(product):
-    gram_matrix = jnp.einsum("...ji,...jk->...ik", product, product, precision=PRECISE)
-    lower_factor = lax.linalg.cholesky(gram_matrix)
-    return lax.linalg.triangular_solve(
-        lower_factor, product, left_side=False, lower=True, transpose_a=True
-    )
-
-
-def soap_update(
-    weight,
-    gradient,
-    first_moment,
-    second_moment,
-    stats_one,
-    stats_two,
-    basis_one,
-    basis_two,
-    correct_one,
-    correct_two,
-):
-    outer_one = jnp.einsum("...ij,...kj->...ik", gradient, gradient, precision=PRECISE)
-    outer_two = jnp.einsum("...ji,...jk->...ik", gradient, gradient, precision=PRECISE)
-    stats_one_new = BETA_TWO * stats_one + (1.0 - BETA_TWO) * outer_one
-    stats_two_new = BETA_TWO * stats_two + (1.0 - BETA_TWO) * outer_two
-    rotated = jnp.einsum("...ji,...jk->...ik", basis_one, gradient, precision=PRECISE)
-    rotated = jnp.einsum("...ij,...jk->...ik", rotated, basis_two, precision=PRECISE)
-    first_new = BETA_ONE * first_moment + (1.0 - BETA_ONE) * rotated
-    second_new = BETA_TWO * second_moment + (1.0 - BETA_TWO) * rotated * rotated
-    scaled = first_new / correct_one / (jnp.sqrt(second_new / correct_two) + ADAM_EPS)
-    returned = jnp.einsum("...ij,...jk->...ik", basis_one, scaled, precision=PRECISE)
-    returned = jnp.einsum("...ij,...kj->...ik", returned, basis_two, precision=PRECISE)
-    weight_new = weight - RATE_TILES * (returned + WEIGHT_DECAY * weight)
-    stats_both = jnp.stack([stats_one_new, stats_two_new])
-    basis_both = jnp.stack([basis_one, basis_two])
-    mixed_both = jnp.einsum("...ij,...jk->...ik", stats_both, basis_both, precision=PRECISE)
-    renewed = orthonormal(mixed_both)
-    return (weight_new, first_new, second_new, stats_one_new, stats_two_new, renewed[0], renewed[1])
-
+def layer_shapes(heads_local, ff_local):
+    return ((D, 3 * heads_local * HD), (heads_local * HD, D), (D, ff_local), (ff_local, D))
+
+
+def tile_places(shapes):
+    places = []
+    for which, (row_total, col_total) in enumerate(shapes):
+        for i in range(row_total // BS):
+            for k in range(col_total // BS):
+                places.append((which, i * BS, k * BS))
+    return places
+
+
+def assemble_kernel(places, owner, tiles, *matrices):
+    for index, (which, row, col) in enumerate(places):
+        matrices[which][row : row + BS, col : col + BS] = tiles[owner[index]]
+
+
+def assemble(tile_owner, tiles, shapes):
+    return pl.pallas_call(
+        functools.partial(assemble_kernel, tile_places(shapes)),
+        in_specs=[
+            pl.BlockSpec(memory_space=pltpu.SMEM),
+            pl.BlockSpec(memory_space=pltpu.VMEM),
+        ],
+        out_specs=[pl.BlockSpec(memory_space=pltpu.VMEM)] * len(shapes),
+        out_shape=[jax.ShapeDtypeStruct(shape, tiles.dtype) for shape in shapes],
+        compiler_params=pltpu.CompilerParams(vmem_limit_bytes=56 * 1024 * 1024),
+        name="assemble",
+    )(tile_owner, tiles)
+
+
+def scatter_kernel(places, owner, *refs):
+    tiles = refs[-1]
+    for index, (which, row, col) in enumerate(places):
+        tiles[owner[index]] = refs[which][row : row + BS, col : col + BS]
+
+
+def scatter_tiles(tile_owner, matrices):
+    shapes = [matrix.shape for matrix in matrices]
+    places = tile_places(shapes)
+    return pl.pallas_call(
+        functools.partial(scatter_kernel, places),
+        in_specs=[pl.BlockSpec(memory_space=pltpu.SMEM)]
+        + [pl.BlockSpec(memory_space=pltpu.VMEM)] * len(matrices),
+        out_specs=pl.BlockSpec(memory_space=pltpu.VMEM),
+        out_shape=jax.ShapeDtypeStruct((len(places), BS, BS), matrices[0].dtype),
+        compiler_params=pltpu.CompilerParams(vmem_limit_bytes=56 * 1024 * 1024),
+        name="scatter",
+    )(tile_owner, *matrices)
+
+
+HB = 64
+GROUP = 0
+UN = 3
+NN = (((1,), (0,)), ((), ()))
+NT = (((1,), (1,)), ((), ()))
+TN = (((0,), (0,)), ((), ()))
+f32 = jnp.float32
+bf16 = jnp.bfloat16
+
+def split(a):
+    hi=a.astype(bf16)
+    return hi,(a-hi.astype(f32)).astype(bf16)
+
+def split3(a):
+    h=a.astype(bf16); r=a-h.astype(f32); m=r.astype(bf16); return h,m,(r-m.astype(f32)).astype(bf16)
+
+def stack(parts,dims_axis):
+    return jnp.concatenate(parts,axis=dims_axis)
+
+def sdot3(a,b,dims):
+    (ca,),(cb,)=dims[0]
+    ah,al=split(a); bh,bl=split(b)
+    return lax.dot_general(stack([ah,ah,al],ca),stack([bh,bl,bh],cb),dims,preferred_element_type=f32)
+
+def sdot6(a,b,dims):
+    (ca,),(cb,)=dims[0]
+    ah,am,al=split3(a); bh,bm,bl=split3(b)
+    return lax.dot_general(stack([ah,ah,am,am,ah,al],ca),stack([bh,bm,bh,bm,bl,bh],cb),dims,preferred_element_type=f32)
+
+D3=sdot3
+D6=sdot6
+
+def eliminate(work, count):
+    lane=lax.broadcasted_iota(jnp.int32,(HB,BS),1)
+    sub=lax.broadcasted_iota(jnp.int32,(HB,BS),0)
+    half=jnp.where(lane>=HB,HB,0)
+    for g0 in range(HB//8):
+        r0=8*g0
+        rows=HB-r0
+        def body(jj,carry):
+            j=r0+jj
+            pick=half[:rows]+j
+            at_pivot=lane[:rows]==pick
+            below=sub[:rows]>jj
+            clear=at_pivot&below
+            group=GROUP or count
+            for t0 in range(0,count,group):
+                span=range(t0,t0+group)
+                rows_in=[work[t,pl.ds(j,1),:] for t in span]
+                kept=[work[t,r0:,:] for t in span]
+                wides=[jnp.broadcast_to(row,(8,BS)) for row in rows_in]
+                pivots=[jnp.take_along_axis(w,pick[:8],axis=1,mode="promise_in_bounds") for w in wides]
+                cs=[jnp.take_along_axis(a,pick,axis=1,mode="promise_in_bounds") for a in kept]
+                scaleds=[jnp.where(at_pivot[:8],1.0,w)/p for w,p in zip(wides,pivots)]
+                for t,a,c,sc in zip(span,kept,cs,scaleds):
+                    work[t,r0:,:]=jnp.where(clear,0.0,a)-jnp.where(below,c,0.0)*sc[:1]
+            return carry
+        lax.fori_loop(0,8,body,0)
+
+def factor_inverse(packed):
+    lane=lax.broadcasted_iota(jnp.int32,(HB,BS),1)
+    sub=lax.broadcasted_iota(jnp.int32,(HB,BS),0)
+    left=lane<HB
+    col=jnp.where(left,lane,lane-HB)
+    diag=jnp.where(col==sub,packed,0.0)
+    d_left=jnp.sum(jnp.where(left,diag,0.0),axis=1,keepdims=True)
+    d_right=jnp.sum(jnp.where(left,0.0,diag),axis=1,keepdims=True)
+    scale=lax.rsqrt(jnp.where(left,d_left,d_right))
+    unit=jnp.where(col<sub,packed,jnp.where(col==sub,1.0,0.0))
+    return unit*scale
+
+def block_diagonal(packed):
+    lane=lax.broadcasted_iota(jnp.int32,(HB,BS),1)
+    left=lane<HB
+    return jnp.concatenate([jnp.where(left,packed,0.0),jnp.where(left,0.0,packed)],axis=0)
+
+def swap(x):
+    return pltpu.roll(x,HB,1)
+
+def soap_kernel(count, per, scal, G, W, m, v, L, R, QL, QR, W_o, low_o, m_o, v_o, L_o, R_o, QL_o, QR_o, ML_s, MR_s, work, A21_s, A22_s, W11_s):
+    step=pl.program_id(0)
+    scale=scal[0]; c1=scal[1]; c2=scal[2]
+    left=lax.broadcasted_iota(jnp.int32,(HB,BS),1)<HB
+    span=range(per)
+    g=[G[s].astype(f32)*scale for s in span]
+    gT=[x.T for x in g]
+    qT=[QL[s].T for s in span]
+    ggl=[D3(x,x,NT) for x in g]
+    ggr=[D3(x,x,NT) for x in gT]
+    rot=[D3(q,x,NN) for q,x in zip(qT,g)]
+    Ln=[BETA_TWO*L[s]+(1-BETA_TWO)*ggl[s] for s in span]
+    Rn=[BETA_TWO*R[s]+(1-BETA_TWO)*ggr[s] for s in span]
+    rot=[D3(x,QR[s],NN) for s,x in enumerate(rot)]
+    for s in span:
+        L_o[s]=Ln[s]; R_o[s]=Rn[s]
+    ML=[D6(Ln[s],QL[s],NN) for s in span]
+    MR=[D6(Rn[s],QR[s],NN) for s in span]
+    xs=[]
+    for s in span:
+        mn=BETA_ONE*m[s]+(1-BETA_ONE)*rot[s]
+        vn=BETA_TWO*v[s]+(1-BETA_TWO)*rot[s]*rot[s]
+        m_o[s]=mn; v_o[s]=vn
+        xs.append((mn/c1)/(jnp.sqrt(vn/c2)+ADAM_EPS))
+    back=[D3(QL[s],xs[s],NN) for s in span]
+    ML=[x*lax.rsqrt(jnp.sum(x*x,keepdims=True)) for x in ML]
+    MR=[x*lax.rsqrt(jnp.sum(x*x,keepdims=True)) for x in MR]
+    back=[D3(back[s],QR[s],NT) for s in span]
+    AL=[D6(x,x,TN) for x in ML]
+    AR=[D6(x,x,TN) for x in MR]
+    for s in span:
+        w=W[s]
+        wn=w-RATE_TILES*(back[s]+WEIGHT_DECAY*w)
+        W_o[s]=wn
+        low_o[s]=wn.astype(bf16)
+        t=step*per+s
+        ML_s[t]=ML[s]; MR_s[t]=MR[s]
+        work[t]=jnp.where(left,AL[s][:HB],swap(AR[s][:HB]))
+        A21_s[t]=jnp.where(left,AL[s][HB:],swap(AR[s][HB:]))
+        A22_s[t]=jnp.where(left,swap(AL[s][HB:]),AR[s][HB:])
+
+    @pl.when(step==pl.num_programs(0)-1)
+    def _():
+        eliminate(work,count)
+        def mid(i,carry):
+            ts=[i*UN+k for k in range(UN)]
+            w11=[factor_inverse(work[t]) for t in ts]
+            for t,w in zip(ts,w11): W11_s[t]=w
+            l21=[D6(A21_s[t],block_diagonal(w),NT) for t,w in zip(ts,w11)]
+            for t,l in zip(ts,l21): A21_s[t]=l
+            low=[D6(l,block_diagonal(l),NT) for l in l21]
+            for t,l in zip(ts,low): work[t]=A22_s[t]-l
+            return carry
+        lax.fori_loop(0,count//UN,mid,0)
+        eliminate(work,count)
+        def last(i,carry):
+            ts=[i*UN+k for k in range(UN)]
+            w22=[factor_inverse(work[t]) for t in ts]
+            w11=[W11_s[t] for t in ts]
+            y=[D6(A21_s[t],block_diagonal(w),NN) for t,w in zip(ts,w11)]
+            w21=[-D6(w,block_diagonal(x),NN) for w,x in zip(w22,y)]
+            cl=[jnp.concatenate([jnp.where(left,a,0.0),jnp.where(left,b,swap(c))],axis=0) for a,b,c in zip(w11,w21,w22)]
+            cr=[jnp.concatenate([jnp.where(left,swap(a),0.0),jnp.where(left,swap(b),c)],axis=0) for a,b,c in zip(w11,w21,w22)]
+            ol=[D3(ML_s[t],c,NT) for t,c in zip(ts,cl)]
+            orr=[D3(MR_s[t],c,NT) for t,c in zip(ts,cr)]
+            for t,a,b in zip(ts,ol,orr):
+                QL_o[t]=a; QR_o[t]=b
+            return carry
+        lax.fori_loop(0,count//UN,last,0)
+
+def soap(scal,G,W,m,v,L,R,QL,QR):
+    count=W.shape[0]
+    per=3 if count%3==0 else 1
+    blk=pl.BlockSpec((per,BS,BS),lambda i:(i,0,0))
+    full=pl.BlockSpec((count,BS,BS),lambda i:(0,0,0))
+    o=lambda dt: jax.ShapeDtypeStruct((count,BS,BS),dt)
+    return pl.pallas_call(
+        functools.partial(soap_kernel,count,per),
+        grid=(count//per,),
+        in_specs=[pl.BlockSpec(memory_space=pltpu.SMEM)]+[blk]*8,
+        out_specs=[blk]*6+[full]*2,
+        out_shape=[o(f32),o(bf16),o(f32),o(f32),o(f32),o(f32),o(f32),o(f32)],
+        scratch_shapes=[pltpu.VMEM((count,BS,BS),f32)]*2+[pltpu.VMEM((count,HB,BS),f32)]*4,
+        compiler_params=pltpu.CompilerParams(vmem_limit_bytes=56*1024*1024),
+        name="soap_tiles",
+    )(scal,G,W,m,v,L,R,QL,QR)
 
 def adamw_update(weight, gradient, first_moment, second_moment, correct_one, correct_two):
     first_new = BETA_ONE * first_moment + (1.0 - BETA_ONE) * gradient
@@ -339,8 +493,8 @@
     ff_local = fc_bias.shape[1]
     block_rows = min(512, seq_len)
     gathered = lax.all_gather(weight_tiles.astype(jnp.bfloat16), "dp", axis=0, tiled=True)
-    natural = jnp.take(gathered, tile_owner, axis=0).reshape((LAYERS, -1, BS, BS))
-    layer_weights = [split_layer(natural[0], heads_local, ff_local)]
+    shapes = layer_shapes(heads_local, ff_local)
+    layer_weights = [assemble(tile_owner, gathered, shapes)]
     flat_tokens = tokens.reshape(slot_count)
     positions = jnp.arange(slot_count, dtype=jnp.int32) % seq_len
     slot_length = jnp.repeat(lengths, seq_len)
@@ -403,23 +557,13 @@
             seq_len,
             heads_local,
         )
-        tile_parts[layer_index] = jnp.concatenate(
-            [matrix_to_tiles(one_grad) for one_grad in weight_grads], axis=0
-        )
+        tile_parts[layer_index] = scatter_tiles(tile_owner, weight_grads)
         bias_rows[layer_index] = in_bias_grad
         vector_rows[3 * layer_index : 3 * layer_index + 3] = list(vector_grads)
     embed_grad = jnp.dot(token_hot.T, residual_grad, precision=PRECISE)
     vectors_grad = jnp.stack(vector_rows)
     fc_bias_grad = jnp.stack(bias_rows)
-    natural_grads = tile_parts[0]
-    inverse = (
-        jnp.zeros_like(tile_owner)
-        .at[tile_owner]
-        .set(jnp.arange(tile_owner.shape[0], dtype=jnp.int32))
-    )
-    grad_share = lax.psum_scatter(
-        jnp.take(natural_grads, inverse, axis=0), "dp", scatter_dimension=0, tiled=True
-    )
+    grad_share = lax.psum_scatter(tile_parts[0], "dp", scatter_dimension=0, tiled=True)
     count_part = jnp.sum((lengths >= 2).astype(jnp.float32))
     embed_grad, head_grad, vectors_grad, fc_bias_grad, loss_sum, protein_count = lax.psum(
         (embed_grad, head_grad, vectors_grad, fc_bias_grad, loss_part, count_part), "dp"
@@ -443,17 +587,16 @@
     factor = jnp.minimum(1.0, CLIP_NORM / grad_norm)
     correct_one = 1.0 - jnp.power(BETA_ONE, step_count.astype(jnp.float32))
     correct_two = 1.0 - jnp.power(BETA_TWO, step_count.astype(jnp.float32))
-    results = soap_update(
+    results = soap(
+        jnp.stack([factor, correct_one, correct_two]),
+        grad_share,
         weight_tiles,
-        factor * grad_share,
         tiles_first,
         tiles_second,
         stats_left,
         stats_right,
         basis_left,
         basis_right,
-        correct_one,
-        correct_two,
     )
     embed_out = adamw_update(
         embedding, factor * embed_grad, embedding_first, embedding_second, correct_one, correct_two
@@ -471,13 +614,13 @@
         loss_sum / protein_count,
         grad_norm,
         results[0],
-        results[0].astype(jnp.bfloat16),
         results[1],
         results[2],
         results[3],
         results[4],
         results[5],
         results[6],
+        results[7],
         embed_out[0],
         embed_out[1],
         embed_out[2],

time: 1850 us -> 808 us (0.44)
  other arithmetic: 1120 us -> 58.5 us
  Pallas kernels: 0 us -> 73.1 us
  local copies, waits for them, and re-layouts: 95.3 us -> 51.1 us
  matrix products: 122 us -> 90 us
  waiting for transfers between devices: 405 us -> 429 us
    another operation x10 -> x5, other arithmetic: 1040 us -> 0.86 us  [the longest x1 0.59 us: local(): jnp.stack([factor, correct_one, correct_two])]
    pallas_call x0 -> x3, Pallas kernels: none -> 73.1 us  [the longest x1 55.9 us: soap(): pl.pallas_call(functools.partial(soap_kernel, count, per), grid=(count //...]
    dot_general x8 -> x0, matrix products: 32.8 us -> none  [the longest x1 6.89 us: orthonormal(): jnp.einsum('...ji,...jk->...ik', product, product, precision=PRECISE)]
    gather x2 -> x0, local copies, waits for them, and re-layouts: 26.4 us -> none  [the longest x1 15.5 us: local(): jnp.take(natural_grads, inverse, axis=0)]
    psum x1, waiting for transfers between devices: 112 us -> 135 us  [normed_combine(): return lax.psum(normed_grad, 'mp')]
  transfers between devices with their start and end apart: 5 -> 5, of which waited for: 5 -> 5; matrix products, arithmetic and copies ran while one was open for 4% -> 4% of each run, Pallas kernels for 0% -> 1%
where the time goes in v1:
time: 808 us; the launch traced here: 800 us
  waiting for transfers between devices  429 us (53%)
  matrix products  90 us (11%)
  Pallas kernels  73.1 us (9%)
  blocking collectives  65.4 us (8%)
  other arithmetic  58.5 us (7%)
  local copies, waits for them, and re-layouts  51.1 us (6%)
  between operations  25 us (3%)
    psum x1, waiting for transfers between devices, mixed_rows(): return lax.psum(branch_part, 'mp')  153 us
    psum x1, waiting for transfers between devices, normed_combine(): return lax.psum(normed_grad, 'mp')  135 us
    reduce_scatter x1, waiting for transfers between devices, local(): lax.psum_scatter(tile_parts[0], 'dp', scatter_dimension=0, tiled=True)  90.2 us
    pallas_call x1, Pallas kernels, soap(): pl.pallas_call(functools.partial(soap_kernel, count, per), grid=(count //...  55.9 us
    all_gather x1, waiting for transfers between devices, local(): lax.all_gather(weight_tiles.astype(jnp.bfloat16), 'dp', axis=0, tiled=True)  42.2 us
    psum x1, blocking collectives, local(): grad_norm = jnp.sqrt(lax.psum(square_part, ('dp', 'mp')))  39.4 us
    psum x1, blocking collectives, local(): lax.psum((embed_grad, head_grad, vectors_grad, fc_bias_grad, loss_part, c...  26 us
    dynamic_update_slice x4, local copies, waits for them, and re-layouts, attention_forward(): lax.map(one_block, jnp.arange(block_count, dtype=jnp.int32))  21.9 us
  transfers between devices with their start and end apart: 5, of which 5 were waited for; matrix products, arithmetic and copies ran while one was open for 4% of the time, Pallas kernels for 1%

profile of v1, /device:TPU:0, one launch (start us, length us, event | category | flops | bytes accessed | tf_op | source)
XLA Modules:
  0.0 800.1 jit_solution(378725686058390727)
XLA Ops:
  7.2 2.4 convert_element_type.124
  10.4 2.9 fusion.81
  16.5 42.2 %all-gather.2.cloned.1.call-done.tiles = bf16[192,128,128]{2,1,0:T(8,128)(2,1)} async-done(((bf16[24,128,128]{2,1,0:T(8,128)(2,1)}), bf16[192,128,128]{2,1,0:T(8,128)(2,1)}) %all-gather.2.cloned.1.call-update) | async-done | bytes 6291472 | tf_op jit(solution)/shard_map/all_gather | solution.py:495
  58.7 7.1 assemble.1
  65.8 3.3 fusion.84
  69.7 21.8 %while.31 = (s32[]{:T(128)}, bf16[2,512,4,64]{1,3,2,0:T(8,128)(2,1)}, f32[2,4,512]{2,1,0:T(4,128)S(1)}, s32[2]{0:T(128)S(1)}, s32[1024]{0:T(1024)S(1)}, /*index=...) while((s32[]{:T(128)}, ...), condition=%wide.region_5.6_spmd, body=%wide.region_2.5_spmd.sunk | while | flops 563084800 | bytes 33364428 | solution.py:323
  74.5 2.3 fusion.149
  76.9 3.0 fusion.150
  85.3 2.3 fusion.149
  87.7 3.0 fusion.150
  93.2 4.8 fusion.85
  98.1 2.6 fusion.71
  100.7 2.7 convolution_add_fusion
  105.6 153.0 %all-reduce.6.cloned.1.call-done = f32[1024,1024]{0,1:T(8,128)} async-done(((f32[1024,1024]{0,1:T(8,128)}), f32[1024,1024]{0,1:T(8,128)}) %all-reduce.6.cloned.1.call-update) | async-done | bytes 4194320 | tf_op jit(solution)/shard_map/psum | solution.py:280
  258.6 4.0 fusion.79
  266.8 3.3 fusion.83
  270.1 5.4 copy.64
  275.5 5.4 multiply_reduce_fusion.1
  287.8 6.8 convert_reduce_fusion.1
  294.6 60.3 %while.32 = (s32[]{:T(128)}, f32[1024,4,64]{0,2,1:T(8,128)S(1)}, f32[1024,4,64]{0,2,1:T(8,128)}, f32[2,512,4,64]{1,0,3,2:T(2,128)}, s32[2]{0:T(128)S(1)}, /*inde...) while((s32[]{:T(128)}, f32[1024,4,64]{0,2,1:T(8,128)S(1)}, ...), condition=%wide.region_19.20_spmd.clone, body=%wide.region_17.19_spmd.clone.sunk | while | flops 1376124416 | bytes 82901536 | solution.py:365
  301.0 3.6 fusion.163
  304.6 4.5 multiply_reduce_fusion.14
  309.2 2.4 multiply_convert_fusion.7
  314.5 10.4 %dynamic_update_slice.28 = f32[2,512,4,64]{1,0,3,2:T(2,128)} dynamic-update-slice(f32[2,512,4,64]{1,0,3,2:T(2,128)} %get-tuple-element.632, f32[1,512,4,64]{1,0,3,2:T(1,128)S(1)} %copy.101, s32[]{:T(128)S(6)} %copy.119, s32[]{:T(128)} %constant.229.clone.1..sunk.1, s32[]{:T(128)} %constant.229.clone.1..sunk.1, s32[]{:T(128)} %constant.229.clone.1..sunk.1) | dynamic-update-slice | bytes 1048580 | tf_op jit(solution)/shard_map/while/body/jit(dynamic_update_index_in_dim)/dynamic_update_slice | solution.py:323
  331.1 3.6 fusion.163
  334.6 4.5 multiply_reduce_fusion.14
  339.2 2.4 multiply_convert_fusion.7
  344.5 10.4 %dynamic_update_slice.28 = f32[2,512,4,64]{1,0,3,2:T(2,128)} dynamic-update-slice(f32[2,512,4,64]{1,0,3,2:T(2,128)} %get-tuple-element.632, f32[1,512,4,64]{1,0,3,2:T(1,128)S(1)} %copy.101, s32[]{:T(128)S(6)} %copy.119, s32[]{:T(128)} %constant.229.clone.1..sunk.1, s32[]{:T(128)} %constant.229.clone.1..sunk.1, s32[]{:T(128)} %constant.229.clone.1..sunk.1) | dynamic-update-slice | bytes 1048580 | tf_op jit(solution)/shard_map/while/body/jit(dynamic_update_index_in_dim)/dynamic_update_slice | solution.py:323
  354.9 2.2 reshape.357
  359.4 2.4 fusion.89
  363.6 3.8 convolution_add_fusion.1
  370.4 6.3 fusion.86.refs_0_
  376.7 4.3 fusion.88.refs_2_
  381.1 5.2 fusion.70.refs_3_
  386.3 135.3 %all-reduce.8.cloned.1.call-done = f32[1024,1024]{0,1:T(8,128)} async-done(((f32[1024,1024]{0,1:T(8,128)}), f32[1024,1024]{0,1:T(8,128)}) %all-reduce.8.cloned.1.call-update) | async-done | bytes 4194320 | tf_op jit(solution)/shard_map/psum | solution.py:284
  521.6 4.5 fusion.72
  527.5 2.1 multiply_reduce_fusion.2
  529.7 4.2 fusion.44
  535.9 10.1 %scatter.1 = f32[192,128,128]{2,1,0:T(8,128)} custom-call(s32[192]{0:T(256)} %owner.3, f32[1024,768]{1,0:T(8,128)} %fusion.86.refs_0_, f32[256,1024]{1,0:T(8,128)} %fusion.87.refs_1_, f32[1024,1024]{1,0:T(8,128)} %fusion.88.refs_2_, f32[1024,1024]{1,0:T(8,128)} %fusion.70.refs_3_), custom_call_target="tpu_custom_call" | custom-call | tf_op jit(solution)/shard_map/scatter/pallas_call | solution.py:95
  548.5 26.0 %all-reduce = (f32[]{:T(128)}, f32[]{:T(128)}, f32[1,1024]{1,0:T(1,128)S(1)}, f32[5,1024]{1,0:T(8,128)S(1)}) all-reduce(f32[]{:T(128)S(6)} %neg.9, f32[]{:T(128)} %bitcast.19, f32[1,1024]{1,0:T(1,128)S(1)} %bitcast.164, f32[5,1024]{1,0:T(8,128)S(1)} %stack.47), channel_id=1, replica_groups=mesh['dp'=8,'mp'=4] {'dp'}, use_global_device_ids=true, to_apply=%region_13.14 | all-reduce | flops 6146 | bytes 49168 | tf_op jit(solution)/shard_map/psum | solution.py:568
  577.7 8.0 all-reduce.10.cloned.1.call-done
  585.7 2.2 multiply_reduce_fusion.9
  587.9 2.2 multiply_reduce_fusion.8
  592.1 90.2 %reduce-scatter.2.cloned.1.call-done = f32[24,128,128]{2,1,0:T(8,128)} async-done(((f32[192,128,128]{2,1,0:T(8,128)}), f32[24,128,128]{2,1,0:T(8,128)}) %reduce-scatter.2.cloned.1.call-update) | async-done | bytes 1572880 | tf_op jit(solution)/shard_map/reduce_scatter | solution.py:566
  682.2 4.2 multiply_reduce_fusion.7
  688.4 39.4 %psum.71 = f32[]{:T(128)} all-reduce(f32[]{:T(128)S(6)} %add.374), channel_id=1, replica_groups=mesh['dp'=8,'mp'=4] {'dp','mp'}, use_global_device_ids=true, to_apply=%region_40.41 | all-reduce | flops 1 | bytes 8 | tf_op jit(solution)/shard_map/psum | solution.py:586
  729.8 2.4 multiply_subtract_fusion.1
  734.9 55.9 %soap_tiles.1 = (f32[24,128,128]{2,1,0:T(8,128)}, bf16[24,128,128]{2,1,0:T(8,128)(2,1)}, f32[24,128,128]{2,1,0:T(8,128)}, f32[24,128,128]{2,1,0:T(8,128)}, f32[2...) custom-call(f32[3]{0:T(128)} %pad_maximum_fusion.4.scal, ...), custom_call_target="tpu_custom_call" | custom-call | tf_op jit(solution)/shard_map/soap_tiles/pallas_call | solution.py:261
  (253 shorter events, 58.7 us)
Async XLA Ops:
  7.2 51.5 %all-gather.2.cloned.1.call-start = ((), (), s32[]{:S(2)}) async-start(), calls=%async_computation.1 | async-start | bytes 7077888 | tf_op jit(solution)/shard_map/all_gather | solution.py:495
  9.7 248.9 %all-reduce.6.cloned.1.call-start = ((), (), s32[]{:S(2)}) async-start(), calls=%async_computation.2 | async-start | bytes 8388608 | tf_op jit(solution)/shard_map/psum | solution.py:280
  10.4 4.4 copy-start.39
  13.3 3.1 copy-start.31
  14.8 51.0 %copy-start.41 = (f32[1024]{0:T(1024)}, f32[1024]{0:T(1024)S(1)}, u32[]{:S(2)}) copy-start(f32[1024]{0:T(1024)S(1)} %fusion.67) | copy-start | bytes 12292
  14.9 50.9 %copy-start.37 = (f32[1,1024]{1,0:T(1,128)}, f32[1,1024]{1,0:T(1,128)S(1)}, u32[]{:S(2)}) copy-start(f32[1,1024]{1,0:T(1,128)S(1)} %get-tuple-element.428) | copy-start | bytes 12292
  15.8 53.6 %copy-start.23 = (f32[1024,16]{0,1:T(8,128)}, f32[1024,16]{0,1:T(8,128)S(1)}, u32[]{:S(2)}) copy-start(f32[1024,16]{0,1:T(8,128)S(1)} %get-tuple-element.432) | copy-start | bytes 196612
  16.5 52.6 %copy-start.14 = (bf16[1024,1024]{0,1:T(8,128)(2,1)}, bf16[1024,1024]{0,1:T(8,128)(2,1)S(1)}, u32[]{:S(2)}) copy-start(bf16[1024,1024]{0,1:T(8,128)(2,1)S(1)} %add_convert_fusion.1) | copy-start | bytes 6291460
  93.2 7.5 copy-start.12
  93.2 4.9 copy-start.56
  93.2 4.9 copy-start.61
  103.4 418.1 %all-reduce.8.cloned.1.call-start = ((), (), s32[]{:S(2)}) async-start(), calls=%async_computation.4 | async-start | bytes 8388608 | tf_op jit(solution)/shard_map/psum | solution.py:284
  275.5 5.4 copy-start.3
  275.5 5.9 copy-start.7
  282.5 3.0 copy-start.4
  282.5 2.9 copy-start.43
  282.5 3.7 copy-start.62
  282.5 5.3 copy-start.65
  283.6 11.0 %copy-start.10 = (bf16[1024,1024]{0,1:T(8,128)(2,1)}, bf16[1024,1024]{0,1:T(8,128)(2,1)S(1)}, u32[]{:S(2)}) copy-start(bf16[1024,1024]{0,1:T(8,128)(2,1)S(1)} %get-tuple-element.399) | copy-start | bytes 6291460
  294.6 62.6 %copy-start.24 = (f32[1024,16]{0,1:T(8,128)S(1)}, f32[1024,16]{0,1:T(8,128)}, u32[]{:S(2)}) copy-start(f32[1024,16]{0,1:T(8,128)} %copy-done.23) | copy-start | bytes 196612
  294.6 62.6 %copy-start.30 = (f32[1024,16]{0,1:T(8,128)S(1)}, f32[1024,16]{0,1:T(8,128)}, u32[]{:S(2)}) copy-start(f32[1024,16]{0,1:T(8,128)} %get-tuple-element.430) | copy-start | bytes 196612
  304.6 4.6 copy-start.20
  334.6 4.6 copy-start.20
  367.4 218.2 %all-reduce.10.cloned.1.call-start = ((), (), s32[]{:S(2)}) async-start(), calls=%async_computation.5 | async-start | bytes 557056 | tf_op jit(solution)/shard_map/psum | solution.py:568
  370.4 6.3 copy-start.15
  370.4 6.3 copy-start.68
  376.7 4.3 copy-start.11
  376.7 4.3 copy-start.66
  381.1 140.5 %copy-start.32 = (f32[1024]{0:T(1024)S(1)}, f32[1024]{0:T(1024)}, u32[]{:S(2)}) copy-start(f32[1024]{0:T(1024)} %copy-done.31) | copy-start | bytes 12292
  381.1 140.5 %copy-start.38 = (f32[1,1024]{1,0:T(1,128)S(1)}, f32[1,1024]{1,0:T(1,128)}, u32[]{:S(2)}) copy-start(f32[1,1024]{1,0:T(1,128)} %copy-done.37) | copy-start | bytes 12292
  386.3 139.8 %copy-start.48 = (f32[1024]{0:T(1024)S(1)}, f32[1024]{0:T(1024)}, u32[]{:S(2)}) copy-start(f32[1024]{0:T(1024)} %copy-done.47) | copy-start | bytes 12292
  386.3 139.9 %copy-start.42 = (f32[1024]{0:T(1024)S(1)}, f32[1024]{0:T(1024)}, u32[]{:S(2)}) copy-start(f32[1024]{0:T(1024)} %copy-done.41) | copy-start | bytes 12292
  521.6 4.6 copy-start.1
  521.6 5.9 copy-start.6
  529.7 4.5 copy-start.13
  533.9 148.3 %reduce-scatter.2.cloned.1.call-start = ((), (), s32[]{:S(2)}) async-start(), calls=%async_computation.3 | async-start | bytes 14155776 | tf_op jit(solution)/shard_map/reduce_scatter | solution.py:566
  546.1 182.4 %copy-start.40 = (f32[5,1024]{1,0:T(8,128)S(1)}, f32[5,1024]{1,0:T(8,128)}, u32[]{:S(2)}) copy-start(f32[5,1024]{1,0:T(8,128)} %param.44) | copy-start | bytes 61444
  546.1 182.4 %copy-start.49 = (f32[5,1024]{1,0:T(8,128)S(1)}, f32[5,1024]{1,0:T(8,128)}, u32[]{:S(2)}) copy-start(f32[5,1024]{1,0:T(8,128)} %param.46) | copy-start | bytes 61444
  546.1 182.4 %copy-start.50 = (f32[5,1024]{1,0:T(8,128)S(1)}, f32[5,1024]{1,0:T(8,128)}, u32[]{:S(2)}) copy-start(f32[5,1024]{1,0:T(8,128)} %param.45) | copy-start | bytes 61444
  546.1 183.7 %copy-start.27 = (f32[32,1024]{1,0:T(8,128)S(1)}, f32[32,1024]{1,0:T(8,128)}, u32[]{:S(2)}) copy-start(f32[32,1024]{1,0:T(8,128)} %param.38) | copy-start | bytes 393220
  546.1 183.7 %copy-start.35 = (f32[32,1024]{1,0:T(8,128)S(1)}, f32[32,1024]{1,0:T(8,128)}, u32[]{:S(2)}) copy-start(f32[32,1024]{1,0:T(8,128)} %param.40) | copy-start | bytes 393220
  546.1 183.7 %copy-start.36 = (f32[32,1024]{1,0:T(8,128)S(1)}, f32[32,1024]{1,0:T(8,128)}, u32[]{:S(2)}) copy-start(f32[32,1024]{1,0:T(8,128)} %param.39) | copy-start | bytes 393220
  546.2 186.0 %copy-start.18 = (f32[1025,32]{0,1:T(8,128)S(1)}, f32[1025,32]{0,1:T(8,128)}, u32[]{:S(2)}) copy-start(f32[1025,32]{0,1:T(8,128)} %param.41) | copy-start | bytes 393604
  546.2 186.0 %copy-start.33 = (f32[1025,32]{0,1:T(8,128)S(1)}, f32[1025,32]{0,1:T(8,128)}, u32[]{:S(2)}) copy-start(f32[1025,32]{0,1:T(8,128)} %param.43) | copy-start | bytes 393604
  546.2 186.0 %copy-start.34 = (f32[1025,32]{0,1:T(8,128)S(1)}, f32[1025,32]{0,1:T(8,128)}, u32[]{:S(2)}) copy-start(f32[1025,32]{0,1:T(8,128)} %param.42) | copy-start | bytes 393604
  546.2 188.1 %copy-start.57 = (f32[1,1024]{1,0:T(1,128)S(1)}, f32[1,1024]{1,0:T(1,128)}, u32[]{:S(2)}) copy-start(f32[1,1024]{1,0:T(1,128)} %param.49) | copy-start | bytes 12292
  546.2 188.1 %copy-start.58 = (f32[1,1024]{1,0:T(1,128)S(1)}, f32[1,1024]{1,0:T(1,128)}, u32[]{:S(2)}) copy-start(f32[1,1024]{1,0:T(1,128)} %param.48) | copy-start | bytes 12292
  585.7 146.5 %copy-start.22 = (f32[1025,32]{0,1:T(8,128)S(1)}, f32[1025,32]{0,1:T(8,128)}, u32[]{:S(2)}) copy-start(f32[1025,32]{0,1:T(8,128)} %get-tuple-element.379) | copy-start | bytes 393604
  (30 other events, 54.2 us)
Sparse Core Ops, SparseCore 0:
  10.5 48.2 all-gather.1
  103.5 154.9 all-reduce.5
  367.6 153.9 all-reduce.7
  534.0 51.5 all-reduce.9
  589.0 93.1 reduce-scatter.1

commit v2 on v1

v2 whole, which is shorter than its diff:
```python
import functools
import math

import jax
import jax.numpy as jnp
import numpy as np
from jax import lax
from jax.experimental import pallas as pl
from jax.experimental.pallas import tpu as pltpu
from jax.sharding import PartitionSpec as P

D = 1024
H = 16
HD = 64
ROT = 32
BS = 128
HB = 64
ROWS = 256
WIDE = 128
MEGA = 1024 * 1024

NORM_EPS = 1e-05
CLIP_NORM = 0.02
RATE_TILES = 0.02
RATE_SMALL = 0.2
BETA_ONE = 0.9
BETA_TWO = 0.95
ADAM_EPS = 1e-08
WEIGHT_DECAY = 0.01
MASKED = -1e30
GELU_A = math.sqrt(2.0 / math.pi)
GELU_B = 0.044715

NN = (((1,), (0,)), ((), ()))
NT = (((1,), (1,)), ((), ()))
TN = (((0,), (0,)), ((), ()))
f32 = jnp.float32
bf16 = jnp.bfloat16
SMEM = pl.BlockSpec(memory_space=pltpu.SMEM)
VMEM = pl.BlockSpec(memory_space=pltpu.VMEM)
ANY = pl.BlockSpec(memory_space=pl.ANY)


def dot(a, b, dims=NN):
    return lax.dot_general(a, b, dims, preferred_element_type=f32)


def split2(a):
    high = a.astype(bf16)
    return high, (a - high.astype(f32)).astype(bf16)


def split3(a):
    high = a.astype(bf16)
    rest = a - high.astype(f32)
    middle = rest.astype(bf16)
    return high, middle, (rest - middle.astype(f32)).astype(bf16)


def dot3(a, b, dims):
    (axis_a,), (axis_b,) = dims[0]
    ah, al = split2(a)
    bh, bl = split2(b)
    return dot(
        jnp.concatenate([ah, ah, al], axis=axis_a),
        jnp.concatenate([bh, bl, bh], axis=axis_b),
        dims,
    )


def dot6(a, b, dims):
    (axis_a,), (axis_b,) = dims[0]
    ah, am, al = split3(a)
    bh, bm, bl = split3(b)
    return dot(
        jnp.concatenate([ah, ah, am, am, ah, al], axis=axis_a),
        jnp.concatenate([bh, bm, bh, bm, bl, bh], axis=axis_b),
        dims,
    )


def rows_times_low(a, low, dims):
    count = a.shape[0]
    parts = dot(jnp.concatenate(split3(a), axis=0), low, dims)
    return parts[:count] + (parts[count : 2 * count] + parts[2 * count :])


def lanes(shape):
    return lax.broadcasted_iota(jnp.int32, shape, len(shape) - 1)


def sublanes(shape):
    return lax.broadcasted_iota(jnp.int32, shape, len(shape) - 2)


def stats_of(values):
    centred = values - jnp.mean(values, axis=-1, keepdims=True)
    spread = jnp.mean(centred * centred, axis=-1, keepdims=True)
    scale = lax.rsqrt(spread + NORM_EPS)
    return centred * scale, scale


def norm_back(grad, normed, scale, gain):
    inner = grad * gain
    mean_one = jnp.mean(inner, axis=-1, keepdims=True)
    mean_two = jnp.mean(inner * normed, axis=-1, keepdims=True)
    return scale * (inner - mean_one - normed * mean_two)


def swap_with(value, axis, mask):
    count = lax.axis_size(axis)
    return lax.ppermute(value, axis, [(i, i ^ mask) for i in range(count)])


def tree_sum(parts):
    while len(parts) > 1:
        parts = [parts[i] + parts[i + 1] for i in range(0, len(parts), 2)]
    return parts[0]


def gather_xor(value, axis):
    return [value] + [swap_with(value, axis, r) for r in range(1, lax.axis_size(axis))]


def gather_tiles(low):
    count = lax.axis_size("dp")
    bits = [1 << k for k in reversed(range(count.bit_length() - 1))]
    half = low.shape[0] // 2
    result = []
    for which in range(2):
        order = bits if which == 0 or len(bits) < 3 else [bits[1], bits[0]] + bits[2:]
        pieces = {0: low[which * half : (which + 1) * half]}
        for bit in order:
            for mask in list(pieces):
                pieces[mask ^ bit] = swap_with(pieces[mask], "dp", bit)
        result.append([pieces[r] for r in range(count)])
    return result


def sum_dp(value):
    count = lax.axis_size("dp")
    upper = (lax.axis_index("dp") & 1) == 1
    half = value.shape[0] // 2
    first, second = value[:half], value[half:]
    kept = jnp.where(upper, second, first) + swap_with(jnp.where(upper, first, second), "dp", 1)
    total = tree_sum([kept] + [swap_with(kept, "dp", r) for r in range(2, count, 2)])
    other = swap_with(total, "dp", 1)
    return jnp.concatenate([jnp.where(upper, other, total), jnp.where(upper, total, other)], axis=0)


def layer_shapes(heads_local, ff_local):
    return ((D, 3 * heads_local * HD), (heads_local * HD, D), (D, ff_local), (ff_local, D))


def tile_places(shapes):
    places = []
    for which, (row_total, col_total) in enumerate(shapes):
        for i in range(row_total // BS):
            for k in range(col_total // BS):
                places.append((which, i, k))
    return places


def tables_kernel(places, heads, pieces_n, place, *refs):
    pieces = refs[:pieces_n]
    (embed, vec, bias), refs = refs[pieces_n : pieces_n + 3], refs[pieces_n + 3 :]
    mats, (proj_o, upper_o, payload_o, normed_o, act_o, values_o, tiles, sems) = refs[:4], refs[4:]
    size = pieces[0].shape[0]
    copies = [
        pltpu.make_async_copy(piece, tiles.at[pl.ds(k * size, size)], sems.at[k])
        for k, piece in enumerate(pieces)
    ]
    for copy in copies:
        copy.start()
    normed, _ = stats_of(embed[...])
    low = (normed * vec[0:1] + vec[1:2]).astype(bf16)
    normed_o[...] = low
    for copy in copies:
        copy.wait()
    for index, (which, i, k) in enumerate(places):
        mats[which][i * BS : (i + 1) * BS, k * BS : (k + 1) * BS] = tiles[place[index]]
    proj = dot(low, mats[0][...])
    proj_o[...] = proj
    upper = dot(low, mats[2][...]) + bias[...]
    upper_o[...] = upper
    act = (0.5 * upper * (1.0 + jnp.tanh(GELU_A * (upper + GELU_B * (upper * upper * upper))))).astype(
        bf16
    )
    act_o[...] = act
    down = dot(act, mats[3][...])
    vocab = embed.shape[0]
    values = proj[:, 2 * heads * HD :]
    shape = (heads * vocab, heads * HD)
    values = jnp.concatenate([values] * heads, axis=0)
    same = sublanes(shape) // vocab == lanes(shape) // HD
    values = jnp.where(same, values, 0.0).astype(bf16)
    values_o[...] = values
    mixed = dot(values, mats[1][...])
    high, rest = split2(down)
    payload_o[...] = jnp.concatenate([mixed.astype(bf16), high, rest], axis=0)


def tables(place, pieces, embedding, vectors, fc_bias, heads, ff_local):
    shapes = layer_shapes(heads, ff_local)
    vocab = embedding.shape[0]
    o = jax.ShapeDtypeStruct
    total = len(pieces) * pieces[0].shape[0]
    return pl.pallas_call(
        functools.partial(tables_kernel, tile_places(shapes), heads, len(pieces)),
        in_specs=[SMEM] + [ANY] * len(pieces) + [VMEM] * 3,
        out_specs=[VMEM] * 10,
        out_shape=[o(shape, bf16) for shape in shapes]
        + [
            o((vocab, 3 * heads * HD), f32),
            o((vocab, ff_local), f32),
            o(((heads + 2) * vocab, D), bf16),
            o((vocab, D), bf16),
            o((vocab, ff_local), bf16),
            o((heads * vocab, heads * HD), bf16),
        ],
        scratch_shapes=[
            pltpu.VMEM((total, BS, BS), bf16),
            pltpu.SemaphoreType.DMA((len(pieces),)),
        ],
        compiler_params=pltpu.CompilerParams(vmem_limit_bytes=56 * MEGA),
        name="tables",
    )(place, *pieces, embedding, vectors, fc_bias)


def rotary_tables(seq_len):
    half = ROT // 2
    frequency = np.float32(10000.0) ** (
        np.float32(-2.0) * np.arange(half, dtype=np.float32) / np.float32(ROT)
    )
    angles = np.arange(seq_len, dtype=np.float32)[:, None] * frequency[None, :].astype(np.float32)
    cosine = np.cos(angles.astype(np.float64)).astype(np.float32)
    sine = np.sin(angles.astype(np.float64)).astype(np.float32)
    wide_cos = np.ones((seq_len, WIDE), np.float32)
    wide_sin = np.zeros((seq_len, WIDE), np.float32)
    wide_cos[:, :half], wide_cos[:, half:ROT] = cosine, cosine
    wide_sin[:, :half], wide_sin[:, half:ROT] = sine, sine
    return wide_cos, wide_sin, np.ascontiguousarray(cosine.T), np.ascontiguousarray(sine.T)


def turned(x):
    half = ROT // 2
    lane = lanes(x.shape)
    return jnp.where(
        lane < half,
        -pltpu.roll(x, WIDE - half, 1),
        jnp.where(lane < ROT, pltpu.roll(x, half, 1), 0.0),
    )


def head_lanes(table, index):
    begin = index // 2 * WIDE
    chunk = table[:, begin : begin + WIDE]
    if index % 2:
        chunk = pltpu.roll(chunk, HD, 1)
    return jnp.where(lanes(chunk.shape) < HD, chunk, 0.0)


def stack_parts(table):
    high, middle, rest = split3(table)
    return jnp.concatenate([high, middle, rest, jnp.zeros_like(high)], axis=0)


def attention_kernel(
    heads, length, token_col, proj, cosine, sine, query_o, key_o, weight_o, hot, key_hot, queries, wide
):
    seq = token_col.shape[0]
    vocab = proj.shape[0]
    lane = lanes((seq, WIDE))
    hot[...] = jnp.where(lane % vocab == token_col[...], 1.0, 0.0).astype(bf16)
    for h in range(heads):
        key_hot[h] = jnp.where(lane == token_col[...] + h * vocab, 1.0, 0.0).astype(bf16)
    one = lanes((vocab, WIDE)) == HD
    ones = (lanes((vocab, WIDE)) > HD) & (lanes((vocab, WIDE)) < HD + 4)
    for which in range(2):
        for h in range(heads):
            own = head_lanes(proj, which * heads + h)
            other = turned(own)
            if which == 0:
                own = jnp.where(one, 1.0, own * 0.125)
                other = other * 0.125
            else:
                own = jnp.where(one | ones, 1.0, own)
            begin = (which * heads + h) * 2 * WIDE
            wide[:, begin : begin + WIDE] = stack_parts(own)
            wide[:, begin + WIDE : begin + 2 * WIDE] = stack_parts(other)
    for i in range(seq // ROWS):
        span = slice(i * ROWS, (i + 1) * ROWS)
        part = hot[span]
        position = i * ROWS + sublanes((ROWS, WIDE))
        bias = jnp.where(position < length[0], 0.0, MASKED)
        cos, sin = cosine[span], sine[span]
        key_cos = jnp.where(lanes((ROWS, WIDE)) == HD, bias, cos)
        for h in range(heads):
            both = dot(part, wide[:, h * 2 * WIDE : (h + 1) * 2 * WIDE])
            queries[h, span] = (both[:, :WIDE] * cos + both[:, WIDE:] * sin).astype(bf16)
            k = heads + h
            both = dot(part, wide[:, k * 2 * WIDE : (k + 1) * 2 * WIDE])
            key_o[h, span] = (both[:, :WIDE] * key_cos + both[:, WIDE:] * sin).astype(bf16)
    allowed = lanes((ROWS, ROWS)) <= sublanes((ROWS, ROWS))
    small = lanes((ROWS, WIDE))
    for i in range(seq // ROWS):
        span = slice(i * ROWS, (i + 1) * ROWS)
        past = i * ROWS
        weights = jnp.zeros((ROWS, WIDE), f32)
        for h in range(heads):
            query = queries[h, span]
            near = jnp.where(allowed, dot(query, key_o[h, span], NT), MASKED)
            top = jnp.max(near, axis=-1, keepdims=True)
            if past:
                far = dot(query, key_o[h, :past], NT)
                top = jnp.maximum(top, jnp.max(far, axis=-1, keepdims=True))
                far = jnp.exp(far - top)
            near = jnp.exp(near - top)
            total = jnp.sum(near, axis=-1, keepdims=True)
            if past:
                total = total + jnp.sum(far, axis=-1, keepdims=True)
            share = 1.0 / total
            weights = weights + dot((near * share).astype(bf16), key_hot[h, span])
            if past:
                weights = weights + dot((far * share).astype(bf16), key_hot[h, :past])
            minus = -(top + jnp.log(total))
            high = minus.astype(bf16).astype(f32)
            middle = (minus - high).astype(bf16).astype(f32)
            rest = minus - high - middle
            query_o[h, span] = jnp.where(
                small == HD + 1,
                high,
                jnp.where(
                    small == HD + 2, middle, jnp.where(small == HD + 3, rest, query.astype(f32))
                ),
            ).astype(bf16)
        weight_o[span] = weights[:, : heads * vocab]


def attention(length, token_col, proj, cosine, sine, heads):
    seq = token_col.shape[0]
    vocab = proj.shape[0]
    o = jax.ShapeDtypeStruct
    return pl.pallas_call(
        functools.partial(attention_kernel, heads),
        in_specs=[SMEM] + [VMEM] * 4,
        out_specs=[VMEM] * 3,
        out_shape=[
            o((heads, seq, WIDE), bf16),
            o((heads, seq, WIDE), bf16),
            o((seq, heads * vocab), f32),
        ],
        scratch_shapes=[
            pltpu.VMEM((seq, WIDE), bf16),
            pltpu.VMEM((heads, seq, WIDE), bf16),
            pltpu.VMEM((heads, seq, WIDE), bf16),
            pltpu.VMEM((WIDE, heads * 4 * WIDE), bf16),
        ],
        compiler_params=pltpu.CompilerParams(vmem_limit_bytes=56 * MEGA),
        name="attention",
    )(length, token_col, proj, cosine, sine)


def attention_back_kernel(
    heads,
    token_col,
    token_row,
    query,
    key,
    weight,
    weight_grad,
    cosine,
    sine,
    cosine_t,
    sine_t,
    table_o,
    hot,
    mixed,
    query_grad,
    key_grad,
):
    seq = token_col.shape[0]
    vocab = weight.shape[1] // heads
    half = ROT // 2
    lane = lanes((seq, WIDE))
    hot[...] = jnp.where(
        (lane == token_col[...]) | (lane == token_col[...] + vocab) | ((lane >= HD) & (lane < HD + 3)),
        1.0,
        0.0,
    ).astype(bf16)
    both = weight[...] * weight_grad[...]
    grads = weight_grad[...]
    if heads * vocab < WIDE:
        pad = jnp.zeros((seq, WIDE - heads * vocab), f32)
        both = jnp.concatenate([both, pad], axis=1)
        grads = jnp.concatenate([grads, pad], axis=1)
    for h in range(heads):
        inside = (lane >= h * vocab) & (lane < (h + 1) * vocab)
        minus = -jnp.sum(jnp.where(inside, both, 0.0), axis=-1, keepdims=True)
        own = grads if h == 0 else pltpu.roll(grads, WIDE - h * vocab, 1)
        own = jnp.where(lane < vocab, own, 0.0)
        high, rest = split2(own)
        m_high = minus.astype(bf16).astype(f32)
        m_middle = (minus - m_high).astype(bf16).astype(f32)
        m_rest = minus - m_high - m_middle
        value = high.astype(f32) + pltpu.roll(rest.astype(f32), vocab, 1)
        value = jnp.where(lane == HD, m_high, value)
        value = jnp.where(lane == HD + 1, m_middle, value)
        value = jnp.where(lane == HD + 2, m_rest, value)
        mixed[h] = value.astype(bf16)
    allowed = lanes((ROWS, ROWS)) <= sublanes((ROWS, ROWS))
    key_grad[...] = jnp.zeros_like(key_grad)
    for h in range(heads):
        for i in range(seq // ROWS):
            span = slice(i * ROWS, (i + 1) * ROWS)
            past = i * ROWS
            part = query[h, span]
            near = jnp.where(allowed, jnp.exp(dot(part, key[h, span], NT)), 0.0)
            near = (near * dot(mixed[h, span], hot[span], NT)).astype(bf16)
            grad = dot(near, key[h, span])
            key_grad[h, :, span] += dot(part, near, TN)[:HD]
            if past:
                far = jnp.exp(dot(part, key[h, :past], NT))
                far = (far * dot(mixed[h, span], hot[:past], NT)).astype(bf16)
                grad = grad + dot(far, key[h, :past])
                key_grad[h, :, :past] += dot(part, far, TN)[:HD]
            grad = grad * 0.125
            query_grad[h, span] = (grad * cosine[span] - turned(grad) * sine[span]).astype(bf16)
    shape = (vocab, seq)
    token_hot = jnp.where(sublanes(shape) == token_row[...], 1.0, 0.0).astype(bf16)
    small = lanes((vocab, WIDE)) < HD
    cos_t, sin_t = cosine_t[...], sine_t[...]
    for pair in range(heads // 2):
        one = dot(token_hot, query_grad[2 * pair])
        two = pltpu.roll(dot(token_hot, query_grad[2 * pair + 1]), HD, 1)
        table_o[:, pair * WIDE : (pair + 1) * WIDE] = jnp.where(small, one, two)
        turned_keys = []
        for h in (2 * pair, 2 * pair + 1):
            front, back = key_grad[h, :half], key_grad[h, half:ROT]
            turned_keys += [
                front * cos_t + back * sin_t,
                back * cos_t - front * sin_t,
                key_grad[h, ROT:],
            ]
        keys = jnp.concatenate(turned_keys, axis=0).astype(bf16)
        begin = heads * HD + pair * WIDE
        table_o[:, begin : begin + WIDE] = dot(token_hot, keys, NT)


def attention_back(
    token_col, token_row, query, key, weight, weight_grad, cosine, sine, cosine_t, sine_t, heads
):
    seq = token_col.shape[0]
    vocab = weight.shape[1] // heads
    return pl.pallas_call(
        functools.partial(attention_back_kernel, heads),
        in_specs=[VMEM] * 10,
        out_specs=VMEM,
        out_shape=jax.ShapeDtypeStruct((vocab, 2 * heads * HD), f32),
        scratch_shapes=[
            pltpu.VMEM((seq, WIDE), bf16),
            pltpu.VMEM((heads, seq, WIDE), bf16),
            pltpu.VMEM((heads, seq, WIDE), bf16),
            pltpu.VMEM((heads, HD, seq), f32),
        ],
        compiler_params=pltpu.CompilerParams(vmem_limit_bytes=56 * MEGA),
        name="attention_back",
    )(token_col, token_row, query, key, weight, weight_grad, cosine, sine, cosine_t, sine_t)


def loss_kernel(
    parts,
    heads,
    ints,
    floats,
    token_col,
    target_col,
    token_row,
    embed,
    head,
    vec,
    *refs,
):
    weights, refs = refs[:parts], refs[parts:]
    payloads, refs = refs[:parts], refs[parts:]
    sums_o, grad_o, mixing, low_weights, table = refs
    step = pl.program_id(0)
    me, length = ints[0], ints[1]
    vocab = embed.shape[0]
    height = heads * vocab

    @pl.when(step == 0)
    def _():
        for r in range(parts):
            mixing[me ^ r] = payloads[r][...]
        down = jnp.zeros((vocab, D), f32)
        for g in range(parts):
            one = mixing[g, height:].astype(f32)
            down = down + (one[:vocab] + one[vocab:])
        table[...] = stack_parts(embed[...] + (down + vec[2:3]))
        sums_o[...] = jnp.zeros_like(sums_o)

    for r in range(parts):
        low_weights[me ^ r] = weights[r][...]
    token = token_col[...]
    hot = jnp.where(lanes((ROWS, WIDE)) % vocab == token, 1.0, 0.0).astype(bf16)
    x = dot(hot, table[...])
    x = x + dot(
        jnp.concatenate([low_weights[g] for g in range(parts)], axis=1),
        jnp.concatenate([mixing[g, :height] for g in range(parts)], axis=0),
    )
    normed, scale = stats_of(x)
    gain = vec[3:4]
    final = (normed * gain + vec[4:5]).astype(bf16)
    head_low = head[:D].astype(bf16)
    logits = dot(final, head_low) + head[D : D + 1]
    shifted = logits - jnp.max(logits, axis=-1, keepdims=True)
    log_probs = shifted - jnp.log(jnp.sum(jnp.exp(shifted), axis=-1, keepdims=True))
    target = lanes((ROWS, vocab)) == target_col[...]
    position = step * ROWS + sublanes((ROWS, 1))
    slot_weight = jnp.where(position < length - 1, floats[0], 0.0)
    picked = jnp.sum(jnp.where(target, log_probs, 0.0), axis=-1, keepdims=True)
    loss = -jnp.sum(slot_weight * picked, keepdims=True)
    logit_grad = ((jnp.exp(log_probs) - jnp.where(target, 1.0, 0.0)) * slot_weight).astype(bf16)
    final_grad = dot(logit_grad, head_low, NT)
    grad = norm_back(final_grad, normed, scale, gain)
    high, rest = split2(grad)
    token_hot = jnp.where(sublanes((vocab, ROWS)) == token_row[...], 1.0, 0.0).astype(bf16)
    sums_o[0:vocab] += dot(token_hot, high) + dot(token_hot, rest)
    sums_o[vocab : 2 * vocab] += dot(logit_grad, final, TN)
    base = 2 * vocab
    sums_o[base : base + 1] += jnp.sum(final_grad * normed, axis=0, keepdims=True)
    sums_o[base + 1 : base + 2] += jnp.sum(final_grad, axis=0, keepdims=True)
    bias_grad = jnp.sum(logit_grad.astype(f32), axis=0, keepdims=True)
    sums_o[base + 2 : base + 3, :vocab] += bias_grad
    lane = lanes((1, WIDE))
    count = jnp.where((step == 0) & (length >= 2), 1.0, 0.0)
    sums_o[base + 3 : base + 4, :WIDE] += jnp.where(
        lane == 0, loss, jnp.where(lane == 1, count, 0.0)
    )
    sums_o[base + 16 : base + 16 + height] += dot(weights[0][...], high, TN)
    grad_o[...] = dot(high, payloads[0][:height], NT)


def loss_rows(ints, floats, token_col, target_col, token_row, embedding, head, vectors, weights, payloads, heads):
    seq = token_col.shape[0]
    vocab = embedding.shape[0]
    parts = len(weights)
    height = heads * vocab
    col = pl.BlockSpec((ROWS, 1), lambda i: (i, 0))
    o = jax.ShapeDtypeStruct
    full = lambda array: pl.BlockSpec(array.shape, lambda i: (0,) * array.ndim)
    sums_shape = (2 * vocab + 16 + height, D)
    return pl.pallas_call(
        functools.partial(loss_kernel, parts, heads),
        grid=(seq // ROWS,),
        in_specs=[SMEM, SMEM, col, col, pl.BlockSpec((1, ROWS), lambda i: (0, i))]
        + [full(embedding), full(head), full(vectors)]
        + [pl.BlockSpec((ROWS, height), lambda i: (i, 0))] * parts
        + [full(payloads[0])] * parts,
        out_specs=[
            pl.BlockSpec(sums_shape, lambda i: (0, 0)),
            pl.BlockSpec((ROWS, height), lambda i: (i, 0)),
        ],
        out_shape=[o(sums_shape, f32), o((seq, height), f32)],
        scratch_shapes=[
            pltpu.VMEM((parts,) + payloads[0].shape, bf16),
            pltpu.VMEM((parts, ROWS, height), bf16),
            pltpu.VMEM((4 * vocab, D), bf16),
        ],
        compiler_params=pltpu.CompilerParams(vmem_limit_bytes=56 * MEGA),
        name="loss_rows",
    )(ints, floats, token_col, target_col, token_row, embedding, head, vectors, *weights, *payloads)


def padded(block):
    lacking = HB - block.shape[0]
    if lacking:
        block = jnp.concatenate([block, jnp.zeros((lacking, block.shape[1]), block.dtype)], axis=0)
    return block


def factors_kernel(
    heads,
    sums,
    table,
    mat_q,
    mat_o,
    mat_u,
    mat_f,
    upper,
    normed,
    act,
    values,
    left_o,
    right_o,
    hidden_o,
    bias_o,
):
    vocab = normed.shape[0]
    width = mat_u.shape[1]
    rows = sums[0:vocab]
    mixed = sums[2 * vocab + 16 :]
    act_grad = rows_times_low(rows, mat_f[...], NT)
    u = upper[...]
    tanh = jnp.tanh(GELU_A * (u + GELU_B * (u * u * u)))
    slope = 0.5 * (1.0 + tanh) + 0.5 * u * (1.0 - tanh * tanh) * (
        GELU_A * (1.0 + 3.0 * GELU_B * (u * u))
    )
    upper_grad = act_grad * slope
    bias_grad = jnp.sum(upper_grad, axis=0, keepdims=True)
    bias_o[...] = bias_grad
    value_grad = rows_times_low(mixed, mat_o[...], NT)
    shape = value_grad.shape
    value_grad = jnp.where(sublanes(shape) // vocab == lanes(shape) // HD, value_grad, 0.0)
    value_table = value_grad[:vocab]
    for h in range(1, heads):
        value_table = value_table + value_grad[h * vocab : (h + 1) * vocab]
    proj_grad = jnp.concatenate([table[...], value_table], axis=1)
    hidden = rows_times_low(upper_grad, mat_u[...], NT) + rows_times_low(proj_grad, mat_q[...], NT)
    hidden_o[0:vocab] = hidden
    low = normed[...].astype(f32)
    own = act[...].astype(f32)
    val = values[...].astype(f32)
    normed_gram = dot6(low, low, NT)
    square = (
        jnp.sum(normed_gram * dot6(proj_grad, proj_grad, NT), keepdims=True)
        + jnp.sum(normed_gram * dot6(upper_grad, upper_grad, NT), keepdims=True)
        + jnp.sum(dot6(own, own, NT) * dot6(rows, rows, NT), keepdims=True)
        + jnp.sum(dot6(val, val, NT) * dot6(mixed, mixed, NT), keepdims=True)
        + jnp.sum(bias_grad * bias_grad, keepdims=True)
    )
    hidden_o[vocab : vocab + 8] = jnp.broadcast_to(square, (8, D))

    def put_left(index, block):
        block = padded(block)
        left_o[index] = jnp.concatenate([block] * 3, axis=0).astype(bf16)

    def put_right(index, block):
        left_o_parts = split3(padded(block))
        right_o[index] = jnp.concatenate(left_o_parts, axis=0)

    at = 0
    for i in range(D // BS):
        put_left(at, low[:, i * BS : (i + 1) * BS])
        at += 1
    for i in range(width // BS):
        put_left(at, own[:, i * BS : (i + 1) * BS])
        at += 1
    pair = 2 * vocab
    for i in range(heads // 2):
        put_left(at, val[i * pair : (i + 1) * pair, i * BS : (i + 1) * BS])
        at += 1
    at = 0
    for k in range(3 * heads * HD // BS):
        put_right(at, proj_grad[:, k * BS : (k + 1) * BS])
        at += 1
    for i in range(heads // 2):
        for k in range(D // BS):
            put_right(at, mixed[i * pair : (i + 1) * pair, k * BS : (k + 1) * BS])
            at += 1
    for k in range(width // BS):
        put_right(at, upper_grad[:, k * BS : (k + 1) * BS])
        at += 1
    for k in range(D // BS):
        put_right(at, rows[:, k * BS : (k + 1) * BS])
        at += 1


def factor_places(heads, ff_local):
    q_cols = 3 * heads * HD // BS
    o_rows = heads // 2
    across = D // BS
    f_rows = ff_local // BS
    left, right = [], []
    for which, i, k in tile_places(layer_shapes(heads, ff_local)):
        if which == 0:
            left.append(i)
            right.append(k)
        elif which == 1:
            left.append(across + f_rows + i)
            right.append(q_cols + i * across + k)
        elif which == 2:
            left.append(i)
            right.append(q_cols + o_rows * across + k)
        else:
            left.append(across + i)
            right.append(q_cols + o_rows * across + f_rows + k)
    return np.array(left, np.int32), np.array(right, np.int32)


def factors(sums, table, mats, upper, normed, act, values, heads):
    vocab = normed.shape[0]
    ff_local = upper.shape[1]
    n_left = D // BS + ff_local // BS + heads // 2
    n_right = 3 * heads * HD // BS + heads // 2 * (D // BS) + ff_local // BS + D // BS
    o = jax.ShapeDtypeStruct
    return pl.pallas_call(
        functools.partial(factors_kernel, heads),
        in_specs=[VMEM] * 10,
        out_specs=[VMEM] * 4,
        out_shape=[
            o((n_left, 3 * HB, BS), bf16),
            o((n_right, 3 * HB, BS), bf16),
            o((vocab + 8, D), f32),
            o((1, ff_local), f32),
        ],
        compiler_params=pltpu.CompilerParams(vmem_limit_bytes=56 * MEGA),
        name="factors",
    )(sums, table, *mats, upper, normed, act, values)


def small_kernel(parts, corrections, sums, *refs):
    hiddens, refs = refs[:parts], refs[parts:]
    bias_grad, refs = refs[0], refs[1:]
    weights, refs = refs[:12], refs[12:]
    outs, scalars = refs[:12], refs[12]
    vocab = weights[0].shape[0]
    base = 2 * vocab
    total = [ref[...] for ref in hiddens]
    total = tree_sum(total)
    hidden = total[:vocab]
    square = total[vocab : vocab + 1, 0:1]
    rows = sums[0:vocab]
    normed, scale = stats_of(weights[0][...])
    gain = weights[6][0:1]
    embed_grad = rows + norm_back(hidden, normed, scale, gain)
    vector_grad = jnp.concatenate(
        [
            jnp.sum(hidden * normed, axis=0, keepdims=True),
            jnp.sum(hidden, axis=0, keepdims=True),
            jnp.sum(rows, axis=0, keepdims=True),
            sums[base : base + 1],
            sums[base + 1 : base + 2],
        ],
        axis=0,
    )
    head_grad = sums[vocab : 2 * vocab]
    head_bias = sums[base + 2 : base + 3, :vocab]
    add = lambda value: jnp.sum(value * value, keepdims=True)
    square = square + add(embed_grad) + add(vector_grad) + add(head_grad) + add(head_bias)
    count = sums[base + 3 : base + 4, 1:2]
    loss = sums[base + 3 : base + 4, 0:1] / count
    norm = jnp.sqrt(square) / count
    scale_all = jnp.minimum(1.0, CLIP_NORM / norm) / count
    one, two = corrections[0], corrections[1]

    def update(index, pick, grad):
        weight, first, second = (weights[3 * index + k][pick] for k in range(3))
        grad = grad * scale_all
        first = BETA_ONE * first + (1.0 - BETA_ONE) * grad
        second = BETA_TWO * second + (1.0 - BETA_TWO) * grad * grad
        step = first / one / (jnp.sqrt(second / two) + ADAM_EPS)
        outs[3 * index][pick] = weight - RATE_SMALL * (step + WEIGHT_DECAY * weight)
        outs[3 * index + 1][pick] = first
        outs[3 * index + 2][pick] = second

    everything = slice(None)
    update(0, everything, embed_grad)
    update(1, slice(0, D), head_grad.T)
    update(1, slice(D, D + 1), head_bias)
    update(2, everything, vector_grad)
    update(3, everything, bias_grad[...])
    lane = lanes((1, WIDE))
    scalars[...] = jnp.where(
        lane == 0, scale_all, jnp.where(lane == 1, loss, jnp.where(lane == 2, norm, 0.0))
    )


def small(corrections, sums, hiddens, bias_grad, weights):
    o = jax.ShapeDtypeStruct
    return pl.pallas_call(
        functools.partial(small_kernel, len(hiddens)),
        in_specs=[SMEM] + [VMEM] * (1 + len(hiddens) + 1 + 12),
        out_specs=[VMEM] * 13,
        out_shape=[o(weight.shape, f32) for weight in weights] + [o((1, WIDE), f32)],
        compiler_params=pltpu.CompilerParams(vmem_limit_bytes=56 * MEGA),
        name="small",
    )(corrections, sums, *hiddens, bias_grad, *weights)


GROUP = 0
UN = 3


def eliminate(work, count):
    lane=lax.broadcasted_iota(jnp.int32,(HB,BS),1)
    sub=lax.broadcasted_iota(jnp.int32,(HB,BS),0)
    half=jnp.where(lane>=HB,HB,0)
    for g0 in range(HB//8):
        r0=8*g0
        rows=HB-r0
        def body(jj,carry):
            j=r0+jj
            pick=half[:rows]+j
            at_pivot=lane[:rows]==pick
            below=sub[:rows]>jj
            clear=at_pivot&below
            group=GROUP or count
            for t0 in range(0,count,group):
                span=range(t0,t0+group)
                rows_in=[work[t,pl.ds(j,1),:] for t in span]
                kept=[work[t,r0:,:] for t in span]
                wides=[jnp.broadcast_to(row,(8,BS)) for row in rows_in]
                pivots=[jnp.take_along_axis(w,pick[:8],axis=1,mode="promise_in_bounds") for w in wides]
                cs=[jnp.take_along_axis(a,pick,axis=1,mode="promise_in_bounds") for a in kept]
                scaleds=[jnp.where(at_pivot[:8],1.0,w)/p for w,p in zip(wides,pivots)]
                for t,a,c,sc in zip(span,kept,cs,scaleds):
                    work[t,r0:,:]=jnp.where(clear,0.0,a)-jnp.where(below,c,0.0)*sc[:1]
            return carry
        lax.fori_loop(0,8,body,0)

def factor_inverse(packed):
    lane=lax.broadcasted_iota(jnp.int32,(HB,BS),1)
    sub=lax.broadcasted_iota(jnp.int32,(HB,BS),0)
    left=lane<HB
    col=jnp.where(left,lane,lane-HB)
    diag=jnp.where(col==sub,packed,0.0)
    d_left=jnp.sum(jnp.where(left,diag,0.0),axis=1,keepdims=True)
    d_right=jnp.sum(jnp.where(left,0.0,diag),axis=1,keepdims=True)
    scale=lax.rsqrt(jnp.where(left,d_left,d_right))
    unit=jnp.where(col<sub,packed,jnp.where(col==sub,1.0,0.0))
    return unit*scale

def block_diagonal(packed):
    lane=lax.broadcasted_iota(jnp.int32,(HB,BS),1)
    left=lane<HB
    return jnp.concatenate([jnp.where(left,packed,0.0),jnp.where(left,0.0,packed)],axis=0)

def swap(x):
    return pltpu.roll(x,HB,1)

def soap_kernel(count, per, scal, left_at, right_at, lefts, rights, W, m, v, L, R, QL, QR, W_o, low_o, m_o, v_o, L_o, R_o, QL_o, QR_o, ML_s, MR_s, work, A21_s, A22_s, W11_s):
    step=pl.program_id(0)
    scale=scal[0]; c1=scal[1]; c2=scal[2]
    left=lax.broadcasted_iota(jnp.int32,(HB,BS),1)<HB
    span=range(per)
    pairs=[(lefts[left_at[step*per+s]],rights[right_at[step*per+s]]) for s in span]
    g=[dot(a,b,TN)*scale for a,b in pairs]
    gT=[dot(b,a,TN)*scale for a,b in pairs]
    qT=[QL[s].T for s in span]
    ggl=[dot3(x,x,NT) for x in g]
    ggr=[dot3(x,x,NT) for x in gT]
    rot=[dot3(q,x,NN) for q,x in zip(qT,g)]
    Ln=[BETA_TWO*L[s]+(1-BETA_TWO)*ggl[s] for s in span]
    Rn=[BETA_TWO*R[s]+(1-BETA_TWO)*ggr[s] for s in span]
    rot=[dot3(x,QR[s],NN) for s,x in enumerate(rot)]
    for s in span:
        L_o[s]=Ln[s]; R_o[s]=Rn[s]
    ML=[dot6(Ln[s],QL[s],NN) for s in span]
    MR=[dot6(Rn[s],QR[s],NN) for s in span]
    xs=[]
    for s in span:
        mn=BETA_ONE*m[s]+(1-BETA_ONE)*rot[s]
        vn=BETA_TWO*v[s]+(1-BETA_TWO)*rot[s]*rot[s]
        m_o[s]=mn; v_o[s]=vn
        xs.append((mn/c1)/(jnp.sqrt(vn/c2)+ADAM_EPS))
    back=[dot3(QL[s],xs[s],NN) for s in span]
    ML=[x*lax.rsqrt(jnp.sum(x*x,keepdims=True)) for x in ML]
    MR=[x*lax.rsqrt(jnp.sum(x*x,keepdims=True)) for x in MR]
    back=[dot3(back[s],QR[s],NT) for s in span]
    AL=[dot6(x,x,TN) for x in ML]
    AR=[dot6(x,x,TN) for x in MR]
    for s in span:
        w=W[s]
        wn=w-RATE_TILES*(back[s]+WEIGHT_DECAY*w)
        W_o[s]=wn
        low_o[s]=wn.astype(bf16)
        t=step*per+s
        ML_s[t]=ML[s]; MR_s[t]=MR[s]
        work[t]=jnp.where(left,AL[s][:HB],swap(AR[s][:HB]))
        A21_s[t]=jnp.where(left,AL[s][HB:],swap(AR[s][HB:]))
        A22_s[t]=jnp.where(left,swap(AL[s][HB:]),AR[s][HB:])

    @pl.when(step==pl.num_programs(0)-1)
    def _():
        eliminate(work,count)
        def mid(i,carry):
            ts=[i*UN+k for k in range(UN)]
            w11=[factor_inverse(work[t]) for t in ts]
            for t,w in zip(ts,w11): W11_s[t]=w
            l21=[dot6(A21_s[t],block_diagonal(w),NT) for t,w in zip(ts,w11)]
            for t,l in zip(ts,l21): A21_s[t]=l
            low=[dot6(l,block_diagonal(l),NT) for l in l21]
            for t,l in zip(ts,low): work[t]=A22_s[t]-l
            return carry
        lax.fori_loop(0,count//UN,mid,0)
        eliminate(work,count)
        def last(i,carry):
            ts=[i*UN+k for k in range(UN)]
            w22=[factor_inverse(work[t]) for t in ts]
            w11=[W11_s[t] for t in ts]
            y=[dot6(A21_s[t],block_diagonal(w),NN) for t,w in zip(ts,w11)]
            w21=[-dot6(w,block_diagonal(x),NN) for w,x in zip(w22,y)]
            cl=[jnp.concatenate([jnp.where(left,a,0.0),jnp.where(left,b,swap(c))],axis=0) for a,b,c in zip(w11,w21,w22)]
            cr=[jnp.concatenate([jnp.where(left,swap(a),0.0),jnp.where(left,swap(b),c)],axis=0) for a,b,c in zip(w11,w21,w22)]
            ol=[dot3(ML_s[t],c,NT) for t,c in zip(ts,cl)]
            orr=[dot3(MR_s[t],c,NT) for t,c in zip(ts,cr)]
            for t,a,b in zip(ts,ol,orr):
                QL_o[t]=a; QR_o[t]=b
            return carry
        lax.fori_loop(0,count//UN,last,0)

def soap(scal,left_at,right_at,lefts,rights,W,m,v,L,R,QL,QR):
    count=W.shape[0]
    per=3 if count%3==0 else 1
    blk=pl.BlockSpec((per,BS,BS),lambda i:(i,0,0))
    full=pl.BlockSpec((count,BS,BS),lambda i:(0,0,0))
    whole=lambda x:pl.BlockSpec(x.shape,lambda i:(0,0,0))
    o=lambda dt: jax.ShapeDtypeStruct((count,BS,BS),dt)
    return pl.pallas_call(
        functools.partial(soap_kernel,count,per),
        grid=(count//per,),
        in_specs=[SMEM]*3+[whole(lefts),whole(rights)]+[blk]*7,
        out_specs=[blk]*6+[full]*2,
        out_shape=[o(f32),o(bf16),o(f32),o(f32),o(f32),o(f32),o(f32),o(f32)],
        scratch_shapes=[pltpu.VMEM((count,BS,BS),f32)]*2+[pltpu.VMEM((count,HB,BS),f32)]*4,
        compiler_params=pltpu.CompilerParams(vmem_limit_bytes=56*1024*1024),
        name="soap_tiles",
    )(scal,left_at,right_at,lefts,rights,W,m,v,L,R,QL,QR)


def local(
    tokens,
    lengths,
    tile_owner,
    step_count,
    weight_tiles,
    tiles_first,
    tiles_second,
    stats_left,
    stats_right,
    basis_left,
    basis_right,
    embedding,
    embedding_first,
    embedding_second,
    head_table,
    head_first,
    head_second,
    vectors,
    vectors_first,
    vectors_second,
    fc_bias,
    fc_bias_first,
    fc_bias_second,
):
    seq = tokens.shape[1]
    mp_count = lax.axis_size("mp")
    dp_count = lax.axis_size("dp")
    dp_index = lax.axis_index("dp")
    mp_index = lax.axis_index("mp")
    heads = H // mp_count
    ff_local = fc_bias.shape[1]
    count = weight_tiles.shape[0]
    half = count // 2

    halves = gather_tiles(weight_tiles.astype(bf16))
    pieces = halves[0] + halves[1]
    holder = tile_owner // count
    inside = tile_owner - holder * count
    place = (
        jnp.where(inside >= half, dp_count * half - half, 0) + (holder ^ dp_index) * half + inside
    )
    result = tables(place, pieces, embedding, vectors, fc_bias, heads, ff_local)
    mats, (proj, upper, payload, normed, act, values) = result[:4], result[4:]

    token_col = tokens.reshape(seq, 1)
    target_col = jnp.roll(tokens, -1, axis=1).reshape(seq, 1)
    cosine, sine, cosine_t, sine_t = rotary_tables(seq)
    payloads = gather_xor(payload, "mp")
    query, key, weight = attention(lengths, token_col, proj, cosine, sine, heads)
    weights = gather_xor(weight.astype(bf16), "mp")
    length = lengths[0]
    inverse_length = 1.0 / jnp.maximum(length - 1, 1).astype(f32)
    sums, weight_grad = loss_rows(
        jnp.stack([mp_index, length]),
        inverse_length[None],
        token_col,
        target_col,
        tokens,
        embedding,
        head_table,
        vectors,
        weights,
        payloads,
        heads,
    )
    sums = sum_dp(sums)
    table = attention_back(
        token_col, tokens, query, key, weight, weight_grad, cosine, sine, cosine_t, sine_t, heads
    )
    table = sum_dp(table)
    left, right, hidden, bias_grad = factors(
        sums, table, mats, upper, normed, act, values, heads
    )
    hiddens = gather_xor(hidden, "mp")
    corrections = 1.0 - jnp.power(
        jnp.array([BETA_ONE, BETA_TWO], f32), step_count.astype(f32)
    )
    small_weights = (
        embedding,
        embedding_first,
        embedding_second,
        head_table,
        head_first,
        head_second,
        vectors,
        vectors_first,
        vectors_second,
        fc_bias,
        fc_bias_first,
        fc_bias_second,
    )
    *small_out, scalars = small(corrections, sums, hiddens, bias_grad, small_weights)
    slots = dp_index * count + jnp.arange(count, dtype=jnp.int32)
    natural = jnp.sum(
        jnp.where(
            tile_owner[None, :] == slots[:, None],
            jnp.arange(tile_owner.shape[0], dtype=jnp.int32)[None, :],
            0,
        ),
        axis=1,
    )
    left_of, right_of = factor_places(heads, ff_local)
    same = natural[:, None] == jnp.arange(tile_owner.shape[0], dtype=jnp.int32)[None, :]
    left_at = jnp.sum(jnp.where(same, left_of[None, :], 0), axis=1)
    right_at = jnp.sum(jnp.where(same, right_of[None, :], 0), axis=1)
    results = soap(
        jnp.concatenate([scalars[0, :1], corrections]),
        left_at,
        right_at,
        left,
        right,
        weight_tiles,
        tiles_first,
        tiles_second,
        stats_left,
        stats_right,
        basis_left,
        basis_right,
    )
    return (scalars[0, 1], scalars[0, 2], *results, *small_out)


def solution(mesh):
    tiled = P("dp", None, "mp")
    split = P(None, "mp")
    in_specs = (P("dp", None), P("dp"), P(), P(), *[tiled] * 7, *[P()] * 9, *[split] * 3)
    out_specs = (P(), P(), *[tiled] * 8, *[P()] * 9, *[split] * 3)
    return jax.shard_map(local, mesh=mesh, in_specs=in_specs, out_specs=out_specs, check_vma=False)
```

time: 808 us -> 272 us (0.34)
  waiting for transfers between devices: 429 us -> 76.3 us
  matrix products: 90 us -> 0 us
  blocking collectives: 65.4 us -> 0 us
  starting transfers between devices: 1.07 us -> 50.3 us
  other arithmetic: 58.5 us -> 12 us
  Pallas kernels: 73.1 us -> 115 us
  local copies, waits for them, and re-layouts: 51.1 us -> 14.5 us
  between operations: 25 us -> 2.62 us
    psum x3 -> x0, waiting for transfers between devices: 296 us -> none  [the longest x1 153 us: mixed_rows(): return lax.psum(branch_part, 'mp')]
    reduce_scatter x1 -> x0, waiting for transfers between devices: 90.2 us -> none  [local(): lax.psum_scatter(tile_parts[0], 'dp', scatter_dimension=0, tiled=True)]
    dot_general x31 -> x0, matrix products: 90 us -> none  [the longest x2 9.09 us: one_block(): jnp.einsum('qhe,khe->hqk', grad_block, value_seq, preferred_element_type=...]
    ppermute x0 -> x33, waiting for transfers between devices: none -> 76.3 us  [swap_with(): return lax.ppermute(value, axis, [(i, i ^ mask) for i in range(count)])]
    psum x2 -> x0, blocking collectives: 65.4 us -> none  [the longest x1 39.4 us: local(): grad_norm = jnp.sqrt(lax.psum(square_part, ('dp', 'mp')))]
    ppermute x0 -> x33, starting transfers between devices: none -> 50.3 us  [swap_with(): return lax.ppermute(value, axis, [(i, i ^ mask) for i in range(count)])]
    all_gather x1 -> x0, waiting for transfers between devices: 42.2 us -> none  [local(): lax.all_gather(weight_tiles.astype(jnp.bfloat16), 'dp', axis=0, tiled=True)]
    pallas_call x2 -> x6, Pallas kernels: 17.2 us -> 57.7 us  [the longest x1 14.1 us: loss_rows(): pl.pallas_call(functools.partial(loss_kernel, parts, heads), grid=(seq //...]
  transfers between devices with their start and end apart: 5 -> 33, of which waited for: 5 -> 14; matrix products, arithmetic and copies ran while one was open for 4% -> 4% of each run, Pallas kernels for 1% -> 4%
where the time goes in v2:
time: 272 us; the launch traced here: 271 us
  Pallas kernels  115 us (42%)
  waiting for transfers between devices  76.3 us (28%)
  starting transfers between devices  50.3 us (18%)
  local copies, waits for them, and re-layouts  14.5 us (5%)
  other arithmetic  12 us (4%)
    ppermute x33, waiting for transfers between devices, swap_with(): return lax.ppermute(value, axis, [(i, i ^ mask) for i in range(count)])  76.3 us
    pallas_call x1, Pallas kernels, soap(): pl.pallas_call(functools.partial(soap_kernel, count, per), grid=(count //...  57.8 us
    ppermute x33, starting transfers between devices, swap_with(): return lax.ppermute(value, axis, [(i, i ^ mask) for i in range(count)])  50.3 us
    pallas_call x1, Pallas kernels, loss_rows(): pl.pallas_call(functools.partial(loss_kernel, parts, heads), grid=(seq //...  14.1 us
    pallas_call x1, Pallas kernels, attention_back(): pl.pallas_call(functools.partial(attention_back_kernel, heads), in_specs=...  11.5 us
    pallas_call x1, Pallas kernels, attention(): pl.pallas_call(functools.partial(attention_kernel, heads), in_specs=[SMEM...  11 us
    unnamed x68, local copies, waits for them, and re-layouts  10.4 us
    pallas_call x1, Pallas kernels, tables(): pl.pallas_call(functools.partial(tables_kernel, tile_places(shapes), head...  8.42 us
  transfers between devices with their start and end apart: 33, of which 14 were waited for; matrix products, arithmetic and copies ran while one was open for 4% of the time, Pallas kernels for 4%

profile of v2, /device:TPU:0, one launch (start us, length us, event | category | flops | bytes accessed | tf_op | source)
XLA Modules:
  0.0 271.2 jit_solution(4208110808462998414)
XLA Ops:
  0.7 1.6 convert_element_type.15
  2.3 3.0 %collective-permute-start.10 = (bf16[12,128,128]{2,1,0:T(8,128)(2,1)S(1)}, bf16[12,128,128]{2,1,0:T(8,128)(2,1)S(1)}, u32[]{:S(2)}, u32[]{:S(2)}) collective-permute-start(bf16[12,128,128]{2,1,0:T(8,128)(2,1)S(1)} %get-tuple-element.172.refs_8_), channel_id=1, source_target_pairs={{0,16},{4,20},{8,24},{12,28},{16,0},{20,4},{24,8},{28,12},{1,17},{... | collective-permute-start | bytes 1179656 | tf_op jit(solution)/shard_map/ppermute | solution.py:112
  5.4 1.5 collective-permute-start.8
  7.5 7.8 %collective-permute-done.10.refs_12_ = bf16[12,128,128]{2,1,0:T(8,128)(2,1)S(1)} collective-permute-done((bf16[12,128,128]{2,1,0:T(8,128)(2,1)S(1)}, bf16[12,128,128]{2,1,0:T(8,128)(2,1)S(1)}, u32[]{:S(2)}, u32[]{:S(2)}) %collective-permute-start.10) | collective-permute-done | bytes 393248 | tf_op jit(solution)/shard_map/ppermute | solution.py:112
  15.3 2.1 collective-permute-done.8.refs_10_
  17.9 5.8 %collective-permute-done.3.refs_4_ = bf16[12,128,128]{2,1,0:T(8,128)(2,1)S(1)} collective-permute-done((bf16[12,128,128]{2,1,0:T(8,128)(2,1)S(1)}, bf16[12,128,128]{2,1,0:T(8,128)(2,1)S(1)}, u32[]{:S(2)}, u32[]{:S(2)}) %collective-permute-start.3) | collective-permute-done | bytes 393248 | tf_op jit(solution)/shard_map/ppermute | solution.py:112
  23.7 2.0 collective-permute-start.5
  26.4 5.1 %collective-permute-done.12.refs_14_ = bf16[12,128,128]{2,1,0:T(8,128)(2,1)} collective-permute-done((bf16[12,128,128]{2,1,0:T(8,128)(2,1)S(1)}, bf16[12,128,128]{2,1,0:T(8,128)(2,1)}, u32[]{:S(2)}, u32[]{:S(2)}) %collective-permute-start.12) | collective-permute-done | bytes 393248 | tf_op jit(solution)/shard_map/ppermute | solution.py:112
  31.4 1.9 collective-permute-done.5.refs_6_
  34.0 1.0 copy.71.token_col
  35.7 8.4 %tables.1 = (bf16[1024,768]{1,0:T(8,128)(2,1)}, bf16[256,1024]{1,0:T(8,128)(2,1)}, bf16[1024,1024]{1,0:T(8,128)(2,1)}, bf16[1024,1024]{1,0:T(8,128)(2,1)}, f32[3...) custom-call(s32[192]{0:T(256)} %fusion.1.place, ...), custom_call_target="tpu_custom_call" | custom-call | tf_op jit(solution)/shard_map/tables/pallas_call | solution.py:208
  44.2 11.0 %attention.1 = (bf16[4,1024,128]{2,1,0:T(8,128)(2,1)}, bf16[4,1024,128]{2,1,0:T(8,128)(2,1)}, f32[1024,128]{1,0:T(8,128)}) custom-call(s32[1]{0:T(128)S(6)} %copy.81.length, s32[1024,1]{1,0:T(8,128)} %copy.71.token_col, f32[32,768]{1,0:T(8,128)} %get-tuple-element.62.proj, f32[1024,128]{1,0:T(8,128)} %constant.51.clone.cosine, f32[1024,128]{1,0:T(8,128)} %constant.52.clone.sine), custom_call_target="tpu_custom_call" | custom-call | tf_op jit(solution)/shard_map/attention/pallas_call | solution.py:344
  55.2 1.1 convert_element_type.16.refs_0_
  56.3 3.6 %collective-permute-start.16 = (bf16[1024,128]{1,0:T(8,128)(2,1)S(1)}, bf16[1024,128]{1,0:T(8,128)(2,1)S(1)}, u32[]{:S(2)}, u32[]{:S(2)}) collective-permute-start(bf16[1024,128]{1,0:T(8,128)(2,1)S(1)} %convert_element_type.16.refs_0_), channel_id=1, source_target_pairs={{0,3},{1,2},{2,1},{3,0},{4,7},{5,6},{6,5},{7,4},{8,11},{9,10},{10,... | collective-permute-start | bytes 786440 | tf_op jit(solution)/shard_map/ppermute | solution.py:112
  60.9 3.4 %collective-permute-start.17 = (bf16[192,1024]{1,0:T(8,128)(2,1)S(1)}, bf16[192,1024]{1,0:T(8,128)(2,1)S(1)}, u32[]{:S(2)}, u32[]{:S(2)}) collective-permute-start(bf16[192,1024]{1,0:T(8,128)(2,1)S(1)} %copy-done.9), channel_id=1, source_target_pairs={{0,1},{1,0},{2,3},{3,2},{4,5},{5,4},{6,7},{7,6},{8,9},{9,8},{10,11... | collective-permute-start | bytes 1179656 | tf_op jit(solution)/shard_map/ppermute | solution.py:112
  64.2 3.2 %collective-permute-done.16.refs_3_ = bf16[1024,128]{1,0:T(8,128)(2,1)S(1)} collective-permute-done((bf16[1024,128]{1,0:T(8,128)(2,1)S(1)}, bf16[1024,128]{1,0:T(8,128)(2,1)S(1)}, u32[]{:S(2)}, u32[]{:S(2)}) %collective-permute-start.16) | collective-permute-done | bytes 262176 | tf_op jit(solution)/shard_map/ppermute | solution.py:112
  67.4 21.9 %collective-permute-start.14 = (bf16[1024,128]{1,0:T(8,128)(2,1)S(1)}, bf16[1024,128]{1,0:T(8,128)(2,1)S(1)}, u32[]{:S(2)}, u32[]{:S(2)}) collective-permute-start(bf16[1024,128]{1,0:T(8,128)(2,1)S(1)} %convert_element_type.16.refs_0_), channel_id=1, source_target_pairs={{0,1},{1,0},{2,3},{3,2},{4,5},{5,4},{6,7},{7,6},{8,9},{9,8},{10,11... | collective-permute-start | bytes 786440 | tf_op jit(solution)/shard_map/ppermute | solution.py:112
  90.0 0.7 add_bitcast_fusion
  90.7 1.0 copy.72.target_col
  91.7 1.2 copy.73.head.refs_8_
  93.5 23.0 %collective-permute-done.15.refs_2_ = bf16[1024,128]{1,0:T(8,128)(2,1)S(1)} collective-permute-done((bf16[1024,128]{1,0:T(8,128)(2,1)S(1)}, bf16[1024,128]{1,0:T(8,128)(2,1)S(1)}, u32[]{:S(2)}, u32[]{:S(2)}) %collective-permute-start.15) | collective-permute-done | bytes 262176 | tf_op jit(solution)/shard_map/ppermute | solution.py:112
  117.6 0.8 copy-done.15
  118.4 14.1 %loss_rows.1 = (f32[208,1024]{1,0:T(8,128)}, f32[1024,128]{1,0:T(8,128)}) custom-call(s32[2]{0:T(128)} %pad_add_fusion.ints, f32[1]{0:T(128)S(6)} %div.10.floats, s32[1024,1]{1,0:T(8,128)} %copy.71.token_col, s32[1024,1]{1,0:T(8,128)} %copy.72.target_col, s32[1,1024]{1,0:T(1,128)} %token_row.3, f32[32,1024]{1,0:T(8,128)} %refs_5_.1, ...), custom_call_target="tpu_custom_call" | custom-call | tf_op jit(solution)/shard_map/loss_rows/pallas_call | solution.py:554
  132.5 1.2 slice_select_fusion
  133.8 11.5 %attention_back.1 = f32[32,512]{1,0:T(8,128)} custom-call(s32[1024,1]{1,0:T(8,128)} %copy.71.token_col, s32[1,1024]{1,0:T(1,128)} %token_row.3, bf16[4,1024,128]{2,1,0:T(8,128)(2,1)} %get-tuple-element.66.query, bf16[4,1024,128]{2,1,0:T(8,128)(2,1)} %get-tuple-element.67.key, f32[1024,128]{1,0:T(8,128)} %get-tuple-element.63.weight, ...), custom_call_target="tpu_custom_call" | custom-call | tf_op jit(solution)/shard_map/attention_back/pallas_call | solution.py:455
  145.2 0.8 slice_select_fusion.1
  147.4 0.8 select_add_fusion.1
  148.2 2.5 collective-permute-start.28
  151.8 2.5 collective-permute-start.23
  156.1 9.5 %collective-permute-done.23 = f32[104,1024]{1,0:T(8,128)S(1)} collective-permute-done((f32[104,1024]{1,0:T(8,128)S(1)}, f32[104,1024]{1,0:T(8,128)S(1)}, u32[]{:S(2)}, u32[]{:S(2)}) %collective-permute-start.23) | collective-permute-done | bytes 426016 | tf_op jit(solution)/shard_map/ppermute | solution.py:112
  165.6 7.7 %collective-permute-done.22 = f32[104,1024]{1,0:T(8,128)S(1)} collective-permute-done((f32[104,1024]{1,0:T(8,128)S(1)}, f32[104,1024]{1,0:T(8,128)S(1)}, u32[]{:S(2)}, u32[]{:S(2)}) %collective-permute-start.22) | collective-permute-done | bytes 426016 | tf_op jit(solution)/shard_map/ppermute | solution.py:112
  174.3 1.1 collective-permute-done.24
  175.4 1.0 pad_maximum_fusion.sums
  176.4 8.0 %factors.1 = (bf16[18,192,128]{2,1,0:T(8,128)(2,1)}, bf16[38,192,128]{2,1,0:T(8,128)(2,1)}, f32[40,1024]{1,0:T(8,128)}, f32[1,1024]{1,0:T(1,128)}) custom-call(f32[208,1024]{1,0:T(8,128)} %pad_maximum_fusion.sums, f32[32,512]{1,0:T(8,128)} %pad_maximum_fusion.1.table, bf16[1024,768]{1,0:T(8,128)(2,1)} %get-tuple-element.69.mat_q, ...), custom_call_target="tpu_custom_call" | custom-call | tf_op jit(solution)/shard_map/factors/pallas_call | solution.py:698
  184.4 2.5 collective-permute-start.32
  186.9 1.9 collective-permute-start.30
  189.0 1.0 copy.76.refs_9_
  190.0 1.0 copy.77.refs_10_
  191.0 0.8 select_reduce_fusion
  191.8 1.9 collective-permute-done.32.refs_3_
  193.6 6.9 %collective-permute-done.31.refs_2_ = f32[40,1024]{1,0:T(8,128)S(1)} collective-permute-done((f32[40,1024]{1,0:T(8,128)}, f32[40,1024]{1,0:T(8,128)S(1)}, u32[]{:S(2)}, u32[]{:S(2)}) %collective-permute-start.31) | collective-permute-done | bytes 163872 | tf_op jit(solution)/shard_map/ppermute | solution.py:112
  201.2 4.7 %small.1 = (f32[32,1024]{1,0:T(8,128)}, f32[32,1024]{1,0:T(8,128)}, f32[32,1024]{1,0:T(8,128)}, f32[1025,32]{1,0:T(8,128)}, f32[1025,32]{1,0:T(8,128)}, /*index=...) custom-call(f32[2]{0:T(128)} %power_subtract_fusion.corrections, ...), custom_call_target="tpu_custom_call" | custom-call | tf_op jit(solution)/shard_map/small/pallas_call | solution.py:772
  205.9 1.4 fusion.3
  207.3 1.3 pad_maximum_fusion.2.scal
  208.6 1.9 copy.78
  210.5 1.9 copy.79
  212.4 0.9 copy.80
  213.3 57.8 %soap_tiles.1 = (f32[24,128,128]{2,1,0:T(8,128)}, bf16[24,128,128]{2,1,0:T(8,128)(2,1)}, f32[24,128,128]{2,1,0:T(8,128)}, f32[24,128,128]{2,1,0:T(8,128)}, f32[2...) custom-call(f32[3]{0:T(128)} %pad_maximum_fusion.2.scal, ...), custom_call_target="tpu_custom_call" | custom-call | tf_op jit(solution)/shard_map/soap_tiles/pallas_call | solution.py:911
  (119 shorter events, 11.1 us)
Async XLA Ops:
  0.7 33.3 %copy-start.25 = (s32[1,1024]{1,0:T(1,128)S(1)}, s32[1,1024]{1,0:T(1,128)}, u32[]{:S(2)}) copy-start(s32[1,1024]{1,0:T(1,128)} %token_row.3) | copy-start | bytes 12292
  2.2 32.8 %copy-start.26 = (s32[192]{0:T(256)S(1)}, s32[192]{0:T(256)}, u32[]{:S(2)}) copy-start(s32[192]{0:T(256)} %param.32) | copy-start | bytes 2308
  2.3 33.3 %copy-start.1 = (bf16[12,128,128]{2,1,0:T(8,128)(2,1)}, bf16[12,128,128]{2,1,0:T(8,128)(2,1)S(1)}, u32[]{:S(2)}) copy-start(bf16[12,128,128]{2,1,0:T(8,128)(2,1)S(1)} %get-tuple-element.172.refs_8_) | copy-start | bytes 1179652
  2.3 33.3 %copy-start.2 = (bf16[12,128,128]{2,1,0:T(8,128)(2,1)}, bf16[12,128,128]{2,1,0:T(8,128)(2,1)S(1)}, u32[]{:S(2)}) copy-start(bf16[12,128,128]{2,1,0:T(8,128)(2,1)S(1)} %get-tuple-element.173.refs_0_) | copy-start | bytes 1179652
  2.3 13.0 %collective-permute-start.10 = (bf16[12,128,128]{2,1,0:T(8,128)(2,1)S(1)}, bf16[12,128,128]{2,1,0:T(8,128)(2,1)S(1)}, u32[]{:S(2)}, u32[]{:S(2)}) collective-permute-start(bf16[12,128,128]{2,1,0:T(8,128)(2,1)S(1)} %get-tuple-element.172.refs_8_), channel_id=1, source_target_pairs={{0,16},{4,20},{8,24},{12,28},{16,0},{20,4},{24,8},{28,12},{1,17},{... | collective-permute-start | bytes 1179656 | tf_op jit(solution)/shard_map/ppermute | solution.py:112
  5.4 12.0 %collective-permute-start.8 = (bf16[12,128,128]{2,1,0:T(8,128)(2,1)S(1)}, bf16[12,128,128]{2,1,0:T(8,128)(2,1)S(1)}, u32[]{:S(2)}, u32[]{:S(2)}) collective-permute-start(bf16[12,128,128]{2,1,0:T(8,128)(2,1)S(1)} %get-tuple-element.172.refs_8_), channel_id=1, source_target_pairs={{0,8},{4,12},{8,0},{12,4},{16,24},{20,28},{24,16},{28,20},{1,9},{5... | collective-permute-start | bytes 1179656 | tf_op jit(solution)/shard_map/ppermute | solution.py:112
  6.9 10.6 %collective-permute-start.7 = (bf16[12,128,128]{2,1,0:T(8,128)(2,1)S(1)}, bf16[12,128,128]{2,1,0:T(8,128)(2,1)S(1)}, u32[]{:S(2)}, u32[]{:S(2)}) collective-permute-start(bf16[12,128,128]{2,1,0:T(8,128)(2,1)S(1)} %get-tuple-element.172.refs_8_), channel_id=1, source_target_pairs={{0,4},{4,0},{8,12},{12,8},{16,20},{20,16},{24,28},{28,24},{1,5},{5... | collective-permute-start | bytes 1179656 | tf_op jit(solution)/shard_map/ppermute | solution.py:112
  6.9 16.9 %collective-permute-start.3 = (bf16[12,128,128]{2,1,0:T(8,128)(2,1)S(1)}, bf16[12,128,128]{2,1,0:T(8,128)(2,1)S(1)}, u32[]{:S(2)}, u32[]{:S(2)}) collective-permute-start(bf16[12,128,128]{2,1,0:T(8,128)(2,1)S(1)} %get-tuple-element.173.refs_0_), channel_id=1, source_target_pairs={{0,16},{4,20},{8,24},{12,28},{16,0},{20,4},{24,8},{28,12},{1,17},{... | collective-permute-start | bytes 1179656 | tf_op jit(solution)/shard_map/ppermute | solution.py:112
  7.4 18.4 %collective-permute-start.1 = (bf16[12,128,128]{2,1,0:T(8,128)(2,1)S(1)}, bf16[12,128,128]{2,1,0:T(8,128)(2,1)S(1)}, u32[]{:S(2)}, u32[]{:S(2)}) collective-permute-start(bf16[12,128,128]{2,1,0:T(8,128)(2,1)S(1)} %get-tuple-element.173.refs_0_), channel_id=1, source_target_pairs={{0,8},{4,12},{8,0},{12,4},{16,24},{20,28},{24,16},{28,20},{1,9},{5... | collective-permute-start | bytes 1179656 | tf_op jit(solution)/shard_map/ppermute | solution.py:112
  15.3 20.3 %copy-start.5 = (bf16[12,128,128]{2,1,0:T(8,128)(2,1)}, bf16[12,128,128]{2,1,0:T(8,128)(2,1)S(1)}, u32[]{:S(2)}) copy-start(bf16[12,128,128]{2,1,0:T(8,128)(2,1)S(1)} %collective-permute-done.10.refs_12_) | copy-start | bytes 1179652
  15.3 10.5 %collective-permute-start = (bf16[12,128,128]{2,1,0:T(8,128)(2,1)S(1)}, bf16[12,128,128]{2,1,0:T(8,128)(2,1)S(1)}, u32[]{:S(2)}, u32[]{:S(2)}) collective-permute-start(bf16[12,128,128]{2,1,0:T(8,128)(2,1)S(1)} %get-tuple-element.173.refs_0_), channel_id=1, source_target_pairs={{0,4},{4,0},{8,12},{12,8},{16,20},{20,16},{24,28},{28,24},{1,5},{5... | collective-permute-start | bytes 1179656 | tf_op jit(solution)/shard_map/ppermute | solution.py:112
  17.4 18.2 %copy-start.6 = (bf16[12,128,128]{2,1,0:T(8,128)(2,1)}, bf16[12,128,128]{2,1,0:T(8,128)(2,1)S(1)}, u32[]{:S(2)}) copy-start(bf16[12,128,128]{2,1,0:T(8,128)(2,1)S(1)} %collective-permute-done.8.refs_10_) | copy-start | bytes 1179652
  17.4 8.9 %collective-permute-start.11 = (bf16[12,128,128]{2,1,0:T(8,128)(2,1)S(1)}, bf16[12,128,128]{2,1,0:T(8,128)(2,1)S(1)}, u32[]{:S(2)}, u32[]{:S(2)}) collective-permute-start(bf16[12,128,128]{2,1,0:T(8,128)(2,1)S(1)} %collective-permute-done.10.refs_12_), channel_id=1, source_target_pairs={{0,4},{4,0},{8,12},{12,8},{16,20},{20,16},{24,28},{28,24},{1,5},{5... | collective-permute-start | bytes 1179656 | tf_op jit(solution)/shard_map/ppermute | solution.py:112
  17.4 18.2 %copy-start.7 = (bf16[12,128,128]{2,1,0:T(8,128)(2,1)}, bf16[12,128,128]{2,1,0:T(8,128)(2,1)S(1)}, u32[]{:S(2)}) copy-start(bf16[12,128,128]{2,1,0:T(8,128)(2,1)S(1)} %collective-permute-done.7.refs_9_) | copy-start | bytes 1179652
  17.4 14.0 %collective-permute-start.12 = (bf16[12,128,128]{2,1,0:T(8,128)(2,1)S(1)}, bf16[12,128,128]{2,1,0:T(8,128)(2,1)}, u32[]{:S(2)}, u32[]{:S(2)}) collective-permute-start(bf16[12,128,128]{2,1,0:T(8,128)(2,1)S(1)} %collective-permute-done.8.refs_10_), channel_id=1, source_target_pairs={{0,16},{4,20},{8,24},{12,28},{16,0},{20,4},{24,8},{28,12},{1,17},{... | collective-permute-start | bytes 1179656 | tf_op jit(solution)/shard_map/ppermute | solution.py:112
  23.7 9.6 %collective-permute-start.5 = (bf16[12,128,128]{2,1,0:T(8,128)(2,1)S(1)}, bf16[12,128,128]{2,1,0:T(8,128)(2,1)}, u32[]{:S(2)}, u32[]{:S(2)}) collective-permute-start(bf16[12,128,128]{2,1,0:T(8,128)(2,1)S(1)} %collective-permute-done.3.refs_4_), channel_id=1, source_target_pairs={{0,8},{4,12},{8,0},{12,4},{16,24},{20,28},{24,16},{28,20},{1,9},{5... | collective-permute-start | bytes 1179656 | tf_op jit(solution)/shard_map/ppermute | solution.py:112
  25.8 9.8 %collective-permute-start.9 = (bf16[12,128,128]{2,1,0:T(8,128)(2,1)S(1)}, bf16[12,128,128]{2,1,0:T(8,128)(2,1)}, u32[]{:S(2)}, u32[]{:S(2)}) collective-permute-start(bf16[12,128,128]{2,1,0:T(8,128)(2,1)S(1)} %collective-permute-done.8.refs_10_), channel_id=1, source_target_pairs={{0,4},{4,0},{8,12},{12,8},{16,20},{20,16},{24,28},{28,24},{1,5},{5... | collective-permute-start | bytes 1179656 | tf_op jit(solution)/shard_map/ppermute | solution.py:112
  25.8 9.8 %collective-permute-start.4 = (bf16[12,128,128]{2,1,0:T(8,128)(2,1)S(1)}, bf16[12,128,128]{2,1,0:T(8,128)(2,1)}, u32[]{:S(2)}, u32[]{:S(2)}) collective-permute-start(bf16[12,128,128]{2,1,0:T(8,128)(2,1)S(1)} %collective-permute-done.3.refs_4_), channel_id=1, source_target_pairs={{0,4},{4,0},{8,12},{12,8},{16,20},{20,16},{24,28},{28,24},{1,5},{5... | collective-permute-start | bytes 1179656 | tf_op jit(solution)/shard_map/ppermute | solution.py:112
  26.3 9.3 %collective-permute-start.2 = (bf16[12,128,128]{2,1,0:T(8,128)(2,1)S(1)}, bf16[12,128,128]{2,1,0:T(8,128)(2,1)}, u32[]{:S(2)}, u32[]{:S(2)}) collective-permute-start(bf16[12,128,128]{2,1,0:T(8,128)(2,1)S(1)} %collective-permute-done.1.refs_2_), channel_id=1, source_target_pairs={{0,4},{4,0},{8,12},{12,8},{16,20},{20,16},{24,28},{28,24},{1,5},{5... | collective-permute-start | bytes 1179656 | tf_op jit(solution)/shard_map/ppermute | solution.py:112
  31.4 4.2 %collective-permute-start.13 = (bf16[12,128,128]{2,1,0:T(8,128)(2,1)}, bf16[12,128,128]{2,1,0:T(8,128)(2,1)}, u32[]{:S(2)}, u32[]{:S(2)}) collective-permute-start(bf16[12,128,128]{2,1,0:T(8,128)(2,1)} %collective-permute-done.12.refs_14_), channel_id=1, source_target_pairs={{0,4},{4,0},{8,12},{12,8},{16,20},{20,16},{24,28},{28,24},{1,5},{5... | collective-permute-start | bytes 1179656 | tf_op jit(solution)/shard_map/ppermute | solution.py:112
  33.3 2.3 collective-permute-start.6
  44.1 15.7 %copy-start.9 = (bf16[192,1024]{1,0:T(8,128)(2,1)S(1)}, bf16[192,1024]{1,0:T(8,128)(2,1)}, u32[]{:S(2)}) copy-start(bf16[192,1024]{1,0:T(8,128)(2,1)} %get-tuple-element.64.refs_4_) | copy-start | bytes 1179652
  44.2 47.6 %copy-start.22 = (f32[1025,32]{0,1:T(8,128)S(1)}, f32[1025,32]{0,1:T(8,128)}, u32[]{:S(2)}) copy-start(f32[1025,32]{0,1:T(8,128)} %param.44) | copy-start | bytes 393604
  56.3 60.3 %copy-start.3 = (bf16[1024,128]{1,0:T(8,128)(2,1)}, bf16[1024,128]{1,0:T(8,128)(2,1)S(1)}, u32[]{:S(2)}) copy-start(bf16[1024,128]{1,0:T(8,128)(2,1)S(1)} %convert_element_type.16.refs_0_) | copy-start | bytes 786436
  56.3 11.2 %collective-permute-start.16 = (bf16[1024,128]{1,0:T(8,128)(2,1)S(1)}, bf16[1024,128]{1,0:T(8,128)(2,1)S(1)}, u32[]{:S(2)}, u32[]{:S(2)}) collective-permute-start(bf16[1024,128]{1,0:T(8,128)(2,1)S(1)} %convert_element_type.16.refs_0_), channel_id=1, source_target_pairs={{0,3},{1,2},{2,1},{3,0},{4,7},{5,6},{6,5},{7,4},{8,11},{9,10},{10,... | collective-permute-start | bytes 786440 | tf_op jit(solution)/shard_map/ppermute | solution.py:112
  59.9 56.7 %collective-permute-start.19 = (bf16[192,1024]{1,0:T(8,128)(2,1)S(1)}, bf16[192,1024]{1,0:T(8,128)(2,1)S(1)}, u32[]{:S(2)}, u32[]{:S(2)}) collective-permute-start(bf16[192,1024]{1,0:T(8,128)(2,1)S(1)} %copy-done.9), channel_id=1, source_target_pairs={{0,3},{1,2},{2,1},{3,0},{4,7},{5,6},{6,5},{7,4},{8,11},{9,10},{10,... | collective-permute-start | bytes 1179656 | tf_op jit(solution)/shard_map/ppermute | solution.py:112
  60.2 56.4 %collective-permute-start.18 = (bf16[192,1024]{1,0:T(8,128)(2,1)S(1)}, bf16[192,1024]{1,0:T(8,128)(2,1)S(1)}, u32[]{:S(2)}, u32[]{:S(2)}) collective-permute-start(bf16[192,1024]{1,0:T(8,128)(2,1)S(1)} %copy-done.9), channel_id=1, source_target_pairs={{0,2},{1,3},{2,0},{3,1},{4,6},{5,7},{6,4},{7,5},{8,10},{9,11},{10,... | collective-permute-start | bytes 1179656 | tf_op jit(solution)/shard_map/ppermute | solution.py:112
  60.9 55.7 %collective-permute-start.17 = (bf16[192,1024]{1,0:T(8,128)(2,1)S(1)}, bf16[192,1024]{1,0:T(8,128)(2,1)S(1)}, u32[]{:S(2)}, u32[]{:S(2)}) collective-permute-start(bf16[192,1024]{1,0:T(8,128)(2,1)S(1)} %copy-done.9), channel_id=1, source_target_pairs={{0,1},{1,0},{2,3},{3,2},{4,5},{5,4},{6,7},{7,6},{8,9},{9,8},{10,11... | collective-permute-start | bytes 1179656 | tf_op jit(solution)/shard_map/ppermute | solution.py:112
  64.2 52.3 %collective-permute-start.15 = (bf16[1024,128]{1,0:T(8,128)(2,1)S(1)}, bf16[1024,128]{1,0:T(8,128)(2,1)S(1)}, u32[]{:S(2)}, u32[]{:S(2)}) collective-permute-start(bf16[1024,128]{1,0:T(8,128)(2,1)S(1)} %convert_element_type.16.refs_0_), channel_id=1, source_target_pairs={{0,2},{1,3},{2,0},{3,1},{4,6},{5,7},{6,4},{7,5},{8,10},{9,11},{10,... | collective-permute-start | bytes 786440 | tf_op jit(solution)/shard_map/ppermute | solution.py:112
  67.4 49.2 %copy-start.16 = (bf16[1024,128]{1,0:T(8,128)(2,1)}, bf16[1024,128]{1,0:T(8,128)(2,1)S(1)}, u32[]{:S(2)}) copy-start(bf16[1024,128]{1,0:T(8,128)(2,1)S(1)} %collective-permute-done.16.refs_3_) | copy-start | bytes 786436
  67.4 49.1 %collective-permute-start.14 = (bf16[1024,128]{1,0:T(8,128)(2,1)S(1)}, bf16[1024,128]{1,0:T(8,128)(2,1)S(1)}, u32[]{:S(2)}, u32[]{:S(2)}) collective-permute-start(bf16[1024,128]{1,0:T(8,128)(2,1)S(1)} %convert_element_type.16.refs_0_), channel_id=1, source_target_pairs={{0,1},{1,0},{2,3},{3,2},{4,5},{5,4},{6,7},{7,6},{8,9},{9,8},{10,11... | collective-permute-start | bytes 786440 | tf_op jit(solution)/shard_map/ppermute | solution.py:112
  133.7 18.1 %collective-permute-start.20 = (f32[104,1024]{1,0:T(8,128)S(1)}, f32[104,1024]{1,0:T(8,128)S(1)}, u32[]{:S(2)}, u32[]{:S(2)}) collective-permute-start(f32[104,1024]{1,0:T(8,128)S(1)} %slice_select_fusion), channel_id=1, source_target_pairs={{0,4},{4,0},{8,12},{12,8},{16,20},{20,16},{24,28},{28,24},{1,5},{5... | collective-permute-start | bytes 1277960 | tf_op jit(solution)/shard_map/ppermute | solution.py:112
  133.7 18.0 %copy-start = (f32[208,1024]{1,0:T(8,128)S(1)}, f32[208,1024]{1,0:T(8,128)}, u32[]{:S(2)}) copy-start(f32[208,1024]{1,0:T(8,128)} %get-tuple-element.65) | copy-start | bytes 2555908
  146.0 1.3 collective-permute-start.25
  148.2 6.6 %collective-permute-start.28 = (f32[16,512]{1,0:T(8,128)S(1)}, f32[16,512]{1,0:T(8,128)S(1)}, u32[]{:S(2)}, u32[]{:S(2)}) collective-permute-start(f32[16,512]{1,0:T(8,128)S(1)} %select_add_fusion.1), channel_id=1, source_target_pairs={{0,24},{4,28},{8,16},{12,20},{16,8},{20,12},{24,0},{28,4},{1,25},{... | collective-permute-start | bytes 98312 | tf_op jit(solution)/shard_map/ppermute | solution.py:112
  150.7 5.3 %collective-permute-start.27 = (f32[16,512]{1,0:T(8,128)S(1)}, f32[16,512]{1,0:T(8,128)S(1)}, u32[]{:S(2)}, u32[]{:S(2)}) collective-permute-start(f32[16,512]{1,0:T(8,128)S(1)} %select_add_fusion.1), channel_id=1, source_target_pairs={{0,16},{4,20},{8,24},{12,28},{16,0},{20,4},{24,8},{28,12},{1,17},{... | collective-permute-start | bytes 98312 | tf_op jit(solution)/shard_map/ppermute | solution.py:112
  151.2 4.8 %collective-permute-start.26 = (f32[16,512]{1,0:T(8,128)S(1)}, f32[16,512]{1,0:T(8,128)S(1)}, u32[]{:S(2)}, u32[]{:S(2)}) collective-permute-start(f32[16,512]{1,0:T(8,128)S(1)} %select_add_fusion.1), channel_id=1, source_target_pairs={{0,8},{4,12},{8,0},{12,4},{16,24},{20,28},{24,16},{28,20},{1,9},{5... | collective-permute-start | bytes 98312 | tf_op jit(solution)/shard_map/ppermute | solution.py:112
  151.8 13.8 %collective-permute-start.23 = (f32[104,1024]{1,0:T(8,128)S(1)}, f32[104,1024]{1,0:T(8,128)S(1)}, u32[]{:S(2)}, u32[]{:S(2)}) collective-permute-start(f32[104,1024]{1,0:T(8,128)S(1)} %select_add_fusion), channel_id=1, source_target_pairs={{0,24},{4,28},{8,16},{12,20},{16,8},{20,12},{24,0},{28,4},{1,25},{... | collective-permute-start | bytes 1277960 | tf_op jit(solution)/shard_map/ppermute | solution.py:112
  154.3 19.0 %collective-permute-start.22 = (f32[104,1024]{1,0:T(8,128)S(1)}, f32[104,1024]{1,0:T(8,128)S(1)}, u32[]{:S(2)}, u32[]{:S(2)}) collective-permute-start(f32[104,1024]{1,0:T(8,128)S(1)} %select_add_fusion), channel_id=1, source_target_pairs={{0,16},{4,20},{8,24},{12,28},{16,0},{20,4},{24,8},{28,12},{1,17},{... | collective-permute-start | bytes 1277960 | tf_op jit(solution)/shard_map/ppermute | solution.py:112
  154.8 18.6 %collective-permute-start.21 = (f32[104,1024]{1,0:T(8,128)S(1)}, f32[104,1024]{1,0:T(8,128)S(1)}, u32[]{:S(2)}, u32[]{:S(2)}) collective-permute-start(f32[104,1024]{1,0:T(8,128)S(1)} %select_add_fusion), channel_id=1, source_target_pairs={{0,8},{4,12},{8,0},{12,4},{16,24},{20,28},{24,16},{28,20},{1,9},{5... | collective-permute-start | bytes 1277960 | tf_op jit(solution)/shard_map/ppermute | solution.py:112
  156.0 17.6 %collective-permute-start.29 = (f32[16,512]{1,0:T(8,128)S(1)}, f32[16,512]{1,0:T(8,128)S(1)}, u32[]{:S(2)}, u32[]{:S(2)}) collective-permute-start(f32[16,512]{1,0:T(8,128)S(1)} %add_add_fusion.1), channel_id=1, source_target_pairs={{0,4},{4,0},{8,12},{12,8},{16,20},{20,16},{24,28},{28,24},{1,5},{5... | collective-permute-start | bytes 98312 | tf_op jit(solution)/shard_map/ppermute | solution.py:112
  173.5 1.8 collective-permute-start.24
  176.4 13.6 %copy-start.24 = (f32[1025,32]{0,1:T(8,128)S(1)}, f32[1025,32]{0,1:T(8,128)}, u32[]{:S(2)}) copy-start(f32[1025,32]{0,1:T(8,128)} %param.46) | copy-start | bytes 393604
  176.4 14.6 %copy-start.27 = (s32[192]{0:T(256)S(1)}, s32[192]{0:T(256)}, u32[]{:S(2)}) copy-start(s32[192]{0:T(256)} %constant.61) | copy-start | bytes 2308
  176.4 14.6 %copy-start.28 = (s32[192]{0:T(256)S(1)}, s32[192]{0:T(256)}, u32[]{:S(2)}) copy-start(s32[192]{0:T(256)} %constant.60) | copy-start | bytes 2308
  184.4 9.2 %collective-permute-start.32 = (f32[40,1024]{1,0:T(8,128)}, f32[40,1024]{1,0:T(8,128)S(1)}, u32[]{:S(2)}, u32[]{:S(2)}) collective-permute-start(f32[40,1024]{1,0:T(8,128)} %get-tuple-element.77.refs_0_), channel_id=1, source_target_pairs={{0,3},{1,2},{2,1},{3,0},{4,7},{5,6},{6,5},{7,4},{8,11},{9,10},{10,... | collective-permute-start | bytes 491528 | tf_op jit(solution)/shard_map/ppermute | solution.py:112
  186.9 13.6 %collective-permute-start.31 = (f32[40,1024]{1,0:T(8,128)}, f32[40,1024]{1,0:T(8,128)S(1)}, u32[]{:S(2)}, u32[]{:S(2)}) collective-permute-start(f32[40,1024]{1,0:T(8,128)} %get-tuple-element.77.refs_0_), channel_id=1, source_target_pairs={{0,2},{1,3},{2,0},{3,1},{4,6},{5,7},{6,4},{7,5},{8,10},{9,11},{10,... | collective-permute-start | bytes 491528 | tf_op jit(solution)/shard_map/ppermute | solution.py:112
  186.9 13.6 %collective-permute-start.30 = (f32[40,1024]{1,0:T(8,128)}, f32[40,1024]{1,0:T(8,128)S(1)}, u32[]{:S(2)}, u32[]{:S(2)}) collective-permute-start(f32[40,1024]{1,0:T(8,128)} %get-tuple-element.77.refs_0_), channel_id=1, source_target_pairs={{0,1},{1,0},{2,3},{3,2},{4,5},{5,4},{6,7},{7,6},{8,9},{9,8},{10,11... | collective-permute-start | bytes 491528 | tf_op jit(solution)/shard_map/ppermute | solution.py:112
  (16 other events, 89.0 us)

commit v3 on v2

--- a/solution.py
+++ b/solution.py
@@ -107,6 +107,15 @@
     return scale * (inner - mean_one - normed * mean_two)
 
 
+def params(microseconds):
+    return dict(
+        compiler_params=pltpu.CompilerParams(vmem_limit_bytes=56 * MEGA),
+        cost_estimate=pl.CostEstimate(
+            flops=int(microseconds * 1.1e9), bytes_accessed=int(microseconds * 1e6), transcendentals=0
+        ),
+    )
+
+
 def swap_with(value, axis, mask):
     count = lax.axis_size(axis)
     return lax.ppermute(value, axis, [(i, i ^ mask) for i in range(count)])
@@ -120,6 +129,14 @@
 
 def gather_xor(value, axis):
     return [value] + [swap_with(value, axis, r) for r in range(1, lax.axis_size(axis))]
+
+
+def gather_shared(value):
+    upper = (lax.axis_index("dp") & 1) == 1
+    half = value.shape[0] // 2
+    mine = jnp.where(upper, value[half:], value[:half])
+    parts = [swap_with(mine, "mp", r) for r in range(1, lax.axis_size("mp"))]
+    return parts, [swap_with(part, "dp", 1) for part in parts]
 
 
 def gather_tiles(low):
@@ -222,8 +239,8 @@
             pltpu.VMEM((total, BS, BS), bf16),
             pltpu.SemaphoreType.DMA((len(pieces),)),
         ],
-        compiler_params=pltpu.CompilerParams(vmem_limit_bytes=56 * MEGA),
         name="tables",
+        **params(8),
     )(place, *pieces, embedding, vectors, fc_bias)
 
 
@@ -266,7 +283,7 @@
 
 
 def attention_kernel(
-    heads, length, token_col, proj, cosine, sine, query_o, key_o, weight_o, hot, key_hot, queries, wide
+    heads, length, token_col, proj, cosine, sine, query_o, key_o, weight_o, low_o, hot, key_hot, queries, wide
 ):
     seq = token_col.shape[0]
     vocab = proj.shape[0]
@@ -335,6 +352,7 @@
                 ),
             ).astype(bf16)
         weight_o[span] = weights[:, : heads * vocab]
+        low_o[span] = weights[:, : heads * vocab].astype(bf16)
 
 
 def attention(length, token_col, proj, cosine, sine, heads):
@@ -344,11 +362,12 @@
     return pl.pallas_call(
         functools.partial(attention_kernel, heads),
         in_specs=[SMEM] + [VMEM] * 4,
-        out_specs=[VMEM] * 3,
+        out_specs=[VMEM] * 4,
         out_shape=[
             o((heads, seq, WIDE), bf16),
             o((heads, seq, WIDE), bf16),
             o((seq, heads * vocab), f32),
+            o((seq, heads * vocab), bf16),
         ],
         scratch_shapes=[
             pltpu.VMEM((seq, WIDE), bf16),
@@ -356,8 +375,8 @@
             pltpu.VMEM((heads, seq, WIDE), bf16),
             pltpu.VMEM((WIDE, heads * 4 * WIDE), bf16),
         ],
-        compiler_params=pltpu.CompilerParams(vmem_limit_bytes=56 * MEGA),
         name="attention",
+        **params(11),
     )(length, token_col, proj, cosine, sine)
 
 
@@ -463,8 +482,8 @@
             pltpu.VMEM((heads, seq, WIDE), bf16),
             pltpu.VMEM((heads, HD, seq), f32),
         ],
-        compiler_params=pltpu.CompilerParams(vmem_limit_bytes=56 * MEGA),
         name="attention_back",
+        **params(11),
     )(token_col, token_row, query, key, weight, weight_grad, cosine, sine, cosine_t, sine_t)
 
 
@@ -482,17 +501,20 @@
     *refs,
 ):
     weights, refs = refs[:parts], refs[parts:]
-    payloads, refs = refs[:parts], refs[parts:]
-    sums_o, grad_o, mixing, low_weights, table = refs
+    payload, mine, others = refs[0], refs[1:parts], refs[parts : 2 * parts - 1]
+    sums_o, grad_o, mixing, low_weights, table = refs[2 * parts - 1 :]
     step = pl.program_id(0)
-    me, length = ints[0], ints[1]
+    me, length, upper = ints[0], ints[1], ints[2]
     vocab = embed.shape[0]
     height = heads * vocab
 
     @pl.when(step == 0)
     def _():
-        for r in range(parts):
-            mixing[me ^ r] = payloads[r][...]
+        mixing[me] = payload[...]
+        size = payload.shape[0] // 2
+        for r in range(1, parts):
+            mixing[me ^ r, pl.ds(pl.multiple_of(upper * size, size), size)] = mine[r - 1][...]
+            mixing[me ^ r, pl.ds(pl.multiple_of((1 - upper) * size, size), size)] = others[r - 1][...]
         down = jnp.zeros((vocab, D), f32)
         for g in range(parts):
             one = mixing[g, height:].astype(f32)
@@ -512,8 +534,12 @@
     normed, scale = stats_of(x)
     gain = vec[3:4]
     final = (normed * gain + vec[4:5]).astype(bf16)
-    head_low = head[:D].astype(bf16)
-    logits = dot(final, head_low) + head[D : D + 1]
+    head_low = head[:, :D].astype(bf16)
+    square = (vocab, vocab)
+    bias_row = jnp.sum(
+        jnp.where(lanes(square) == sublanes(square), head[:, D : D + 1], 0.0), axis=0, keepdims=True
+    )
+    logits = dot(final, head_low, NT) + bias_row
     shifted = logits - jnp.max(logits, axis=-1, keepdims=True)
     log_probs = shifted - jnp.log(jnp.sum(jnp.exp(shifted), axis=-1, keepdims=True))
     target = lanes((ROWS, vocab)) == target_col[...]
@@ -522,11 +548,15 @@
     picked = jnp.sum(jnp.where(target, log_probs, 0.0), axis=-1, keepdims=True)
     loss = -jnp.sum(slot_weight * picked, keepdims=True)
     logit_grad = ((jnp.exp(log_probs) - jnp.where(target, 1.0, 0.0)) * slot_weight).astype(bf16)
-    final_grad = dot(logit_grad, head_low, NT)
+    final_grad = dot(logit_grad, head_low)
     grad = norm_back(final_grad, normed, scale, gain)
-    high, rest = split2(grad)
+    high = grad.astype(bf16)
     token_hot = jnp.where(sublanes((vocab, ROWS)) == token_row[...], 1.0, 0.0).astype(bf16)
-    sums_o[0:vocab] += dot(token_hot, high) + dot(token_hot, rest)
+    own = weights[0][...].astype(f32)
+    if height < WIDE:
+        own = jnp.concatenate([own, jnp.zeros((ROWS, WIDE - height), f32)], axis=1)
+    both = dot(jnp.concatenate([own.T.astype(bf16), token_hot], axis=0), high)
+    sums_o[0:vocab] += both[WIDE:]
     sums_o[vocab : 2 * vocab] += dot(logit_grad, final, TN)
     base = 2 * vocab
     sums_o[base : base + 1] += jnp.sum(final_grad * normed, axis=0, keepdims=True)
@@ -538,11 +568,25 @@
     sums_o[base + 3 : base + 4, :WIDE] += jnp.where(
         lane == 0, loss, jnp.where(lane == 1, count, 0.0)
     )
-    sums_o[base + 16 : base + 16 + height] += dot(weights[0][...], high, TN)
-    grad_o[...] = dot(high, payloads[0][:height], NT)
-
-
-def loss_rows(ints, floats, token_col, target_col, token_row, embedding, head, vectors, weights, payloads, heads):
+    sums_o[base + 16 : base + 16 + height] += both[:height]
+    grad_o[...] = dot(high, payload[:height], NT)
+
+
+def loss_rows(
+    ints,
+    floats,
+    token_col,
+    target_col,
+    token_row,
+    embedding,
+    head,
+    vectors,
+    weights,
+    payload,
+    mine,
+    others,
+    heads,
+):
     seq = token_col.shape[0]
     vocab = embedding.shape[0]
     parts = len(weights)
@@ -557,20 +601,34 @@
         in_specs=[SMEM, SMEM, col, col, pl.BlockSpec((1, ROWS), lambda i: (0, i))]
         + [full(embedding), full(head), full(vectors)]
         + [pl.BlockSpec((ROWS, height), lambda i: (i, 0))] * parts
-        + [full(payloads[0])] * parts,
+        + [full(payload)]
+        + [full(mine[0])] * (2 * parts - 2),
         out_specs=[
             pl.BlockSpec(sums_shape, lambda i: (0, 0)),
             pl.BlockSpec((ROWS, height), lambda i: (i, 0)),
         ],
         out_shape=[o(sums_shape, f32), o((seq, height), f32)],
         scratch_shapes=[
-            pltpu.VMEM((parts,) + payloads[0].shape, bf16),
+            pltpu.VMEM((parts,) + payload.shape, bf16),
             pltpu.VMEM((parts, ROWS, height), bf16),
             pltpu.VMEM((4 * vocab, D), bf16),
         ],
-        compiler_params=pltpu.CompilerParams(vmem_limit_bytes=56 * MEGA),
         name="loss_rows",
-    )(ints, floats, token_col, target_col, token_row, embedding, head, vectors, *weights, *payloads)
+        **params(12),
+    )(
+        ints,
+        floats,
+        token_col,
+        target_col,
+        token_row,
+        embedding,
+        head,
+        vectors,
+        *weights,
+        payload,
+        *mine,
+        *others,
+    )
 
 
 def padded(block):
@@ -630,7 +688,7 @@
         + jnp.sum(dot6(val, val, NT) * dot6(mixed, mixed, NT), keepdims=True)
         + jnp.sum(bias_grad * bias_grad, keepdims=True)
     )
-    hidden_o[vocab : vocab + 8] = jnp.broadcast_to(square, (8, D))
+    hidden_o[vocab : vocab + 16] = jnp.broadcast_to(square, (16, D))
 
     def put_left(index, block):
         block = padded(block)
@@ -702,23 +760,25 @@
         out_shape=[
             o((n_left, 3 * HB, BS), bf16),
             o((n_right, 3 * HB, BS), bf16),
-            o((vocab + 8, D), f32),
+            o((vocab + 16, D), f32),
             o((1, ff_local), f32),
         ],
-        compiler_params=pltpu.CompilerParams(vmem_limit_bytes=56 * MEGA),
         name="factors",
+        **params(7),
     )(sums, table, *mats, upper, normed, act, values)
 
 
-def small_kernel(parts, corrections, sums, *refs):
-    hiddens, refs = refs[:parts], refs[parts:]
+def small_kernel(parts, corrections, ints, sums, own, *refs):
+    mine, others, refs = refs[: parts - 1], refs[parts - 1 : 2 * parts - 2], refs[2 * parts - 2 :]
     bias_grad, refs = refs[0], refs[1:]
     weights, refs = refs[:12], refs[12:]
-    outs, scalars = refs[:12], refs[12]
+    outs, scalars, total = refs[:12], refs[12], refs[13]
     vocab = weights[0].shape[0]
     base = 2 * vocab
-    total = [ref[...] for ref in hiddens]
-    total = tree_sum(total)
+    size = own.shape[0] // 2
+    for place, group in ((ints[0], mine), (1 - ints[0], others)):
+        span = pl.ds(pl.multiple_of(place * size, size), size)
+        total[span] = tree_sum([own[span]] + [ref[...] for ref in group])
     hidden = total[:vocab]
     square = total[vocab : vocab + 1, 0:1]
     rows = sums[0:vocab]
@@ -757,8 +817,12 @@
 
     everything = slice(None)
     update(0, everything, embed_grad)
-    update(1, slice(0, D), head_grad.T)
-    update(1, slice(D, D + 1), head_bias)
+    shape = (vocab, vocab)
+    head_column = jnp.sum(
+        jnp.where(lanes(shape) == sublanes(shape), head_bias, 0.0), axis=1, keepdims=True
+    )
+    update(1, (everything, slice(0, D)), head_grad)
+    update(1, (everything, slice(D, D + 1)), head_column)
     update(2, everything, vector_grad)
     update(3, everything, bias_grad[...])
     lane = lanes((1, WIDE))
@@ -767,16 +831,17 @@
     )
 
 
-def small(corrections, sums, hiddens, bias_grad, weights):
+def small(corrections, upper, sums, hidden, mine, others, bias_grad, weights):
     o = jax.ShapeDtypeStruct
     return pl.pallas_call(
-        functools.partial(small_kernel, len(hiddens)),
-        in_specs=[SMEM] + [VMEM] * (1 + len(hiddens) + 1 + 12),
+        functools.partial(small_kernel, 1 + len(mine)),
+        in_specs=[SMEM] * 2 + [VMEM] * (2 + 2 * len(mine) + 1 + 12),
         out_specs=[VMEM] * 13,
         out_shape=[o(weight.shape, f32) for weight in weights] + [o((1, WIDE), f32)],
-        compiler_params=pltpu.CompilerParams(vmem_limit_bytes=56 * MEGA),
+        scratch_shapes=[pltpu.VMEM(hidden.shape, f32)],
         name="small",
-    )(corrections, sums, *hiddens, bias_grad, *weights)
+        **params(4),
+    )(corrections, upper, sums, hidden, *mine, *others, bias_grad, *weights)
 
 
 GROUP = 0
@@ -830,9 +895,9 @@
 def swap(x):
     return pltpu.roll(x,HB,1)
 
-def soap_kernel(count, per, scal, left_at, right_at, lefts, rights, W, m, v, L, R, QL, QR, W_o, low_o, m_o, v_o, L_o, R_o, QL_o, QR_o, ML_s, MR_s, work, A21_s, A22_s, W11_s):
+def soap_kernel(count, per, corrections, scal, left_at, right_at, lefts, rights, W, m, v, L, R, QL, QR, W_o, low_o, m_o, v_o, L_o, R_o, QL_o, QR_o, ML_s, MR_s, work, A21_s, A22_s, W11_s):
     step=pl.program_id(0)
-    scale=scal[0]; c1=scal[1]; c2=scal[2]
+    scale=scal[0:1,0:1]; c1=corrections[0]; c2=corrections[1]
     left=lax.broadcasted_iota(jnp.int32,(HB,BS),1)<HB
     span=range(per)
     pairs=[(lefts[left_at[step*per+s]],rights[right_at[step*per+s]]) for s in span]
@@ -901,7 +966,7 @@
             return carry
         lax.fori_loop(0,count//UN,last,0)
 
-def soap(scal,left_at,right_at,lefts,rights,W,m,v,L,R,QL,QR):
+def soap(corrections,scal,left_at,right_at,lefts,rights,W,m,v,L,R,QL,QR):
     count=W.shape[0]
     per=3 if count%3==0 else 1
     blk=pl.BlockSpec((per,BS,BS),lambda i:(i,0,0))
@@ -911,13 +976,13 @@
     return pl.pallas_call(
         functools.partial(soap_kernel,count,per),
         grid=(count//per,),
-        in_specs=[SMEM]*3+[whole(lefts),whole(rights)]+[blk]*7,
+        in_specs=[SMEM,pl.BlockSpec((1,WIDE),lambda i:(0,0)),SMEM,SMEM]+[whole(lefts),whole(rights)]+[blk]*7,
         out_specs=[blk]*6+[full]*2,
         out_shape=[o(f32),o(bf16),o(f32),o(f32),o(f32),o(f32),o(f32),o(f32)],
         scratch_shapes=[pltpu.VMEM((count,BS,BS),f32)]*2+[pltpu.VMEM((count,HB,BS),f32)]*4,
         compiler_params=pltpu.CompilerParams(vmem_limit_bytes=56*1024*1024),
         name="soap_tiles",
-    )(scal,left_at,right_at,lefts,rights,W,m,v,L,R,QL,QR)
+    )(corrections,scal,left_at,right_at,lefts,rights,W,m,v,L,R,QL,QR)
 
 
 def local(
@@ -950,6 +1015,7 @@
     dp_count = lax.axis_size("dp")
     dp_index = lax.axis_index("dp")
     mp_index = lax.axis_index("mp")
+    upper_pair = dp_index & 1
     heads = H // mp_count
     ff_local = fc_bias.shape[1]
     count = weight_tiles.shape[0]
@@ -968,22 +1034,24 @@
     token_col = tokens.reshape(seq, 1)
     target_col = jnp.roll(tokens, -1, axis=1).reshape(seq, 1)
     cosine, sine, cosine_t, sine_t = rotary_tables(seq)
-    payloads = gather_xor(payload, "mp")
-    query, key, weight = attention(lengths, token_col, proj, cosine, sine, heads)
-    weights = gather_xor(weight.astype(bf16), "mp")
+    parts, others = gather_shared(payload)
+    query, key, weight, weight_low = attention(lengths, token_col, proj, cosine, sine, heads)
+    weights = gather_xor(weight_low, "mp")
     length = lengths[0]
     inverse_length = 1.0 / jnp.maximum(length - 1, 1).astype(f32)
     sums, weight_grad = loss_rows(
-        jnp.stack([mp_index, length]),
+        jnp.stack([mp_index, length, upper_pair]),
         inverse_length[None],
         token_col,
         target_col,
         tokens,
         embedding,
-        head_table,
+        head_table.T,
         vectors,
         weights,
-        payloads,
+        payload,
+        parts,
+        others,
         heads,
     )
     sums = sum_dp(sums)
@@ -994,7 +1062,7 @@
     left, right, hidden, bias_grad = factors(
         sums, table, mats, upper, normed, act, values, heads
     )
-    hiddens = gather_xor(hidden, "mp")
+    hidden_parts, hidden_others = gather_shared(hidden)
     corrections = 1.0 - jnp.power(
         jnp.array([BETA_ONE, BETA_TWO], f32), step_count.astype(f32)
     )
@@ -1002,9 +1070,9 @@
         embedding,
         embedding_first,
         embedding_second,
-        head_table,
-        head_first,
-        head_second,
+        head_table.T,
+        head_first.T,
+        head_second.T,
         vectors,
         vectors_first,
         vectors_second,
@@ -1012,7 +1080,17 @@
         fc_bias_first,
         fc_bias_second,
     )
-    *small_out, scalars = small(corrections, sums, hiddens, bias_grad, small_weights)
+    *small_out, scalars = small(
+        corrections,
+        upper_pair[None],
+        sums,
+        hidden,
+        hidden_parts,
+        hidden_others,
+        bias_grad,
+        small_weights,
+    )
+    small_out[3:6] = [value.T for value in small_out[3:6]]
     slots = dp_index * count + jnp.arange(count, dtype=jnp.int32)
     natural = jnp.sum(
         jnp.where(
@@ -1027,7 +1105,8 @@
     left_at = jnp.sum(jnp.where(same, left_of[None, :], 0), axis=1)
     right_at = jnp.sum(jnp.where(same, right_of[None, :], 0), axis=1)
     results = soap(
-        jnp.concatenate([scalars[0, :1], corrections]),
+        corrections,
+        scalars,
         left_at,
         right_at,
         left,

time: 272 us -> 246 us (0.904)
  starting transfers between devices: 50.3 us -> 38.3 us
  local copies, waits for them, and re-layouts: 14.5 us -> 6.39 us
  waiting for transfers between devices: 76.3 us -> 73.4 us
    ppermute x33 -> x39, starting transfers between devices: 50.3 us -> 38.3 us  [swap_with(): return lax.ppermute(value, axis, [(i, i ^ mask) for i in range(count)])]
    unnamed x68 -> x62, local copies, waits for them, and re-layouts: 10.4 us -> 2.4 us
    ppermute x33 -> x39, waiting for transfers between devices: 76.3 us -> 73.4 us  [swap_with(): return lax.ppermute(value, axis, [(i, i ^ mask) for i in range(count)])]
  transfers between devices with their start and end apart: 33 -> 39, of which waited for: 14 -> 15; matrix products, arithmetic and copies ran while one was open for 4% -> 3% of each run, Pallas kernels for 4% -> 5%
where the time goes in v3:
time: 246 us; the launch traced here: 245 us
  Pallas kernels  114 us (46%)
  waiting for transfers between devices  73.4 us (30%)
  starting transfers between devices  38.3 us (16%)
  other arithmetic  10.6 us (4%)
  local copies, waits for them, and re-layouts  6.39 us (3%)
  between operations  2.65 us (1%)
    ppermute x39, waiting for transfers between devices, swap_with(): return lax.ppermute(value, axis, [(i, i ^ mask) for i in range(count)])  73.4 us
    pallas_call x1, Pallas kernels, soap(): pl.pallas_call(functools.partial(soap_kernel, count, per), grid=(count //...  57.9 us
    ppermute x39, starting transfers between devices, swap_with(): return lax.ppermute(value, axis, [(i, i ^ mask) for i in range(count)])  38.3 us
    pallas_call x1, Pallas kernels, loss_rows(): pl.pallas_call(functools.partial(loss_kernel, parts, heads), grid=(seq //...  13.5 us
    pallas_call x1, Pallas kernels, attention_back(): pl.pallas_call(functools.partial(attention_back_kernel, heads), in_specs=...  11.5 us
    pallas_call x1, Pallas kernels, attention(): pl.pallas_call(functools.partial(attention_kernel, heads), in_specs=[SMEM...  11.1 us
    pallas_call x1, Pallas kernels, tables(): pl.pallas_call(functools.partial(tables_kernel, tile_places(shapes), head...  8.42 us
    pallas_call x1, Pallas kernels, factors(): pl.pallas_call(functools.partial(factors_kernel, heads), in_specs=[VMEM]...  7.96 us
  transfers between devices with their start and end apart: 39, of which 15 were waited for; matrix products, arithmetic and copies ran while one was open for 3% of the time, Pallas kernels for 5%

profile of v3, /device:TPU:0, one launch (start us, length us, event | category | flops | bytes accessed | tf_op | source)
XLA Modules:
  0.0 245.0 jit_solution(4831763145682993661)
XLA Ops:
  0.7 1.6 convert_element_type.12
  2.3 3.0 %collective-permute-start.8 = (bf16[12,128,128]{2,1,0:T(8,128)(2,1)S(1)}, bf16[12,128,128]{2,1,0:T(8,128)(2,1)S(1)}, u32[]{:S(2)}, u32[]{:S(2)}) collective-permute-start(bf16[12,128,128]{2,1,0:T(8,128)(2,1)S(1)} %get-tuple-element.108.refs_8_), channel_id=1, source_target_pairs={{0,8},{4,12},{8,0},{12,4},{16,24},{20,28},{24,16},{28,20},{1,9},{5... | collective-permute-start | bytes 1179656 | tf_op jit(solution)/shard_map/ppermute | solution.py:121
  5.3 1.5 collective-permute-start.3
  7.5 7.8 %collective-permute-done.8.refs_10_ = bf16[12,128,128]{2,1,0:T(8,128)(2,1)S(1)} collective-permute-done((bf16[12,128,128]{2,1,0:T(8,128)(2,1)S(1)}, bf16[12,128,128]{2,1,0:T(8,128)(2,1)S(1)}, u32[]{:S(2)}, u32[]{:S(2)}) %collective-permute-start.8) | collective-permute-done | bytes 393248 | tf_op jit(solution)/shard_map/ppermute | solution.py:121
  15.3 2.1 collective-permute-done.3.refs_4_
  17.4 1.5 collective-permute-start.12
  18.9 6.9 %collective-permute-done.10.refs_12_ = bf16[12,128,128]{2,1,0:T(8,128)(2,1)S(1)} collective-permute-done((bf16[12,128,128]{2,1,0:T(8,128)(2,1)S(1)}, bf16[12,128,128]{2,1,0:T(8,128)(2,1)S(1)}, u32[]{:S(2)}, u32[]{:S(2)}) %collective-permute-start.10) | collective-permute-done | bytes 393248 | tf_op jit(solution)/shard_map/ppermute | solution.py:121
  26.5 6.4 %collective-permute-done.12.refs_14_ = bf16[12,128,128]{2,1,0:T(8,128)(2,1)} collective-permute-done((bf16[12,128,128]{2,1,0:T(8,128)(2,1)S(1)}, bf16[12,128,128]{2,1,0:T(8,128)(2,1)}, u32[]{:S(2)}, u32[]{:S(2)}) %collective-permute-start.12) | collective-permute-done | bytes 393248 | tf_op jit(solution)/shard_map/ppermute | solution.py:121
  32.9 1.2 collective-permute-done.5.refs_6_
  34.1 0.7 copy-done.14
  35.4 1.0 copy.57.token_col
  37.8 8.4 %tables.1 = (bf16[1024,768]{1,0:T(8,128)(2,1)}, bf16[256,1024]{1,0:T(8,128)(2,1)}, bf16[1024,1024]{1,0:T(8,128)(2,1)}, bf16[1024,1024]{1,0:T(8,128)(2,1)}, f32[3...) custom-call(s32[192]{0:T(256)} %fusion.1.place, ...), custom_call_target="tpu_custom_call" | custom-call | flops 8800000000 | bytes 8000000 | tf_op jit(solution)/shard_map/tables/pallas_call | solution.py:225
  46.2 11.1 %attention.1 = (bf16[4,1024,128]{2,1,0:T(8,128)(2,1)}, bf16[4,1024,128]{2,1,0:T(8,128)(2,1)}, f32[1024,128]{1,0:T(8,128)}, bf16[1024,128]{1,0:T(8,128)(2,1)}) custom-call(s32[1]{0:T(128)S(6)} %copy.60.length, s32[1024,1]{1,0:T(8,128)} %copy.57.token_col, f32[32,768]{1,0:T(8,128)} %get-tuple-element.63.proj, f32[1024,128]{1,0:T(8,128)} %constant.51.clone.cosine, ...), custom_call_target="tpu_custom_call" | custom-call | flops 12099999744 | bytes 11000000 | tf_op jit(solution)/shard_map/attention/pallas_call | solution.py:362
  57.3 1.6 collective-permute-start.14
  59.4 2.6 %collective-permute-start.18 = (bf16[96,1024]{1,0:T(8,128)(2,1)S(1)}, bf16[96,1024]{1,0:T(8,128)(2,1)S(1)}, u32[]{:S(2)}, u32[]{:S(2)}) collective-permute-start(bf16[96,1024]{1,0:T(8,128)(2,1)S(1)} %slice_select_fusion.1), channel_id=1, source_target_pairs={{0,2},{1,3},{2,0},{3,1},{4,6},{5,7},{6,4},{7,5},{8,10},{9,11},{10,... | collective-permute-start | bytes 589832 | tf_op jit(solution)/shard_map/ppermute | solution.py:121
  62.0 1.3 collective-permute-start.19
  63.4 1.7 collective-permute-start.15
  65.1 10.7 %collective-permute-done.17.refs_5_ = bf16[96,1024]{1,0:T(8,128)(2,1)S(1)} collective-permute-done((bf16[96,1024]{1,0:T(8,128)(2,1)S(1)}, bf16[96,1024]{1,0:T(8,128)(2,1)S(1)}, u32[]{:S(2)}, u32[]{:S(2)}) %collective-permute-start.17) | collective-permute-done | bytes 196640 | tf_op jit(solution)/shard_map/ppermute | solution.py:121
  75.8 5.9 %collective-permute-start.16 = (bf16[1024,128]{1,0:T(8,128)(2,1)}, bf16[1024,128]{1,0:T(8,128)(2,1)S(1)}, u32[]{:S(2)}, u32[]{:S(2)}) collective-permute-start(bf16[1024,128]{1,0:T(8,128)(2,1)} %get-tuple-element.64.refs_0_), channel_id=1, source_target_pairs={{0,3},{1,2},{2,1},{3,0},{4,7},{5,6},{6,5},{7,4},{8,11},{9,10},{10,... | collective-permute-start | bytes 786440 | tf_op jit(solution)/shard_map/ppermute | solution.py:121
  83.0 0.7 add_bitcast_fusion
  83.7 1.0 copy.58.target_col
  85.4 12.2 %collective-permute-done.15.refs_2_ = bf16[1024,128]{1,0:T(8,128)(2,1)S(1)} collective-permute-done((bf16[1024,128]{1,0:T(8,128)(2,1)}, bf16[1024,128]{1,0:T(8,128)(2,1)S(1)}, u32[]{:S(2)}, u32[]{:S(2)}) %collective-permute-start.15) | collective-permute-done | bytes 262176 | tf_op jit(solution)/shard_map/ppermute | solution.py:121
  98.7 13.5 %loss_rows.1 = (f32[208,1024]{1,0:T(8,128)}, f32[1024,128]{1,0:T(8,128)}) custom-call(s32[3]{0:T(128)} %pad_add_fusion.ints, f32[1]{0:T(128)S(6)} %div.10.floats, s32[1024,1]{1,0:T(8,128)} %copy.57.token_col, s32[1024,1]{1,0:T(8,128)} %copy.58.target_col, s32[1,1024]{1,0:T(1,128)} %token_row.3, f32[32,1024]{1,0:T(8,128)} %refs_7_.1, f32[32,1025]{1,0:T(8,128)} %bitcast.14, ...), custom_call_target="tpu_custom_call" | custom-call | flops 13200000000 | bytes 12000000 | tf_op jit(solution)/shard_map/loss_rows/pallas_call | solution.py:598
  112.2 1.2 slice_select_fusion
  113.5 11.5 %attention_back.1 = f32[32,512]{1,0:T(8,128)} custom-call(s32[1024,1]{1,0:T(8,128)} %copy.57.token_col, s32[1,1024]{1,0:T(1,128)} %token_row.3, bf16[4,1024,128]{2,1,0:T(8,128)(2,1)} %get-tuple-element.67.query, bf16[4,1024,128]{2,1,0:T(8,128)(2,1)} %get-tuple-element.68.key, f32[1024,128]{1,0:T(8,128)} %get-tuple-element.69.weight, ...), custom_call_target="tpu_custom_call" | custom-call | flops 12099999744 | bytes 11000000 | tf_op jit(solution)/shard_map/attention_back/pallas_call | solution.py:474
  125.0 0.8 slice_select_fusion.3
  127.1 0.8 select_add_fusion.1
  127.9 0.7 collective-permute-start.29
  128.6 1.4 collective-permute-start.30
  130.0 1.4 collective-permute-start.31
  131.5 0.7 collective-permute-start.24
  132.3 1.4 collective-permute-start.25
  133.6 1.4 collective-permute-start.26
  135.8 8.5 %collective-permute-done.24 = f32[104,1024]{1,0:T(8,128)S(1)} collective-permute-done((f32[104,1024]{1,0:T(8,128)S(1)}, f32[104,1024]{1,0:T(8,128)S(1)}, u32[]{:S(2)}, u32[]{:S(2)}) %collective-permute-start.24) | collective-permute-done | bytes 426016 | tf_op jit(solution)/shard_map/ppermute | solution.py:121
  144.6 8.5 %collective-permute-done.26 = f32[104,1024]{1,0:T(8,128)S(1)} collective-permute-done((f32[104,1024]{1,0:T(8,128)S(1)}, f32[104,1024]{1,0:T(8,128)S(1)}, u32[]{:S(2)}, u32[]{:S(2)}) %collective-permute-start.26) | collective-permute-done | bytes 426016 | tf_op jit(solution)/shard_map/ppermute | solution.py:121
  153.9 1.1 collective-permute-done.27
  155.1 1.0 pad_maximum_fusion.sums
  156.1 8.0 %factors.1 = (bf16[18,192,128]{2,1,0:T(8,128)(2,1)}, bf16[38,192,128]{2,1,0:T(8,128)(2,1)}, f32[48,1024]{1,0:T(8,128)}, f32[1,1024]{1,0:T(1,128)}) custom-call(f32[208,1024]{1,0:T(8,128)} %pad_maximum_fusion.sums, f32[32,512]{1,0:T(8,128)} %pad_maximum_fusion.1.table, bf16[1024,768]{1,0:T(8,128)(2,1)} %get-tuple-element.71.mat_q, ...), custom_call_target="tpu_custom_call" | custom-call | flops 7699999744 | bytes 7000000 | tf_op jit(solution)/shard_map/factors/pallas_call | solution.py:756
  164.1 1.0 slice_select_fusion.2
  165.0 5.0 %collective-permute-start.33 = (f32[24,1024]{1,0:T(8,128)S(1)}, f32[24,1024]{1,0:T(8,128)S(1)}, u32[]{:S(2)}, u32[]{:S(2)}) collective-permute-start(f32[24,1024]{1,0:T(8,128)S(1)} %slice_select_fusion.2), channel_id=1, source_target_pairs={{0,1},{1,0},{2,3},{3,2},{4,5},{5,4},{6,7},{7,6},{8,9},{9,8},{10,11... | collective-permute-start | bytes 294920 | tf_op jit(solution)/shard_map/ppermute | solution.py:121
  170.0 1.9 collective-permute-start.34
  171.9 1.4 collective-permute-start.35
  173.6 2.5 %collective-permute-done.34.refs_1_ = f32[24,1024]{1,0:T(8,128)S(1)} collective-permute-done((f32[24,1024]{1,0:T(8,128)S(1)}, f32[24,1024]{1,0:T(8,128)S(1)}, u32[]{:S(2)}, u32[]{:S(2)}) %collective-permute-start.34) | collective-permute-done | bytes 98336 | tf_op jit(solution)/shard_map/ppermute | solution.py:121
  176.1 4.3 %collective-permute-done.35.refs_2_ = f32[24,1024]{1,0:T(8,128)S(1)} collective-permute-done((f32[24,1024]{1,0:T(8,128)S(1)}, f32[24,1024]{1,0:T(8,128)S(1)}, u32[]{:S(2)}, u32[]{:S(2)}) %collective-permute-start.35) | collective-permute-done | bytes 98336 | tf_op jit(solution)/shard_map/ppermute | solution.py:121
  180.4 0.7 select_reduce_fusion
  182.4 3.3 %small.1 = (f32[32,1024]{1,0:T(8,128)}, f32[32,1024]{1,0:T(8,128)}, f32[32,1024]{1,0:T(8,128)}, f32[32,1025]{1,0:T(8,128)}, f32[32,1025]{1,0:T(8,128)}, /*index=...) custom-call(f32[2]{0:T(128)} %power_subtract_fusion.corrections, ...), custom_call_target="tpu_custom_call" | custom-call | flops 4400000000 | bytes 4000000 | tf_op jit(solution)/shard_map/small/pallas_call | solution.py:836
  185.6 1.3 fusion.3
  186.9 57.9 %soap_tiles.1 = (f32[24,128,128]{2,1,0:T(8,128)}, bf16[24,128,128]{2,1,0:T(8,128)(2,1)}, f32[24,128,128]{2,1,0:T(8,128)}, f32[24,128,128]{2,1,0:T(8,128)}, f32[2...) custom-call(f32[2]{0:T(128)} %power_subtract_fusion.corrections, ...), custom_call_target="tpu_custom_call" | custom-call | tf_op jit(solution)/shard_map/soap_tiles/pallas_call | solution.py:976
  (125 shorter events, 10.1 us)
Async XLA Ops:
  0.7 34.7 %copy-start.4 = (s32[1,1024]{1,0:T(1,128)S(1)}, s32[1,1024]{1,0:T(1,128)}, u32[]{:S(2)}) copy-start(s32[1,1024]{1,0:T(1,128)} %token_row.3) | copy-start | bytes 12292
  2.2 34.8 %copy-start.5 = (s32[192]{0:T(256)S(1)}, s32[192]{0:T(256)}, u32[]{:S(2)}) copy-start(s32[192]{0:T(256)} %param.32) | copy-start | bytes 2308
  2.3 35.4 %copy-start.1 = (bf16[12,128,128]{2,1,0:T(8,128)(2,1)}, bf16[12,128,128]{2,1,0:T(8,128)(2,1)S(1)}, u32[]{:S(2)}) copy-start(bf16[12,128,128]{2,1,0:T(8,128)(2,1)S(1)} %get-tuple-element.108.refs_8_) | copy-start | bytes 1179652
  2.3 35.4 %copy-start.2 = (bf16[12,128,128]{2,1,0:T(8,128)(2,1)}, bf16[12,128,128]{2,1,0:T(8,128)(2,1)S(1)}, u32[]{:S(2)}) copy-start(bf16[12,128,128]{2,1,0:T(8,128)(2,1)S(1)} %get-tuple-element.109.refs_0_) | copy-start | bytes 1179652
  2.3 12.9 %collective-permute-start.8 = (bf16[12,128,128]{2,1,0:T(8,128)(2,1)S(1)}, bf16[12,128,128]{2,1,0:T(8,128)(2,1)S(1)}, u32[]{:S(2)}, u32[]{:S(2)}) collective-permute-start(bf16[12,128,128]{2,1,0:T(8,128)(2,1)S(1)} %get-tuple-element.108.refs_8_), channel_id=1, source_target_pairs={{0,8},{4,12},{8,0},{12,4},{16,24},{20,28},{24,16},{28,20},{1,9},{5... | collective-permute-start | bytes 1179656 | tf_op jit(solution)/shard_map/ppermute | solution.py:121
  5.3 12.0 %collective-permute-start.3 = (bf16[12,128,128]{2,1,0:T(8,128)(2,1)S(1)}, bf16[12,128,128]{2,1,0:T(8,128)(2,1)S(1)}, u32[]{:S(2)}, u32[]{:S(2)}) collective-permute-start(bf16[12,128,128]{2,1,0:T(8,128)(2,1)S(1)} %get-tuple-element.109.refs_0_), channel_id=1, source_target_pairs={{0,16},{4,20},{8,24},{12,28},{16,0},{20,4},{24,8},{28,12},{1,17},{... | collective-permute-start | bytes 1179656 | tf_op jit(solution)/shard_map/ppermute | solution.py:121
  6.9 18.9 %collective-permute-start.10 = (bf16[12,128,128]{2,1,0:T(8,128)(2,1)S(1)}, bf16[12,128,128]{2,1,0:T(8,128)(2,1)S(1)}, u32[]{:S(2)}, u32[]{:S(2)}) collective-permute-start(bf16[12,128,128]{2,1,0:T(8,128)(2,1)S(1)} %get-tuple-element.108.refs_8_), channel_id=1, source_target_pairs={{0,16},{4,20},{8,24},{12,28},{16,0},{20,4},{24,8},{28,12},{1,17},{... | collective-permute-start | bytes 1179656 | tf_op jit(solution)/shard_map/ppermute | solution.py:121
  7.4 18.5 %collective-permute-start.1 = (bf16[12,128,128]{2,1,0:T(8,128)(2,1)S(1)}, bf16[12,128,128]{2,1,0:T(8,128)(2,1)S(1)}, u32[]{:S(2)}, u32[]{:S(2)}) collective-permute-start(bf16[12,128,128]{2,1,0:T(8,128)(2,1)S(1)} %get-tuple-element.109.refs_0_), channel_id=1, source_target_pairs={{0,8},{4,12},{8,0},{12,4},{16,24},{20,28},{24,16},{28,20},{1,9},{5... | collective-permute-start | bytes 1179656 | tf_op jit(solution)/shard_map/ppermute | solution.py:121
  7.4 18.5 %collective-permute-start = (bf16[12,128,128]{2,1,0:T(8,128)(2,1)S(1)}, bf16[12,128,128]{2,1,0:T(8,128)(2,1)S(1)}, u32[]{:S(2)}, u32[]{:S(2)}) collective-permute-start(bf16[12,128,128]{2,1,0:T(8,128)(2,1)S(1)} %get-tuple-element.109.refs_0_), channel_id=1, source_target_pairs={{0,4},{4,0},{8,12},{12,8},{16,20},{20,16},{24,28},{28,24},{1,5},{5... | collective-permute-start | bytes 1179656 | tf_op jit(solution)/shard_map/ppermute | solution.py:121
  15.3 22.4 %copy-start.8 = (bf16[12,128,128]{2,1,0:T(8,128)(2,1)}, bf16[12,128,128]{2,1,0:T(8,128)(2,1)S(1)}, u32[]{:S(2)}) copy-start(bf16[12,128,128]{2,1,0:T(8,128)(2,1)S(1)} %collective-permute-done.8.refs_10_) | copy-start | bytes 1179652
  15.3 11.1 %collective-permute-start.7 = (bf16[12,128,128]{2,1,0:T(8,128)(2,1)S(1)}, bf16[12,128,128]{2,1,0:T(8,128)(2,1)S(1)}, u32[]{:S(2)}, u32[]{:S(2)}) collective-permute-start(bf16[12,128,128]{2,1,0:T(8,128)(2,1)S(1)} %get-tuple-element.108.refs_8_), channel_id=1, source_target_pairs={{0,4},{4,0},{8,12},{12,8},{16,20},{20,16},{24,28},{28,24},{1,5},{5... | collective-permute-start | bytes 1179656 | tf_op jit(solution)/shard_map/ppermute | solution.py:121
  17.4 20.3 %copy-start.9 = (bf16[12,128,128]{2,1,0:T(8,128)(2,1)}, bf16[12,128,128]{2,1,0:T(8,128)(2,1)S(1)}, u32[]{:S(2)}) copy-start(bf16[12,128,128]{2,1,0:T(8,128)(2,1)S(1)} %collective-permute-done.3.refs_4_) | copy-start | bytes 1179652
  17.4 15.5 %collective-permute-start.12 = (bf16[12,128,128]{2,1,0:T(8,128)(2,1)S(1)}, bf16[12,128,128]{2,1,0:T(8,128)(2,1)}, u32[]{:S(2)}, u32[]{:S(2)}) collective-permute-start(bf16[12,128,128]{2,1,0:T(8,128)(2,1)S(1)} %collective-permute-done.8.refs_10_), channel_id=1, source_target_pairs={{0,16},{4,20},{8,24},{12,28},{16,0},{20,4},{24,8},{28,12},{1,17},{... | collective-permute-start | bytes 1179656 | tf_op jit(solution)/shard_map/ppermute | solution.py:121
  25.8 8.3 %collective-permute-start.5 = (bf16[12,128,128]{2,1,0:T(8,128)(2,1)S(1)}, bf16[12,128,128]{2,1,0:T(8,128)(2,1)}, u32[]{:S(2)}, u32[]{:S(2)}) collective-permute-start(bf16[12,128,128]{2,1,0:T(8,128)(2,1)S(1)} %collective-permute-done.3.refs_4_), channel_id=1, source_target_pairs={{0,8},{4,12},{8,0},{12,4},{16,24},{20,28},{24,16},{28,20},{1,9},{5... | collective-permute-start | bytes 1179656 | tf_op jit(solution)/shard_map/ppermute | solution.py:121
  25.9 8.3 %collective-permute-start.4 = (bf16[12,128,128]{2,1,0:T(8,128)(2,1)S(1)}, bf16[12,128,128]{2,1,0:T(8,128)(2,1)S(1)}, u32[]{:S(2)}, u32[]{:S(2)}) collective-permute-start(bf16[12,128,128]{2,1,0:T(8,128)(2,1)S(1)} %collective-permute-done.3.refs_4_), channel_id=1, source_target_pairs={{0,4},{4,0},{8,12},{12,8},{16,20},{20,16},{24,28},{28,24},{1,5},{5... | collective-permute-start | bytes 1179656 | tf_op jit(solution)/shard_map/ppermute | solution.py:121
  25.9 11.7 %collective-permute-start.9 = (bf16[12,128,128]{2,1,0:T(8,128)(2,1)S(1)}, bf16[12,128,128]{2,1,0:T(8,128)(2,1)}, u32[]{:S(2)}, u32[]{:S(2)}) collective-permute-start(bf16[12,128,128]{2,1,0:T(8,128)(2,1)S(1)} %collective-permute-done.8.refs_10_), channel_id=1, source_target_pairs={{0,4},{4,0},{8,12},{12,8},{16,20},{20,16},{24,28},{28,24},{1,5},{5... | collective-permute-start | bytes 1179656 | tf_op jit(solution)/shard_map/ppermute | solution.py:121
  26.4 11.2 %collective-permute-start.11 = (bf16[12,128,128]{2,1,0:T(8,128)(2,1)S(1)}, bf16[12,128,128]{2,1,0:T(8,128)(2,1)}, u32[]{:S(2)}, u32[]{:S(2)}) collective-permute-start(bf16[12,128,128]{2,1,0:T(8,128)(2,1)S(1)} %collective-permute-done.10.refs_12_), channel_id=1, source_target_pairs={{0,4},{4,0},{8,12},{12,8},{16,20},{20,16},{24,28},{28,24},{1,5},{5... | collective-permute-start | bytes 1179656 | tf_op jit(solution)/shard_map/ppermute | solution.py:121
  32.9 4.8 %collective-permute-start.2 = (bf16[12,128,128]{2,1,0:T(8,128)(2,1)S(1)}, bf16[12,128,128]{2,1,0:T(8,128)(2,1)}, u32[]{:S(2)}, u32[]{:S(2)}) collective-permute-start(bf16[12,128,128]{2,1,0:T(8,128)(2,1)S(1)} %collective-permute-done.1.refs_2_), channel_id=1, source_target_pairs={{0,4},{4,0},{8,12},{12,8},{16,20},{20,16},{24,28},{28,24},{1,5},{5... | collective-permute-start | bytes 1179656 | tf_op jit(solution)/shard_map/ppermute | solution.py:121
  34.1 3.5 %collective-permute-start.13 = (bf16[12,128,128]{2,1,0:T(8,128)(2,1)}, bf16[12,128,128]{2,1,0:T(8,128)(2,1)}, u32[]{:S(2)}, u32[]{:S(2)}) collective-permute-start(bf16[12,128,128]{2,1,0:T(8,128)(2,1)} %collective-permute-done.12.refs_14_), channel_id=1, source_target_pairs={{0,4},{4,0},{8,12},{12,8},{16,20},{20,16},{24,28},{28,24},{1,5},{5... | collective-permute-start | bytes 1179656 | tf_op jit(solution)/shard_map/ppermute | solution.py:121
  34.9 2.8 %collective-permute-start.6 = (bf16[12,128,128]{2,1,0:T(8,128)(2,1)}, bf16[12,128,128]{2,1,0:T(8,128)(2,1)}, u32[]{:S(2)}, u32[]{:S(2)}) collective-permute-start(bf16[12,128,128]{2,1,0:T(8,128)(2,1)} %collective-permute-done.5.refs_6_), channel_id=1, source_target_pairs={{0,4},{4,0},{8,12},{12,8},{16,20},{20,16},{24,28},{28,24},{1,5},{5... | collective-permute-start | bytes 1179656 | tf_op jit(solution)/shard_map/ppermute | solution.py:121
  57.3 25.4 %collective-permute-start.14 = (bf16[1024,128]{1,0:T(8,128)(2,1)}, bf16[1024,128]{1,0:T(8,128)(2,1)S(1)}, u32[]{:S(2)}, u32[]{:S(2)}) collective-permute-start(bf16[1024,128]{1,0:T(8,128)(2,1)} %get-tuple-element.64.refs_0_), channel_id=1, source_target_pairs={{0,1},{1,0},{2,3},{3,2},{4,5},{5,4},{6,7},{7,6},{8,9},{9,8},{10,11... | collective-permute-start | bytes 786440 | tf_op jit(solution)/shard_map/ppermute | solution.py:121
  58.9 16.9 %collective-permute-start.17 = (bf16[96,1024]{1,0:T(8,128)(2,1)S(1)}, bf16[96,1024]{1,0:T(8,128)(2,1)S(1)}, u32[]{:S(2)}, u32[]{:S(2)}) collective-permute-start(bf16[96,1024]{1,0:T(8,128)(2,1)S(1)} %slice_select_fusion.1), channel_id=1, source_target_pairs={{0,1},{1,0},{2,3},{3,2},{4,5},{5,4},{6,7},{7,6},{8,9},{9,8},{10,11... | collective-permute-start | bytes 589832 | tf_op jit(solution)/shard_map/ppermute | solution.py:121
  59.4 22.8 %collective-permute-start.18 = (bf16[96,1024]{1,0:T(8,128)(2,1)S(1)}, bf16[96,1024]{1,0:T(8,128)(2,1)S(1)}, u32[]{:S(2)}, u32[]{:S(2)}) collective-permute-start(bf16[96,1024]{1,0:T(8,128)(2,1)S(1)} %slice_select_fusion.1), channel_id=1, source_target_pairs={{0,2},{1,3},{2,0},{3,1},{4,6},{5,7},{6,4},{7,5},{8,10},{9,11},{10,... | collective-permute-start | bytes 589832 | tf_op jit(solution)/shard_map/ppermute | solution.py:121
  62.0 20.2 %collective-permute-start.19 = (bf16[96,1024]{1,0:T(8,128)(2,1)S(1)}, bf16[96,1024]{1,0:T(8,128)(2,1)S(1)}, u32[]{:S(2)}, u32[]{:S(2)}) collective-permute-start(bf16[96,1024]{1,0:T(8,128)(2,1)S(1)} %slice_select_fusion.1), channel_id=1, source_target_pairs={{0,3},{1,2},{2,1},{3,0},{4,7},{5,6},{6,5},{7,4},{8,11},{9,10},{10,... | collective-permute-start | bytes 589832 | tf_op jit(solution)/shard_map/ppermute | solution.py:121
  63.4 34.3 %collective-permute-start.15 = (bf16[1024,128]{1,0:T(8,128)(2,1)}, bf16[1024,128]{1,0:T(8,128)(2,1)S(1)}, u32[]{:S(2)}, u32[]{:S(2)}) collective-permute-start(bf16[1024,128]{1,0:T(8,128)(2,1)} %get-tuple-element.64.refs_0_), channel_id=1, source_target_pairs={{0,2},{1,3},{2,0},{3,1},{4,6},{5,7},{6,4},{7,5},{8,10},{9,11},{10,... | collective-permute-start | bytes 786440 | tf_op jit(solution)/shard_map/ppermute | solution.py:121
  75.8 22.0 %copy-start.18 = (bf16[96,1024]{1,0:T(8,128)(2,1)}, bf16[96,1024]{1,0:T(8,128)(2,1)S(1)}, u32[]{:S(2)}) copy-start(bf16[96,1024]{1,0:T(8,128)(2,1)S(1)} %collective-permute-done.17.refs_5_) | copy-start | bytes 589828
  75.8 21.9 %collective-permute-start.16 = (bf16[1024,128]{1,0:T(8,128)(2,1)}, bf16[1024,128]{1,0:T(8,128)(2,1)S(1)}, u32[]{:S(2)}, u32[]{:S(2)}) collective-permute-start(bf16[1024,128]{1,0:T(8,128)(2,1)} %get-tuple-element.64.refs_0_), channel_id=1, source_target_pairs={{0,3},{1,2},{2,1},{3,0},{4,7},{5,6},{6,5},{7,4},{8,11},{9,10},{10,... | collective-permute-start | bytes 786440 | tf_op jit(solution)/shard_map/ppermute | solution.py:121
  82.2 15.4 %collective-permute-start.20 = (bf16[96,1024]{1,0:T(8,128)(2,1)S(1)}, bf16[96,1024]{1,0:T(8,128)(2,1)S(1)}, u32[]{:S(2)}, u32[]{:S(2)}) collective-permute-start(bf16[96,1024]{1,0:T(8,128)(2,1)S(1)} %collective-permute-done.17.refs_5_), channel_id=1, source_target_pairs={{0,4},{4,0},{8,12},{12,8},{16,20},{20,16},{24,28},{28,24},{1,5},{5... | collective-permute-start | bytes 589832 | tf_op jit(solution)/shard_map/ppermute | solution.py:121
  82.3 15.4 %collective-permute-start.21 = (bf16[96,1024]{1,0:T(8,128)(2,1)S(1)}, bf16[96,1024]{1,0:T(8,128)(2,1)S(1)}, u32[]{:S(2)}, u32[]{:S(2)}) collective-permute-start(bf16[96,1024]{1,0:T(8,128)(2,1)S(1)} %collective-permute-done.18.refs_6_), channel_id=1, source_target_pairs={{0,4},{4,0},{8,12},{12,8},{16,20},{20,16},{24,28},{28,24},{1,5},{5... | collective-permute-start | bytes 589832 | tf_op jit(solution)/shard_map/ppermute | solution.py:121
  82.8 14.9 %collective-permute-start.22 = (bf16[96,1024]{1,0:T(8,128)(2,1)S(1)}, bf16[96,1024]{1,0:T(8,128)(2,1)S(1)}, u32[]{:S(2)}, u32[]{:S(2)}) collective-permute-start(bf16[96,1024]{1,0:T(8,128)(2,1)S(1)} %collective-permute-done.19.refs_7_), channel_id=1, source_target_pairs={{0,4},{4,0},{8,12},{12,8},{16,20},{20,16},{24,28},{28,24},{1,5},{5... | collective-permute-start | bytes 589832 | tf_op jit(solution)/shard_map/ppermute | solution.py:121
  113.4 18.0 %collective-permute-start.23 = (f32[104,1024]{1,0:T(8,128)S(1)}, f32[104,1024]{1,0:T(8,128)S(1)}, u32[]{:S(2)}, u32[]{:S(2)}) collective-permute-start(f32[104,1024]{1,0:T(8,128)S(1)} %slice_select_fusion), channel_id=1, source_target_pairs={{0,4},{4,0},{8,12},{12,8},{16,20},{20,16},{24,28},{28,24},{1,5},{5... | collective-permute-start | bytes 1277960 | tf_op jit(solution)/shard_map/ppermute | solution.py:121
  125.8 1.3 collective-permute-start.28
  127.9 5.8 %collective-permute-start.29 = (f32[16,512]{1,0:T(8,128)S(1)}, f32[16,512]{1,0:T(8,128)S(1)}, u32[]{:S(2)}, u32[]{:S(2)}) collective-permute-start(f32[16,512]{1,0:T(8,128)S(1)} %select_add_fusion.1), channel_id=1, source_target_pairs={{0,8},{4,12},{8,0},{12,4},{16,24},{20,28},{24,16},{28,20},{1,9},{5... | collective-permute-start | bytes 98312 | tf_op jit(solution)/shard_map/ppermute | solution.py:121
  128.6 7.1 %collective-permute-start.30 = (f32[16,512]{1,0:T(8,128)S(1)}, f32[16,512]{1,0:T(8,128)S(1)}, u32[]{:S(2)}, u32[]{:S(2)}) collective-permute-start(f32[16,512]{1,0:T(8,128)S(1)} %select_add_fusion.1), channel_id=1, source_target_pairs={{0,16},{4,20},{8,24},{12,28},{16,0},{20,4},{24,8},{28,12},{1,17},{... | collective-permute-start | bytes 98312 | tf_op jit(solution)/shard_map/ppermute | solution.py:121
  130.0 5.7 %collective-permute-start.31 = (f32[16,512]{1,0:T(8,128)S(1)}, f32[16,512]{1,0:T(8,128)S(1)}, u32[]{:S(2)}, u32[]{:S(2)}) collective-permute-start(f32[16,512]{1,0:T(8,128)S(1)} %select_add_fusion.1), channel_id=1, source_target_pairs={{0,24},{4,28},{8,16},{12,20},{16,8},{20,12},{24,0},{28,4},{1,25},{... | collective-permute-start | bytes 98312 | tf_op jit(solution)/shard_map/ppermute | solution.py:121
  131.5 12.8 %collective-permute-start.24 = (f32[104,1024]{1,0:T(8,128)S(1)}, f32[104,1024]{1,0:T(8,128)S(1)}, u32[]{:S(2)}, u32[]{:S(2)}) collective-permute-start(f32[104,1024]{1,0:T(8,128)S(1)} %select_add_fusion), channel_id=1, source_target_pairs={{0,8},{4,12},{8,0},{12,4},{16,24},{20,28},{24,16},{28,20},{1,9},{5... | collective-permute-start | bytes 1277960 | tf_op jit(solution)/shard_map/ppermute | solution.py:121
  132.3 12.3 %collective-permute-start.25 = (f32[104,1024]{1,0:T(8,128)S(1)}, f32[104,1024]{1,0:T(8,128)S(1)}, u32[]{:S(2)}, u32[]{:S(2)}) collective-permute-start(f32[104,1024]{1,0:T(8,128)S(1)} %select_add_fusion), channel_id=1, source_target_pairs={{0,16},{4,20},{8,24},{12,28},{16,0},{20,4},{24,8},{28,12},{1,17},{... | collective-permute-start | bytes 1277960 | tf_op jit(solution)/shard_map/ppermute | solution.py:121
  133.6 19.4 %collective-permute-start.26 = (f32[104,1024]{1,0:T(8,128)S(1)}, f32[104,1024]{1,0:T(8,128)S(1)}, u32[]{:S(2)}, u32[]{:S(2)}) collective-permute-start(f32[104,1024]{1,0:T(8,128)S(1)} %select_add_fusion), channel_id=1, source_target_pairs={{0,24},{4,28},{8,16},{12,20},{16,8},{20,12},{24,0},{28,4},{1,25},{... | collective-permute-start | bytes 1277960 | tf_op jit(solution)/shard_map/ppermute | solution.py:121
  135.7 17.6 %collective-permute-start.32 = (f32[16,512]{1,0:T(8,128)S(1)}, f32[16,512]{1,0:T(8,128)S(1)}, u32[]{:S(2)}, u32[]{:S(2)}) collective-permute-start(f32[16,512]{1,0:T(8,128)S(1)} %add_add_fusion.1), channel_id=1, source_target_pairs={{0,4},{4,0},{8,12},{12,8},{16,20},{20,16},{24,28},{28,24},{1,5},{5... | collective-permute-start | bytes 98312 | tf_op jit(solution)/shard_map/ppermute | solution.py:121
  153.2 1.8 collective-permute-start.27
  156.1 24.3 %copy-start.6 = (s32[192]{0:T(256)S(1)}, s32[192]{0:T(256)}, u32[]{:S(2)}) copy-start(s32[192]{0:T(256)} %constant.60) | copy-start | bytes 2308
  156.1 24.3 %copy-start.7 = (s32[192]{0:T(256)S(1)}, s32[192]{0:T(256)}, u32[]{:S(2)}) copy-start(s32[192]{0:T(256)} %constant.61) | copy-start | bytes 2308
  165.0 8.5 %collective-permute-start.33 = (f32[24,1024]{1,0:T(8,128)S(1)}, f32[24,1024]{1,0:T(8,128)S(1)}, u32[]{:S(2)}, u32[]{:S(2)}) collective-permute-start(f32[24,1024]{1,0:T(8,128)S(1)} %slice_select_fusion.2), channel_id=1, source_target_pairs={{0,1},{1,0},{2,3},{3,2},{4,5},{5,4},{6,7},{7,6},{8,9},{9,8},{10,11... | collective-permute-start | bytes 294920 | tf_op jit(solution)/shard_map/ppermute | solution.py:121
  170.0 6.1 %collective-permute-start.34 = (f32[24,1024]{1,0:T(8,128)S(1)}, f32[24,1024]{1,0:T(8,128)S(1)}, u32[]{:S(2)}, u32[]{:S(2)}) collective-permute-start(f32[24,1024]{1,0:T(8,128)S(1)} %slice_select_fusion.2), channel_id=1, source_target_pairs={{0,2},{1,3},{2,0},{3,1},{4,6},{5,7},{6,4},{7,5},{8,10},{9,11},{10,... | collective-permute-start | bytes 294920 | tf_op jit(solution)/shard_map/ppermute | solution.py:121
  171.9 8.5 %collective-permute-start.35 = (f32[24,1024]{1,0:T(8,128)S(1)}, f32[24,1024]{1,0:T(8,128)S(1)}, u32[]{:S(2)}, u32[]{:S(2)}) collective-permute-start(f32[24,1024]{1,0:T(8,128)S(1)} %slice_select_fusion.2), channel_id=1, source_target_pairs={{0,3},{1,2},{2,1},{3,0},{4,7},{5,6},{6,5},{7,4},{8,11},{9,10},{10,... | collective-permute-start | bytes 294920 | tf_op jit(solution)/shard_map/ppermute | solution.py:121
  173.5 7.7 %collective-permute-start.36 = (f32[24,1024]{1,0:T(8,128)S(1)}, f32[24,1024]{1,0:T(8,128)S(1)}, u32[]{:S(2)}, u32[]{:S(2)}) collective-permute-start(f32[24,1024]{1,0:T(8,128)S(1)} %collective-permute-done.33.refs_0_), channel_id=1, source_target_pairs={{0,4},{4,0},{8,12},{12,8},{16,20},{20,16},{24,28},{28,24},{1,5},{5... | collective-permute-start | bytes 294920 | tf_op jit(solution)/shard_map/ppermute | solution.py:121
  176.1 5.1 %collective-permute-start.37 = (f32[24,1024]{1,0:T(8,128)S(1)}, f32[24,1024]{1,0:T(8,128)S(1)}, u32[]{:S(2)}, u32[]{:S(2)}) collective-permute-start(f32[24,1024]{1,0:T(8,128)S(1)} %collective-permute-done.34.refs_1_), channel_id=1, source_target_pairs={{0,4},{4,0},{8,12},{12,8},{16,20},{20,16},{24,28},{28,24},{1,5},{5... | collective-permute-start | bytes 294920 | tf_op jit(solution)/shard_map/ppermute | solution.py:121
  180.4 1.3 collective-permute-start.38
  (22 other events, 155.9 us)
